TPU v7x, 512 devices: a whole 4x4x16 slice. The times are simulated.
512 devices in a mesh: row: 32 (over y, z_hi, core), col: 16 (over z_lo, x).
Axes of the slice: x: 4, y: 4, z: 16 (z_hi: 4, z_lo: 4; z = z_hi * 4 + z_lo), core: 2. Of those that a mesh axis runs over, the one named last changes fastest.
Arguments:
- alignment: float32 [768, 64, 64], P('row', 'col'), may hold values from -6 to 6
- pair_state: float32 [768, 768, 128], P('row', 'col'), may hold values from -6 to 6
- pair_weights: float32 [8, 768, 768], P(None, 'row', 'col'), may hold values from 0 to 1, as said below
- align_gain: float32 [64], replicated, may hold values from 0.5 to 2
- value_weight: float32 [64, 256], replicated, may hold values from -0.75 to 0.75
- gate_weight: float32 [64, 256], replicated, may hold values from -0.75 to 0.75
- output_weight: float32 [256, 64], replicated, may hold values from -0.375 to 0.375
- outer_gain: float32 [64], replicated, may hold values from 0.5 to 2
- left_weight: float32 [64, 32], replicated, may hold values from -0.75 to 0.75
- right_weight: float32 [64, 32], replicated, may hold values from -0.75 to 0.75
- outer_weight: float32 [1024, 128], replicated, may hold values from -0.75 to 0.75
- outer_bias: float32 [128], replicated, may hold values from -3 to 3
Outputs:
- alignment_out: float32 [768, 64, 64], P('row', 'col')
- pair_out: float32 [768, 768, 128], P('row', 'col')
Inputs may be any that keep to these rules, and one draw needn't show every extreme that they name: `pair_weights`: every entry is positive, and for each head and row token the weights over the 768 column tokens sum to one.
All inputs are finite; a program needn't handle non-finite values.
Results may differ from a plain program's by a relative error of at most 0.00011.
Values sent between devices are 32-bit elements; how exact they have to be, the bound alone decides.
No kernel may reach another device: no remote copies, remote signals or barrier semaphores. Data moves between devices by JAX's collectives and lax.ppermute only.
A program may use at most 64 MiB of HBM per device.

v0:
```python
import jax
import jax.numpy as jnp
from jax import lax
from jax.sharding import PartitionSpec as P

PRECISE = lax.Precision.HIGHEST


def from_everyone(value, axis):
    count = lax.axis_size(axis)
    return lax.all_to_all(
        jnp.broadcast_to(value[None], (count, *value.shape)), axis, 0, 0, tiled=True
    )


def in_order(tiles, dim):
    tiles = jnp.moveaxis(tiles, 0, dim)
    lengths = tiles.shape
    return tiles.reshape(*lengths[:dim], lengths[dim] * lengths[dim + 1], *lengths[dim + 2 :])


def collect(value, axis, dim):
    tiles = from_everyone(value, axis)
    return in_order(tiles, dim)


def normalize(features, channel_gain):
    channel_mean = jnp.mean(features, axis=-1, keepdims=True)
    centered = features - channel_mean
    spread = jnp.mean(centered * centered, axis=-1, keepdims=True)
    return centered * lax.rsqrt(spread + 1e-05) * channel_gain


def on_device(
    alignment,
    pair_state,
    pair_weights,
    align_gain,
    value_weight,
    gate_weight,
    output_weight,
    outer_gain,
    left_weight,
    right_weight,
    outer_weight,
    outer_bias,
):
    head_count = pair_weights.shape[0]
    local_rows = alignment.shape[0]
    local_seqs = alignment.shape[1]
    channels = alignment.shape[2]
    normed = normalize(alignment, align_gain)
    flat_normed = normed.reshape(local_rows, local_seqs * channels)
    gathered = lax.all_gather(flat_normed, "row", axis=0, tiled=True)
    gathered = gathered.reshape(-1, local_seqs, channels)
    mixed_rows = jnp.einsum(
        "hij,jsc->ishc", collect(pair_weights, "col", 2), gathered, precision=PRECISE
    )
    per_head = value_weight.reshape(channels, head_count, -1)
    averaged = jnp.einsum("ishc,chd->ishd", mixed_rows, per_head, precision=PRECISE)
    gate_values = jax.nn.sigmoid(jnp.einsum("nsc,cd->nsd", normed, gate_weight, precision=PRECISE))
    gated_heads = gate_values * averaged.reshape(gate_values.shape)
    alignment_out = alignment + jnp.einsum(
        "nsd,dc->nsc", gated_heads, output_weight, precision=PRECISE
    )
    normed_out = normalize(alignment_out, outer_gain)
    left_side = jnp.einsum("nsc,cd->nsd", normed_out, left_weight, precision=PRECISE)
    right_side = jnp.einsum("nsc,cd->nsd", normed_out, right_weight, precision=PRECISE)
    factor_width = left_side.shape[2]
    columns = pair_state.shape[1]
    left_flat = left_side.transpose(1, 0, 2).reshape(local_seqs, local_rows * factor_width)
    right_rows = right_side.reshape(local_rows, local_seqs * factor_width)
    right_tokens = collect(right_rows, "row", 0)
    right_tokens = right_tokens.reshape(-1, local_seqs, factor_width)
    right_columns = lax.all_to_all(right_tokens, "col", split_axis=0, concat_axis=1, tiled=True)
    right_all = right_columns.transpose(1, 0, 2)
    left_all = collect(left_flat, "col", 0)
    sequences = left_all.shape[0]
    left_all = left_all.reshape(sequences, local_rows, factor_width)
    block_rows = 8
    left_blocks = left_all.reshape(
        sequences, local_rows // block_rows, block_rows, factor_width
    ).transpose(1, 2, 0, 3)

    def outer_block(left_block):
        product = jnp.einsum("isc,sjd->ijcd", left_block, right_all, precision=PRECISE) / sequences
        flattened = product.reshape(-1, factor_width * factor_width)
        projected = jnp.dot(
            flattened, outer_weight, precision=PRECISE, preferred_element_type=jnp.float32
        )
        return projected.reshape(block_rows, columns, -1)

    update = lax.map(outer_block, left_blocks).reshape(pair_state.shape)
    pair_out = pair_state + update + outer_bias
    return (alignment_out, pair_out)


def solution(mesh):
    return jax.shard_map(
        on_device,
        mesh=mesh,
        in_specs=(
            P("row", "col", None),
            P("row", "col", None),
            P(None, "row", "col"),
            P(),
            P(),
            P(),
            P(),
            P(),
            P(),
            P(),
            P(),
            P(),
        ),
        out_specs=(P("row", "col", None), P("row", "col", None)),
        check_vma=False,
    )
```

profile of v0, /device:TPU:8, one launch (start us, length us, event | category | flops | bytes accessed | tf_op | source)
XLA Modules:
  0.0 219.8 jit_solution(15116444611378009533)
XLA Ops:
  0.6 0.0 copy-start
  0.6 1.1 broadcast_in_dim.13
  1.7 0.0 copy-start.3
  1.7 0.0 copy-start.6
  1.7 2.4 %reshape.79 = f32[16,1,9216]{2,1,0:T(1,128)} reshape(f32[16,8,24,48]{3,2,1,0:T(8,128)S(1)} %broadcast_in_dim.13) | data formatting | bytes 1179648
  4.1 8.5 %all-to-all-start = ((f32[16,1,9216]{2,1,0:T(1,128)}), f32[16,1,9216]{2,1,0:T(1,128)S(1)}, u32[]{:S(2)}, u32[]{:S(2)}) async-start(f32[16,1,9216]{2,1,0:T(1,128)} %reshape.79), calls=%async_computation | async-start | bytes 1179648 | tf_op jit(solution)/shard_map/all_to_all | solution.py:11
  12.6 0.0 copy-start.4
  12.6 0.1 reduce_sum.36
  12.7 0.2 multiply_reduce_fusion.1
  12.9 0.1 multiply_multiply_fusion.1
  13.1 0.1 reshape.62
  13.2 58.9 %all_gather.3 = f32[768,256]{1,0:T(8,128)S(1)} all-gather(f32[24,256]{1,0:T(8,128)S(1)} %reshape.62), channel_id=1, replica_groups=mesh['row'=32,'col'=16] {'row'}, dimensions={0}, use_global_device_ids=true | all-gather | bytes 811008 | tf_op jit(solution)/shard_map/all_gather | solution.py:54
  72.0 1.2 copy.71
  73.2 0.1 copy.73
  73.3 0.5 broadcast.67
  73.8 2.0 reduce
  75.9 0.7 reshape.80
  76.5 0.9 copy.72
  77.5 0.7 reshape.73
  78.2 0.4 copy-done.2
  78.6 1.1 convolution_bitcast_fusion.2
  79.7 0.0 copy-start.5
  79.7 0.5 convolution_bitcast_fusion.1
  80.2 0.2 copy.74
  80.5 0.2 reshape.66
  80.7 0.2 fusion.9
  80.9 0.3 fusion.24
  81.2 0.2 multiply_reduce_fusion
  81.4 0.2 fusion.15
  81.7 0.1 broadcast_in_dim.17
  81.8 0.8 broadcast_in_dim.19
  82.6 10.2 %all-to-all-start.2 = ((f32[32,24,128]{2,1,0:T(8,128)}), f32[32,24,128]{2,1,0:T(8,128)S(1)}, u32[]{:S(2)}, u32[]{:S(2)}) async-start(f32[32,24,128]{2,1,0:T(8,128)} %broadcast_in_dim.19), calls=%async_computation.2 | async-start | bytes 786432 | tf_op jit(solution)/shard_map/all_to_all | solution.py:11
  92.8 0.2 convolution_bitcast_fusion.3
  93.0 0.1 broadcast_in_dim.15
  93.1 19.2 %all-to-all-done.2 = f32[32,24,128]{2,1,0:T(8,128)S(1)} async-done(((f32[32,24,128]{2,1,0:T(8,128)}), f32[32,24,128]{2,1,0:T(8,128)S(1)}, u32[]{:S(2)}, u32[]{:S(2)}) %all-to-all-start.2) | async-done | bytes 393248 | tf_op jit(solution)/shard_map/all_to_all | solution.py:11
  112.3 0.7 broadcast_in_dim.16
  113.0 13.8 %all-to-all-start.1 = ((f32[16,4,768]{2,1,0:T(4,128)}), f32[16,4,768]{2,1,0:T(4,128)S(1)}, u32[]{:S(2)}, u32[]{:S(2)}) async-start(f32[16,4,768]{2,1,0:T(4,128)} %broadcast_in_dim.16), calls=%async_computation.1 | async-start | bytes 393216 | tf_op jit(solution)/shard_map/all_to_all | solution.py:11
  126.8 0.7 reshape_reshape.3
  127.5 1.8 reshape.81
  129.3 8.0 %all-to-all-done.1 = f32[16,4,768]{2,1,0:T(4,128)S(1)} async-done(((f32[16,4,768]{2,1,0:T(4,128)}), f32[16,4,768]{2,1,0:T(4,128)S(1)}, u32[]{:S(2)}, u32[]{:S(2)}) %all-to-all-start.1) | async-done | bytes 196640 | tf_op jit(solution)/shard_map/all_to_all | solution.py:11
  137.2 3.7 %all-to-all-start.3 = ((f32[16,1,6144]{2,1,0:T(1,128)}), f32[16,1,6144]{2,1,0:T(1,128)S(1)}, u32[]{:S(2)}, u32[]{:S(2)}) async-start(f32[16,1,6144]{2,1,0:T(1,128)} %reshape.81), calls=%async_computation.3 | async-start | bytes 786432 | tf_op jit(solution)/shard_map/all_to_all | solution.py:75
  141.0 0.6 copy.81
  141.6 0.3 reshape_reshape_reshape.3
  141.9 0.3 copy.79
  142.2 11.7 %all-to-all-done.3 = f32[16,1,6144]{2,1,0:T(1,128)S(1)} async-done(((f32[16,1,6144]{2,1,0:T(1,128)}), f32[16,1,6144]{2,1,0:T(1,128)S(1)}, u32[]{:S(2)}, u32[]{:S(2)}) %all-to-all-start.3) | async-done | bytes 393248 | tf_op jit(solution)/shard_map/all_to_all | solution.py:75
  153.8 1.6 reduce.1
  155.4 0.8 reshape.82
  156.2 0.7 copy.86
  156.9 0.6 copy.80
  157.5 0.4 copy-done.1
  157.9 59.8 %while.10 = (s32[]{:T(128)}, f32[3,8,48,128]{3,2,1,0:T(8,128)}, f32[3,8,64,32]{2,3,1,0:T(8,128)S(1)}, f32[64,48,32]{0,1,2:T(8,128)S(1)}, f32[1024,128]{1,0:T(8,128)S(1)}, /*index=5*/s32[]{:T(128)}) while((s32[]{:T(128)}, f32[3,8,48,128]{3,2,1,0:T(8,128)}, f32[3,8,64,32]{2,3,1,0:T(8,128)S(1)}, f32[64,48,32]{0,1,2:T(8,128)S(1)}, ...), condition=%wide.region_5.6_spmd, body=%wide.region_4.5_spmd.sunk | while | flops 906362880 | bytes 11076169 | solution.py:93
  157.9 4.9 %multiply_bitcast_fusion.2 = f32[8,48,32,32]{1,2,3,0:T(8,128)} fusion(f32[64,48,32]{0,1,2:T(8,128)S(1)} %get-tuple-element.118, f32[3,8,64,32]{2,3,1,0:T(8,128)S(1)} %get-tuple-element.117, s32[]{:T(128)} %get-tuple-element.109), kind=kOutput, calls=%fused_computation.clone.1 | convolution fusion | flops 302383104 | bytes 2490372 | tf_op jit(solution)/shard_map/while/body/eval_jaxpr/isc,sjd->ijcd/dot_general | solution.py:86
  162.9 7.9 %copy.93 = f32[8,48,32,32]{3,2,1,0:T(8,128)} copy(f32[8,48,32,32]{1,2,3,0:T(8,128)} %multiply_bitcast_fusion.2) | data formatting | bytes 3145728 | tf_op jit(solution)/shard_map/while/body/eval_jaxpr/div | solution.py:86
  170.7 5.0 %reshape.84 = f32[8,48,1024]{2,1,0:T(8,128)S(1)} reshape(f32[8,48,32,32]{3,2,1,0:T(8,128)} %copy.93) | data formatting | bytes 3145728 | tf_op jit(solution)/shard_map/reshape.25
  175.8 2.1 fusion.39
  177.8 4.9 %multiply_bitcast_fusion.2 = f32[8,48,32,32]{1,2,3,0:T(8,128)} fusion(f32[64,48,32]{0,1,2:T(8,128)S(1)} %get-tuple-element.118, f32[3,8,64,32]{2,3,1,0:T(8,128)S(1)} %get-tuple-element.117, s32[]{:T(128)} %get-tuple-element.109), kind=kOutput, calls=%fused_computation.clone.1 | convolution fusion | flops 302383104 | bytes 2490372 | tf_op jit(solution)/shard_map/while/body/eval_jaxpr/isc,sjd->ijcd/dot_general | solution.py:86
  182.8 7.9 %copy.93 = f32[8,48,32,32]{3,2,1,0:T(8,128)} copy(f32[8,48,32,32]{1,2,3,0:T(8,128)} %multiply_bitcast_fusion.2) | data formatting | bytes 3145728 | tf_op jit(solution)/shard_map/while/body/eval_jaxpr/div | solution.py:86
  190.6 5.0 %reshape.84 = f32[8,48,1024]{2,1,0:T(8,128)S(1)} reshape(f32[8,48,32,32]{3,2,1,0:T(8,128)} %copy.93) | data formatting | bytes 3145728 | tf_op jit(solution)/shard_map/reshape.25
  195.7 2.1 fusion.39
  197.8 4.9 %multiply_bitcast_fusion.2 = f32[8,48,32,32]{1,2,3,0:T(8,128)} fusion(f32[64,48,32]{0,1,2:T(8,128)S(1)} %get-tuple-element.118, f32[3,8,64,32]{2,3,1,0:T(8,128)S(1)} %get-tuple-element.117, s32[]{:T(128)} %get-tuple-element.109), kind=kOutput, calls=%fused_computation.clone.1 | convolution fusion | flops 302383104 | bytes 2490372 | tf_op jit(solution)/shard_map/while/body/eval_jaxpr/isc,sjd->ijcd/dot_general | solution.py:86
  202.7 7.9 %copy.93 = f32[8,48,32,32]{3,2,1,0:T(8,128)} copy(f32[8,48,32,32]{1,2,3,0:T(8,128)} %multiply_bitcast_fusion.2) | data formatting | bytes 3145728 | tf_op jit(solution)/shard_map/while/body/eval_jaxpr/div | solution.py:86
  210.6 5.0 %reshape.84 = f32[8,48,1024]{2,1,0:T(8,128)S(1)} reshape(f32[8,48,32,32]{3,2,1,0:T(8,128)} %copy.93) | data formatting | bytes 3145728 | tf_op jit(solution)/shard_map/reshape.25
  215.6 2.1 fusion.39
  217.7 2.1 fusion.10
  (22 shorter events, 0.1 us)
Async XLA Ops:
  0.6 80.0 %copy-start = (f32[64,256]{1,0:T(8,128)S(1)}, f32[64,256]{1,0:T(8,128)}, u32[]{:S(2)}) copy-start(f32[64,256]{1,0:T(8,128)} %param.19) | copy-start | bytes 196612
  1.7 10.9 %copy-start.3 = (f32[24,4,64]{2,1,0:T(4,128)S(1)}, f32[24,4,64]{2,1,0:T(4,128)}, u32[]{:S(2)}) copy-start(f32[24,4,64]{2,1,0:T(4,128)} %param.14) | copy-start | bytes 73732
  1.7 11.2 %copy-start.6 = (f32[64]{0:T(128)S(1)}, f32[64]{0:T(128)}, u32[]{:S(2)}) copy-start(f32[64]{0:T(128)} %param.17) | copy-start | bytes 772
  4.1 69.2 %all-to-all-start = ((f32[16,1,9216]{2,1,0:T(1,128)}), f32[16,1,9216]{2,1,0:T(1,128)S(1)}, u32[]{:S(2)}, u32[]{:S(2)}) async-start(f32[16,1,9216]{2,1,0:T(1,128)} %reshape.79), calls=%async_computation | async-start | bytes 1179648 | tf_op jit(solution)/shard_map/all_to_all | solution.py:11
  12.6 60.6 %copy-start.4 = (f32[64,256]{1,0:T(8,128)S(1)}, f32[64,256]{1,0:T(8,128)}, u32[]{:S(2)}) copy-start(f32[64,256]{1,0:T(8,128)} %param.18) | copy-start | bytes 196612
  77.5 1.1 copy-start.2
  79.7 1.2 copy-start.5
  79.7 1.7 copy-start.8
  79.7 1.7 copy-start.10
  80.2 12.5 %copy-start.9 = (f32[64,32]{0,1:T(8,128)S(1)}, f32[64,32]{0,1:T(8,128)}, u32[]{:S(2)}) copy-start(f32[64,32]{0,1:T(8,128)} %param.22) | copy-start | bytes 24580
  82.6 29.7 %all-to-all-start.2 = ((f32[32,24,128]{2,1,0:T(8,128)}), f32[32,24,128]{2,1,0:T(8,128)S(1)}, u32[]{:S(2)}, u32[]{:S(2)}) async-start(f32[32,24,128]{2,1,0:T(8,128)} %broadcast_in_dim.19), calls=%async_computation.2 | async-start | bytes 786432 | tf_op jit(solution)/shard_map/all_to_all | solution.py:11
  113.0 24.2 %all-to-all-start.1 = ((f32[16,4,768]{2,1,0:T(4,128)}), f32[16,4,768]{2,1,0:T(4,128)S(1)}, u32[]{:S(2)}, u32[]{:S(2)}) async-start(f32[16,4,768]{2,1,0:T(4,128)} %broadcast_in_dim.16), calls=%async_computation.1 | async-start | bytes 393216 | tf_op jit(solution)/shard_map/all_to_all | solution.py:11
  137.2 16.6 %all-to-all-start.3 = ((f32[16,1,6144]{2,1,0:T(1,128)}), f32[16,1,6144]{2,1,0:T(1,128)S(1)}, u32[]{:S(2)}, u32[]{:S(2)}) async-start(f32[16,1,6144]{2,1,0:T(1,128)} %reshape.81), calls=%async_computation.3 | async-start | bytes 786432 | tf_op jit(solution)/shard_map/all_to_all | solution.py:75
  156.9 1.0 copy-start.1
  157.9 59.8 %copy-start.7 = (f32[128]{0:T(128)S(1)}, f32[128]{0:T(128)}, u32[]{:S(2)}) copy-start(f32[128]{0:T(128)} %param.25) | copy-start | bytes 1540
where the time goes:
time: 221 us; the launch traced here: 220 us
  blocking collectives  58.9 us (27%)
  local copies, waits for them, and re-layouts  54.9 us (25%)
  waiting for transfers between devices  38.8 us (18%)
  starting transfers between devices  36.2 us (16%)
  matrix products  23.7 us (11%)
  other arithmetic  6.28 us (3%)
    all_gather x1, blocking collectives, on_device(): gathered = lax.all_gather(flat_normed, 'row', axis=0, tiled=True)  58.9 us
    all_to_all x3, starting transfers between devices, from_everyone(): lax.all_to_all(jnp.broadcast_to(value[None], (count, *value.shape)), axis...  32.5 us
    all_to_all x3, waiting for transfers between devices, from_everyone(): lax.all_to_all(jnp.broadcast_to(value[None], (count, *value.shape)), axis...  27.2 us
    div x3, local copies, waits for them, and re-layouts, outer_block(): jnp.einsum('isc,sjd->ijcd', left_block, right_all, precision=PRECISE)  23.6 us
    another operation x3, local copies, waits for them, and re-layouts  15.1 us
    dot_general x3, matrix products, outer_block(): jnp.einsum('isc,sjd->ijcd', left_block, right_all, precision=PRECISE)  14.8 us
    all_to_all x1, waiting for transfers between devices, on_device(): lax.all_to_all(right_tokens, 'col', split_axis=0, concat_axis=1, tiled=True)  11.7 us
    unnamed x28, local copies, waits for them, and re-layouts  7.25 us
  transfers between devices with their start and end apart: 4, of which 3 were waited for; matrix products, arithmetic and copies ran while one was open for 3% of the time, Pallas kernels for 0%

commit v1 on v0

v1 whole, which is shorter than its diff:
```python
import functools

import jax
import jax.numpy as jnp
from jax import lax
from jax.experimental import pallas as pl
from jax.experimental.pallas import tpu as pltpu
from jax.sharding import Mesh, PartitionSpec as P

F32 = jnp.float32
BF16 = jnp.bfloat16
ROW = ("y", "zh", "core")
COL = ("zl", "x")
ALL = ROW + COL
LANES = 128


def split(value):
    high = value.astype(BF16)
    low = (value - high.astype(F32)).astype(BF16)
    return high, low


def dot(a, b):
    return jnp.dot(a, b, preferred_element_type=F32)


def dot3(a, b):
    ah, al = split(a)
    bh, bl = split(b)
    return dot(ah, bh) + (dot(ah, bl) + dot(al, bh))


def normalize(features, gain):
    mean = jnp.mean(features, axis=-1, keepdims=True)
    centered = features - mean
    spread = jnp.mean(centered * centered, axis=-1, keepdims=True)
    return centered * lax.rsqrt(spread + 1e-05) * gain


def twice(weight):
    zeros = jnp.zeros_like(weight)
    return jnp.concatenate(
        [jnp.concatenate([weight, zeros], 1), jnp.concatenate([zeros, weight], 1)], 0
    )


def prepare_kernel(align_ref, pair_w_ref, gain_ref, normed_ref, weights_ref):
    rows = align_ref.shape[0]
    heads, _, columns = pair_w_ref.shape
    parts = [normalize(align_ref[:, s, :], gain_ref[...]) for s in range(4)]
    normed_ref[0:rows, :] = jnp.concatenate(parts[0:2], axis=1)
    normed_ref[rows : 2 * rows, :] = jnp.concatenate(parts[2:4], axis=1)
    turned = pair_w_ref[...].reshape(heads * rows, columns).T
    half = columns // 2
    tail = turned[:, LANES:]
    tail = jnp.concatenate([tail[:half], tail[half:]], axis=1)
    for k in range(weights_ref.shape[0]):
        weights_ref[k, 0:columns, :] = turned[:, :LANES]
        weights_ref[k, columns:, :] = tail


def average_kernel(
    weights_ref,
    gathered_ref,
    normed_ref,
    align_ref,
    value_ref,
    gate_ref,
    output_ref,
    gain_ref,
    sides_ref,
    out_ref,
    left_ref,
    right_ref,
    left_tmp,
    right_tmp,
):
    rows = align_ref.shape[0]
    columns = 2 * rows
    heads = 8
    first = weights_ref[:, 0:columns, :].reshape(-1, LANES)
    tail = weights_ref[:, columns:, :]
    second = jnp.concatenate([tail[:, :, :64], tail[:, :, 64:]], axis=1).reshape(-1, 64)
    weights = jnp.concatenate([first.T, second.T], axis=0)
    value2 = twice(value_ref[...])
    gate2 = twice(gate_ref[...])
    lane = lax.broadcasted_iota(jnp.int32, (rows, 512), 1)
    lane_head = lax.rem(lax.div(lane, 32), heads)
    wh, wl = split(weights)
    vh, vl = split(value2)
    gated = []
    for p in range(2):
        blocks = [
            gathered_ref[(r % 2) * 16 + r // 2, p * rows : (p + 1) * rows, :] for r in range(32)
        ]
        fh, fl = split(jnp.concatenate(blocks, axis=0))
        mixed = dot(wh, fh) + (dot(wh, fl) + dot(wl, fh))
        mh, ml = split(mixed)
        by_head = dot(mh, vh) + (dot(mh, vl) + dot(ml, vh))
        averaged = jnp.zeros((rows, 512), F32)
        for h in range(heads):
            averaged += jnp.where(lane_head == h, by_head[h * rows : (h + 1) * rows], 0.0)
        gate = jax.nn.sigmoid(dot3(normed_ref[p * rows : (p + 1) * rows, :], gate2))
        product = gate * averaged
        gated += [product[:, :256], product[:, 256:]]
    update = dot3(jnp.concatenate(gated, axis=0), output_ref[...])
    aligned = jnp.concatenate([align_ref[:, s, :] for s in range(4)], axis=0) + update
    for s in range(4):
        out_ref[:, s, :] = aligned[s * rows : (s + 1) * rows]
    sides = dot3(normalize(aligned, gain_ref[...]), sides_ref[...])
    left_tmp[...] = sides[:, :LANES]
    right_tmp[...] = sides[:, LANES:]
    left = jnp.concatenate(
        [left_tmp[pl.ds(k, rows, stride=4), 0:32] for k in range(4)], axis=1
    )
    right = jnp.concatenate(
        [right_tmp[pl.ds(k, rows, stride=4), 0:32] for k in range(4)], axis=1
    )
    for k in range(left_ref.shape[0]):
        left_ref[k] = left
    right_ref[...] = right


CHUNK = 4


def outer_kernel(
    left_ref,
    right_ref,
    state_ref,
    outer_ref,
    bias_ref,
    out_ref,
    turned,
    spread_h,
    spread_l,
    total,
):
    lefts = [
        left_ref[pl.ds(g, 64, stride=6), :] * (1.0 / 64.0) for g in range(6)
    ]
    left = jnp.concatenate(lefts, axis=1)
    lh, ll = split(left)
    left4 = jnp.concatenate([lh, lh, ll, ll], axis=0)
    for core in range(2):
        for g in range(6):
            block = right_ref[pl.ds(core * 384 + g, 64, stride=6), :]
            high = block.astype(BF16).astype(F32)
            stacked = jnp.concatenate([high, block - high], axis=0)
            turned[(core * 6 + g) * LANES : (core * 6 + g + 1) * LANES, :] = stacked.T
    spread_h[...] = jnp.zeros_like(spread_h)
    spread_l[...] = jnp.zeros_like(spread_l)
    for t in range(32 // CHUNK):
        rights = []
        for e in range(CHUNK):
            d = t * CHUNK + e
            right = turned[pl.ds(d, 48, stride=32), :].astype(BF16)
            rights.append(jnp.concatenate([right, right], axis=1))
            wh, wl = split(outer_ref[pl.ds(d, 32, stride=32), :])
            for k in range(4):
                at = (pl.ds(e * LANES + 32 * k, 32), pl.ds(k * LANES, LANES))
                spread_h[at] = wh
                spread_l[at] = wl
        product = dot(jnp.concatenate(rights, axis=0), left4)
        ph, pl_ = split(product)

        def regroup(x):
            return jnp.concatenate(
                [
                    jnp.concatenate(
                        [
                            x[e * 48 : (e + 1) * 48, g * LANES : (g + 1) * LANES]
                            for e in range(CHUNK)
                        ],
                        axis=1,
                    )
                    for g in range(6)
                ],
                axis=0,
            )

        ah, al = regroup(ph), regroup(pl_)
        bh, bl = spread_h[...], spread_l[...]
        step = dot(ah, bh) + (dot(ah, bl) + dot(al, bh))
        if t == 0:
            total[...] = step
        else:
            total[...] += step
    for g in range(6):
        for k in range(4):
            out_ref[g * 4 + k] = (
                state_ref[g * 4 + k]
                + total[g * 48 : (g + 1) * 48, k * LANES : (k + 1) * LANES]
                + bias_ref[...]
            )


def copies(value, axis):
    return jnp.broadcast_to(value[None], (lax.axis_size(axis), *value.shape))


def everyone(value, axis):
    return lax.all_to_all(copies(value, axis), axis, 0, 0, tiled=True)


def to_columns():
    pairs = []
    for y in range(4):
        for zh in range(4):
            for core in range(2):
                for zl in range(4):
                    for x in range(4):
                        source = (((y * 4 + zh) * 2 + core) * 4 + zl) * 4 + x
                        target = (((zl * 4 + x) * 2 + core) * 4 + y) * 4 + zh
                        pairs.append((source, target))
    return pairs


PARAMS = pltpu.CompilerParams(vmem_limit_bytes=48 * 1024 * 1024)


def shape(*dims):
    return jax.ShapeDtypeStruct(dims, F32)


def on_device(
    alignment,
    pair_state,
    pair_weights,
    align_gain,
    value_weight,
    gate_weight,
    output_weight,
    outer_gain,
    left_weight,
    right_weight,
    outer_weight,
    outer_bias,
):
    normed, packed = pl.pallas_call(
        prepare_kernel,
        out_shape=(shape(48, 128), shape(16, 72, 128)),
        compiler_params=PARAMS,
    )(alignment, pair_weights, align_gain[None])
    weights = lax.all_to_all(packed, COL, 0, 0, tiled=True)
    near = lax.all_gather(normed, "zh", axis=0, tiled=True)
    wide = everyone(near, "y").reshape(16 * 48, 128)
    gathered = lax.all_gather(wide, "core", axis=0, tiled=True).reshape(32, 48, 128)
    pad = jnp.zeros((64, 96), F32)
    sides = jnp.concatenate([left_weight, pad, right_weight, pad], axis=1)
    alignment_out, left, right = pl.pallas_call(
        average_kernel,
        out_shape=(shape(24, 4, 64), shape(16, 24, 128), shape(24, 128)),
        scratch_shapes=[pltpu.VMEM((96, 128), F32), pltpu.VMEM((96, 128), F32)],
        compiler_params=PARAMS,
    )(
        weights,
        gathered,
        normed,
        alignment,
        value_weight,
        gate_weight,
        output_weight,
        outer_gain[None],
        sides,
    )
    left_all = lax.all_to_all(left, COL, 0, 0, tiled=True).reshape(384, 128)
    right = lax.ppermute(right, ALL, to_columns())
    right = everyone(right, "zh").reshape(96, 128)
    right = everyone(right, "y").reshape(384, 128)
    right_all = lax.all_gather(right, "core", axis=0, tiled=True)
    pair_out = pl.pallas_call(
        outer_kernel,
        out_shape=shape(24, 48, 128),
        scratch_shapes=[
            pltpu.VMEM((1536, 128), F32),
            pltpu.VMEM((CHUNK * LANES, 512), BF16),
            pltpu.VMEM((CHUNK * LANES, 512), BF16),
            pltpu.VMEM((288, 512), F32),
        ],
        compiler_params=PARAMS,
    )(left_all, right_all, pair_state, outer_weight, outer_bias[None])
    return alignment_out, pair_out


def solution(mesh):
    torus = Mesh(mesh.devices.reshape(4, 4, 2, 4, 4), ALL)
    return jax.shard_map(
        on_device,
        mesh=torus,
        in_specs=(P(ROW, COL, None), P(ROW, COL, None), P(None, ROW, COL)) + (P(),) * 9,
        out_specs=(P(ROW, COL, None), P(ROW, COL, None)),
        check_vma=False,
    )
```

time: 221 us -> 129 us (0.58)
  the two profiles are of different devices: /device:TPU:8 before, /device:TPU:2 now
where the time goes in v1:
time: 129 us; the launch traced here: 128 us
  blocking collectives  73.7 us (57%)
  starting transfers between devices  19.9 us (15%)
  waiting for transfers between devices  18.5 us (14%)
  Pallas kernels  10.3 us (8%)
  local copies, waits for them, and re-layouts  5.22 us (4%)
    all_to_all x3, blocking collectives, everyone(): return lax.all_to_all(copies(value, axis), axis, 0, 0, tiled=True)  43.4 us
    all_gather x1, blocking collectives, on_device(): near = lax.all_gather(normed, 'zh', axis=0, tiled=True)  25.8 us
    all_to_all x1, starting transfers between devices, on_device(): left_all = lax.all_to_all(left, COL, 0, 0, tiled=True).reshape(384, 128)  8.37 us
    all_to_all x1, waiting for transfers between devices, on_device(): weights = lax.all_to_all(packed, COL, 0, 0, tiled=True)  7.27 us
    pallas_call x1, Pallas kernels, on_device(): pl.pallas_call(outer_kernel, out_shape=shape(24, 48, 128), scratch_shapes...  6.4 us
    all_to_all x1, starting transfers between devices, on_device(): weights = lax.all_to_all(packed, COL, 0, 0, tiled=True)  6.34 us
    all_to_all x1, waiting for transfers between devices, on_device(): left_all = lax.all_to_all(left, COL, 0, 0, tiled=True).reshape(384, 128)  6.02 us
    ppermute x1, starting transfers between devices, on_device(): right = lax.ppermute(right, ALL, to_columns())  5.19 us
  transfers between devices with their start and end apart: 3, of which 3 were waited for; matrix products, arithmetic and copies ran while one was open for 0% of the time, Pallas kernels for 0%

profile of v1, /device:TPU:2, one launch (start us, length us, event | category | flops | bytes accessed | tf_op | source)
XLA Modules:
  0.0 128.4 jit_solution(13546978435741366637)
XLA Ops:
  0.6 0.0 copy-start.7
  0.6 0.6 copy-done.7
  1.3 0.0 copy-start.2
  1.3 0.8 copy-done.2
  2.1 0.0 copy-start.4
  2.1 0.9 copy-done.4
  3.0 1.2 shard_map.131
  4.2 25.8 %all_gather.9 = f32[192,128]{1,0:T(8,128)S(1)} all-gather(f32[48,128]{1,0:T(8,128)S(1)} %get-tuple-element.8.normed_ref), channel_id=1, replica_groups=mesh['y'=4,'zh'=4,'core'=2,'zl'=4,'x'=4] {'zh'}, dimensions={0}, use_global_device_ids=true | all-gather | bytes 122880 | tf_op jit(solution)/shard_map/all_gather | solution.py:247
  29.9 11.6 %all_to_all.25 = f32[4,192,128]{2,1,0:T(8,128)S(1)} all-to-all(f32[4,192,128]{2,1,0:T(8,128)S(1)} %broadcast_in_dim.32), channel_id=1, replica_groups=mesh['y'=4,'zh'=4,'core'=2,'zl'=4,'x'=4] {'y'}, dimensions={0} | all-to-all | bytes 786432 | tf_op jit(solution)/shard_map/all_to_all | solution.py:204
  41.6 0.0 copy-start.10
  41.6 6.3 %all-to-all-start = ((f32[16,72,128]{2,1,0:T(8,128)}), f32[16,72,128]{2,1,0:T(8,128)S(1)}, u32[]{:S(2)}, u32[]{:S(2)}) async-start(f32[16,72,128]{2,1,0:T(8,128)} %get-tuple-element.7), calls=%async_computation | async-start | bytes 1179648 | tf_op jit(solution)/shard_map/all_to_all | solution.py:246
  47.9 0.0 copy-done.10
  47.9 0.0 copy-start.11
  47.9 0.1 copy.16.output_ref
  48.0 0.6 copy-done.11
  48.7 0.0 copy-start.12
  48.7 0.1 copy.15
  48.7 0.6 copy-done.12
  49.4 0.1 copy.14
  49.5 0.1 pad_maximum_fusion.sides_ref
  49.6 0.0 copy-start.3
  49.6 0.0 copy-start.5
  49.6 0.0 copy-start.6
  49.6 2.5 %all_gather.10 = f32[1536,128]{1,0:T(8,128)S(1)} all-gather(f32[768,128]{1,0:T(8,128)S(1)} %bitcast.13), channel_id=1, replica_groups=mesh['y'=4,'zh'=4,'core'=2,'zl'=4,'x'=4] {'core'}, dimensions={0}, use_global_device_ids=true | all-gather | bytes 1179648 | tf_op jit(solution)/shard_map/all_gather | solution.py:249
  52.1 7.3 %all-to-all-done.weights_ref = f32[16,72,128]{2,1,0:T(8,128)S(1)} async-done(((f32[16,72,128]{2,1,0:T(8,128)}), f32[16,72,128]{2,1,0:T(8,128)S(1)}, u32[]{:S(2)}, u32[]{:S(2)}) %all-to-all-start) | async-done | bytes 589856 | tf_op jit(solution)/shard_map/all_to_all | solution.py:246
  59.4 0.0 copy-start.9
  59.4 0.0 copy-done.3
  59.4 0.0 copy-done.5
  59.4 0.0 copy-done.6
  59.4 0.6 copy-done.9
  60.0 2.7 %shard_map.132 = (f32[24,4,64]{2,1,0:T(4,128)}, f32[16,24,128]{2,1,0:T(8,128)}, f32[24,128]{1,0:T(8,128)S(1)}) custom-call(f32[16,72,128]{2,1,0:T(8,128)S(1)} %all-to-all-done.weights_ref, f32[32,48,128]{2,1,0:T(8,128)S(1)} %bitcast.8, f32[48,128]{1,0:T(8,128)S(1)} %get-tuple-element.8.normed_ref, f32[24,4,64]{2,1,0:T(4,128)S(1)} %copy-done.3, ...), custom_call_target="tpu_custom_call" | custom-call | tf_op jit(solution)/shard_map/pallas_call | solution.py:252
  62.7 5.2 %collective-permute-start = (f32[24,128]{1,0:T(8,128)S(1)}, f32[24,128]{1,0:T(8,128)S(1)}, u32[]{:S(2)}, u32[]{:S(2)}) collective-permute-start(f32[24,128]{1,0:T(8,128)S(1)} %get-tuple-element.11), channel_id=1, source_target_pairs={{0,0},{1,32},{2,64},{3,96},{4,128},{5,160},{6,192},{7,224},{8,256}... | collective-permute-start | bytes 36872 | tf_op jit(solution)/shard_map/ppermute | solution.py:269
  67.9 5.2 %collective-permute-done = f32[24,128]{1,0:T(8,128)S(1)} collective-permute-done((f32[24,128]{1,0:T(8,128)S(1)}, f32[24,128]{1,0:T(8,128)S(1)}, u32[]{:S(2)}, u32[]{:S(2)}) %collective-permute-start) | collective-permute-done | bytes 12320 | tf_op jit(solution)/shard_map/ppermute | solution.py:269
  73.1 22.9 %all_to_all.26 = f32[4,24,128]{2,1,0:T(8,128)S(1)} all-to-all(f32[4,24,128]{2,1,0:T(8,128)S(1)} %broadcast_in_dim.35), channel_id=1, replica_groups=mesh['y'=4,'zh'=4,'core'=2,'zl'=4,'x'=4] {'zh'}, dimensions={0} | all-to-all | bytes 98304 | tf_op jit(solution)/shard_map/all_to_all | solution.py:204
  96.1 0.0 copy-start.1
  96.1 8.8 %all_to_all.27 = f32[4,96,128]{2,1,0:T(8,128)S(1)} all-to-all(f32[4,96,128]{2,1,0:T(8,128)S(1)} %broadcast_in_dim.37), channel_id=1, replica_groups=mesh['y'=4,'zh'=4,'core'=2,'zl'=4,'x'=4] {'y'}, dimensions={0} | all-to-all | bytes 393216 | tf_op jit(solution)/shard_map/all_to_all | solution.py:204
  104.9 0.0 copy-start
  104.9 8.4 %all-to-all-start.2 = ((f32[16,24,128]{2,1,0:T(8,128)}), f32[16,24,128]{2,1,0:T(8,128)S(1)}, u32[]{:S(2)}, u32[]{:S(2)}) async-start(f32[16,24,128]{2,1,0:T(8,128)} %get-tuple-element.10), calls=%async_computation.2 | async-start | bytes 393216 | tf_op jit(solution)/shard_map/all_to_all | solution.py:268
  113.3 2.1 %all_gather.11.right_ref = f32[768,128]{1,0:T(8,128)S(1)} all-gather(f32[384,128]{1,0:T(8,128)S(1)} %bitcast.14), channel_id=1, replica_groups=mesh['y'=4,'zh'=4,'core'=2,'zl'=4,'x'=4] {'core'}, dimensions={0}, use_global_device_ids=true | all-gather | bytes 589824 | tf_op jit(solution)/shard_map/all_gather | solution.py:272
  115.3 6.0 %all-to-all-done.2 = f32[16,24,128]{2,1,0:T(8,128)S(1)} async-done(((f32[16,24,128]{2,1,0:T(8,128)}), f32[16,24,128]{2,1,0:T(8,128)S(1)}, u32[]{:S(2)}, u32[]{:S(2)}) %all-to-all-start.2) | async-done | bytes 196640 | tf_op jit(solution)/shard_map/all_to_all | solution.py:268
  121.4 0.0 copy-start.8
  121.4 0.0 copy-done.1
  121.4 0.0 copy-done
  121.4 0.6 copy-done.8
  122.0 6.4 %shard_map.133 = f32[24,48,128]{2,1,0:T(8,128)} custom-call(f32[384,128]{1,0:T(8,128)S(1)} %bitcast.9, f32[768,128]{1,0:T(8,128)S(1)} %all_gather.11.right_ref, f32[24,48,128]{2,1,0:T(8,128)S(1)} %copy-done, f32[1024,128]{1,0:T(8,128)S(1)} %copy-done.1, f32[1,128]{1,0:T(1,128)S(1)} %bitcast.11), custom_call_target="tpu_custom_call" | custom-call | tf_op jit(solution)/shard_map/pallas_call | solution.py:273
  (4 shorter events, 0.0 us)
Async XLA Ops:
  0.6 0.7 copy-start.7
  1.3 0.8 copy-start.2
  2.1 0.9 copy-start.4
  41.6 6.3 %copy-start.10 = (f32[256,64]{0,1:T(8,128)S(1)}, f32[256,64]{0,1:T(8,128)}, u32[]{:S(2)}) copy-start(f32[256,64]{0,1:T(8,128)} %param.18) | copy-start | bytes 196612
  41.6 17.8 %all-to-all-start = ((f32[16,72,128]{2,1,0:T(8,128)}), f32[16,72,128]{2,1,0:T(8,128)S(1)}, u32[]{:S(2)}, u32[]{:S(2)}) async-start(f32[16,72,128]{2,1,0:T(8,128)} %get-tuple-element.7), calls=%async_computation | async-start | bytes 1179648 | tf_op jit(solution)/shard_map/all_to_all | solution.py:246
  47.9 0.7 copy-start.11
  48.7 0.7 copy-start.12
  49.6 9.8 %copy-start.3 = (f32[24,4,64]{2,1,0:T(4,128)S(1)}, f32[24,4,64]{2,1,0:T(4,128)}, u32[]{:S(2)}) copy-start(f32[24,4,64]{2,1,0:T(4,128)} %align_ref.3) | copy-start | bytes 73732
  49.6 9.8 %copy-start.5 = (f32[64,256]{1,0:T(8,128)S(1)}, f32[64,256]{1,0:T(8,128)}, u32[]{:S(2)}) copy-start(f32[64,256]{1,0:T(8,128)} %value_ref.1) | copy-start | bytes 196612
  49.6 9.8 %copy-start.6 = (f32[64,256]{1,0:T(8,128)S(1)}, f32[64,256]{1,0:T(8,128)}, u32[]{:S(2)}) copy-start(f32[64,256]{1,0:T(8,128)} %gate_ref.1) | copy-start | bytes 196612
  59.4 0.7 copy-start.9
  62.7 10.4 %collective-permute-start = (f32[24,128]{1,0:T(8,128)S(1)}, f32[24,128]{1,0:T(8,128)S(1)}, u32[]{:S(2)}, u32[]{:S(2)}) collective-permute-start(f32[24,128]{1,0:T(8,128)S(1)} %get-tuple-element.11), channel_id=1, source_target_pairs={{0,0},{1,32},{2,64},{3,96},{4,128},{5,160},{6,192},{7,224},{8,256}... | collective-permute-start | bytes 36872 | tf_op jit(solution)/shard_map/ppermute | solution.py:269
  96.1 25.3 %copy-start.1 = (f32[1024,128]{1,0:T(8,128)S(1)}, f32[1024,128]{1,0:T(8,128)}, u32[]{:S(2)}) copy-start(f32[1024,128]{1,0:T(8,128)} %outer_ref.1) | copy-start | bytes 1572868
  104.9 16.5 %copy-start = (f32[24,48,128]{2,1,0:T(8,128)S(1)}, f32[24,48,128]{2,1,0:T(8,128)}, u32[]{:S(2)}) copy-start(f32[24,48,128]{2,1,0:T(8,128)} %state_ref.1) | copy-start | bytes 1769476
  104.9 16.5 %all-to-all-start.2 = ((f32[16,24,128]{2,1,0:T(8,128)}), f32[16,24,128]{2,1,0:T(8,128)S(1)}, u32[]{:S(2)}, u32[]{:S(2)}) async-start(f32[16,24,128]{2,1,0:T(8,128)} %get-tuple-element.10), calls=%async_computation.2 | async-start | bytes 393216 | tf_op jit(solution)/shard_map/all_to_all | solution.py:268
  121.4 0.7 copy-start.8

commit v2 on v1

--- a/solution.py
+++ b/solution.py
@@ -245,6 +245,7 @@
     )(alignment, pair_weights, align_gain[None])
     weights = lax.all_to_all(packed, COL, 0, 0, tiled=True)
     near = lax.all_gather(normed, "zh", axis=0, tiled=True)
+    near, weights = lax.optimization_barrier((near, weights))
     wide = everyone(near, "y").reshape(16 * 48, 128)
     gathered = lax.all_gather(wide, "core", axis=0, tiled=True).reshape(32, 48, 128)
     pad = jnp.zeros((64, 96), F32)
@@ -267,6 +268,7 @@
     )
     left_all = lax.all_to_all(left, COL, 0, 0, tiled=True).reshape(384, 128)
     right = lax.ppermute(right, ALL, to_columns())
+    right, left_all = lax.optimization_barrier((right, left_all))
     right = everyone(right, "zh").reshape(96, 128)
     right = everyone(right, "y").reshape(384, 128)
     right_all = lax.all_gather(right, "core", axis=0, tiled=True)

time: 129 us -> 126 us (0.977)
  the two profiles are of different devices: /device:TPU:2 before, /device:TPU:1 now
where the time goes in v2:
time: 126 us; the launch traced here: 125 us
  blocking collectives  71.3 us (57%)
  starting transfers between devices  24 us (19%)
  waiting for transfers between devices  13.4 us (11%)
  Pallas kernels  10.3 us (8%)
  local copies, waits for them, and re-layouts  5.38 us (4%)
    all_to_all x2, blocking collectives, everyone(): return lax.all_to_all(copies(value, axis), axis, 0, 0, tiled=True)  32.3 us
    all_gather x1, blocking collectives, on_device(): near = lax.all_gather(normed, 'zh', axis=0, tiled=True)  25.3 us
    all_to_all x1, starting transfers between devices, on_device(): left_all = lax.all_to_all(left, COL, 0, 0, tiled=True).reshape(384, 128)  10.1 us
    all_to_all x1, starting transfers between devices, on_device(): weights = lax.all_to_all(packed, COL, 0, 0, tiled=True)  9.01 us
    all_to_all x1, waiting for transfers between devices, on_device(): left_all = lax.all_to_all(left, COL, 0, 0, tiled=True).reshape(384, 128)  8.19 us
    all_gather x1, blocking collectives, on_device(): lax.all_gather(wide, 'core', axis=0, tiled=True).reshape(32, 48, 128)  7.28 us
    all_gather x1, blocking collectives, on_device(): right_all = lax.all_gather(right, 'core', axis=0, tiled=True)  6.47 us
    pallas_call x1, Pallas kernels, on_device(): pl.pallas_call(outer_kernel, out_shape=shape(24, 48, 128), scratch_shapes...  6.39 us
  transfers between devices with their start and end apart: 4, of which 2 were waited for; matrix products, arithmetic and copies ran while one was open for 0% of the time, Pallas kernels for 0%

profile of v2, /device:TPU:1, one launch (start us, length us, event | category | flops | bytes accessed | tf_op | source)
XLA Modules:
  0.0 125.2 jit_solution(2556964776840426164)
XLA Ops:
  0.6 0.0 copy-start.7
  0.6 0.6 copy-done.7
  1.3 0.0 copy-start.2
  1.3 0.8 copy-done.2
  2.1 0.0 copy-start.4
  2.1 0.9 copy-done.4
  3.0 1.2 shard_map.131
  4.2 9.0 %all-to-all-start = ((f32[16,72,128]{2,1,0:T(8,128)}), f32[16,72,128]{2,1,0:T(8,128)S(1)}, u32[]{:S(2)}, u32[]{:S(2)}) async-start(f32[16,72,128]{2,1,0:T(8,128)} %get-tuple-element.12), calls=%async_computation | async-start | bytes 1179648 | tf_op jit(solution)/shard_map/all_to_all | solution.py:246
  13.2 25.3 %all_gather.9 = f32[192,128]{1,0:T(8,128)S(1)} all-gather(f32[48,128]{1,0:T(8,128)S(1)} %get-tuple-element.11.normed_ref), channel_id=1, replica_groups=mesh['y'=4,'zh'=4,'core'=2,'zl'=4,'x'=4] {'zh'}, dimensions={0}, use_global_device_ids=true | all-gather | bytes 122880 | tf_op jit(solution)/shard_map/all_gather | solution.py:247
  38.5 0.0 all-to-all-done.weights_ref
  38.5 0.8 broadcast_in_dim.32
  39.3 0.0 copy-start.11
  39.3 0.0 copy-start.12
  39.3 4.3 %all-to-all-start.1 = ((f32[4,192,128]{2,1,0:T(8,128)}), f32[4,192,128]{2,1,0:T(8,128)S(1)}, u32[]{:S(2)}, u32[]{:S(2)}) async-start(f32[4,192,128]{2,1,0:T(8,128)} %broadcast_in_dim.32), calls=%async_computation.1 | async-start | bytes 786432 | tf_op jit(solution)/shard_map/all_to_all | solution.py:204
  43.6 0.0 copy-done.11
  43.6 0.0 copy-start.10
  43.6 0.1 copy.14
  43.7 0.0 copy-done.12
  43.7 0.1 copy.15
  43.8 0.7 copy-done.10
  44.4 0.1 copy.16.output_ref
  44.5 0.1 pad_maximum_fusion.sides_ref
  44.6 5.2 %all-to-all-done.1 = f32[4,192,128]{2,1,0:T(8,128)S(1)} async-done(((f32[4,192,128]{2,1,0:T(8,128)}), f32[4,192,128]{2,1,0:T(8,128)S(1)}, u32[]{:S(2)}, u32[]{:S(2)}) %all-to-all-start.1) | async-done | bytes 393248 | tf_op jit(solution)/shard_map/all_to_all | solution.py:204
  49.8 0.0 copy-start.3
  49.8 0.0 copy-start.5
  49.8 0.0 copy-start.6
  49.8 7.3 %all_gather.10 = f32[1536,128]{1,0:T(8,128)S(1)} all-gather(f32[768,128]{1,0:T(8,128)S(1)} %bitcast.13), channel_id=1, replica_groups=mesh['y'=4,'zh'=4,'core'=2,'zl'=4,'x'=4] {'core'}, dimensions={0}, use_global_device_ids=true | all-gather | bytes 1179648 | tf_op jit(solution)/shard_map/all_gather | solution.py:250
  57.1 0.0 copy-start.9
  57.1 0.0 copy-done.3
  57.1 0.0 copy-done.5
  57.1 0.0 copy-done.6
  57.1 0.6 copy-done.9
  57.8 2.7 %shard_map.132 = (f32[24,4,64]{2,1,0:T(4,128)}, f32[16,24,128]{2,1,0:T(8,128)}, f32[24,128]{1,0:T(8,128)S(1)}) custom-call(f32[16,72,128]{2,1,0:T(8,128)S(1)} %all-to-all-done.weights_ref, f32[32,48,128]{2,1,0:T(8,128)S(1)} %bitcast.8, f32[48,128]{1,0:T(8,128)S(1)} %get-tuple-element.11.normed_ref, f32[24,4,64]{2,1,0:T(4,128)S(1)} %copy-done.3, ...), custom_call_target="tpu_custom_call" | custom-call | tf_op jit(solution)/shard_map/pallas_call | solution.py:253
  60.5 10.1 %all-to-all-start.2 = ((f32[16,24,128]{2,1,0:T(8,128)}), f32[16,24,128]{2,1,0:T(8,128)S(1)}, u32[]{:S(2)}, u32[]{:S(2)}) async-start(f32[16,24,128]{2,1,0:T(8,128)} %get-tuple-element.17), calls=%async_computation.2 | async-start | bytes 393216 | tf_op jit(solution)/shard_map/all_to_all | solution.py:269
  70.6 0.7 collective-permute-start
  71.2 0.0 collective-permute-done
  71.2 8.2 %all-to-all-done.2 = f32[16,24,128]{2,1,0:T(8,128)S(1)} async-done(((f32[16,24,128]{2,1,0:T(8,128)}), f32[16,24,128]{2,1,0:T(8,128)S(1)}, u32[]{:S(2)}, u32[]{:S(2)}) %all-to-all-start.2) | async-done | bytes 196640 | tf_op jit(solution)/shard_map/all_to_all | solution.py:269
  79.4 24.6 %all_to_all.25 = f32[4,24,128]{2,1,0:T(8,128)S(1)} all-to-all(f32[4,24,128]{2,1,0:T(8,128)S(1)} %broadcast_in_dim.35), channel_id=1, replica_groups=mesh['y'=4,'zh'=4,'core'=2,'zl'=4,'x'=4] {'zh'}, dimensions={0} | all-to-all | bytes 98304 | tf_op jit(solution)/shard_map/all_to_all | solution.py:204
  104.0 0.0 copy-start
  104.0 0.0 copy-start.1
  104.0 7.7 %all_to_all.26 = f32[4,96,128]{2,1,0:T(8,128)S(1)} all-to-all(f32[4,96,128]{2,1,0:T(8,128)S(1)} %broadcast_in_dim.37), channel_id=1, replica_groups=mesh['y'=4,'zh'=4,'core'=2,'zl'=4,'x'=4] {'y'}, dimensions={0} | all-to-all | bytes 393216 | tf_op jit(solution)/shard_map/all_to_all | solution.py:204
  111.7 6.5 %all_gather.11.right_ref = f32[768,128]{1,0:T(8,128)S(1)} all-gather(f32[384,128]{1,0:T(8,128)S(1)} %bitcast.14), channel_id=1, replica_groups=mesh['y'=4,'zh'=4,'core'=2,'zl'=4,'x'=4] {'core'}, dimensions={0}, use_global_device_ids=true | all-gather | bytes 589824 | tf_op jit(solution)/shard_map/all_gather | solution.py:274
  118.2 0.0 copy-start.8
  118.2 0.0 copy-done
  118.2 0.0 copy-done.1
  118.2 0.6 copy-done.8
  118.8 6.4 %shard_map.133 = f32[24,48,128]{2,1,0:T(8,128)} custom-call(f32[384,128]{1,0:T(8,128)S(1)} %bitcast.9, f32[768,128]{1,0:T(8,128)S(1)} %all_gather.11.right_ref, f32[24,48,128]{2,1,0:T(8,128)S(1)} %copy-done, f32[1024,128]{1,0:T(8,128)S(1)} %copy-done.1, f32[1,128]{1,0:T(1,128)S(1)} %bitcast.11), custom_call_target="tpu_custom_call" | custom-call | tf_op jit(solution)/shard_map/pallas_call | solution.py:275
  (3 shorter events, 0.0 us)
Async XLA Ops:
  0.6 0.7 copy-start.7
  1.3 0.8 copy-start.2
  2.1 0.9 copy-start.4
  4.2 34.4 %all-to-all-start = ((f32[16,72,128]{2,1,0:T(8,128)}), f32[16,72,128]{2,1,0:T(8,128)S(1)}, u32[]{:S(2)}, u32[]{:S(2)}) async-start(f32[16,72,128]{2,1,0:T(8,128)} %get-tuple-element.12), calls=%async_computation | async-start | bytes 1179648 | tf_op jit(solution)/shard_map/all_to_all | solution.py:246
  39.3 4.3 %copy-start.11 = (f32[64,32]{0,1:T(8,128)S(1)}, f32[64,32]{0,1:T(8,128)}, u32[]{:S(2)}) copy-start(f32[64,32]{0,1:T(8,128)} %param.20) | copy-start | bytes 24580
  39.3 4.4 %copy-start.12 = (f32[64,32]{0,1:T(8,128)S(1)}, f32[64,32]{0,1:T(8,128)}, u32[]{:S(2)}) copy-start(f32[64,32]{0,1:T(8,128)} %param.21) | copy-start | bytes 24580
  39.3 10.5 %all-to-all-start.1 = ((f32[4,192,128]{2,1,0:T(8,128)}), f32[4,192,128]{2,1,0:T(8,128)S(1)}, u32[]{:S(2)}, u32[]{:S(2)}) async-start(f32[4,192,128]{2,1,0:T(8,128)} %broadcast_in_dim.32), calls=%async_computation.1 | async-start | bytes 786432 | tf_op jit(solution)/shard_map/all_to_all | solution.py:204
  43.6 0.8 copy-start.10
  49.8 7.3 %copy-start.3 = (f32[24,4,64]{2,1,0:T(4,128)S(1)}, f32[24,4,64]{2,1,0:T(4,128)}, u32[]{:S(2)}) copy-start(f32[24,4,64]{2,1,0:T(4,128)} %align_ref.3) | copy-start | bytes 73732
  49.8 7.3 %copy-start.5 = (f32[64,256]{1,0:T(8,128)S(1)}, f32[64,256]{1,0:T(8,128)}, u32[]{:S(2)}) copy-start(f32[64,256]{1,0:T(8,128)} %value_ref.1) | copy-start | bytes 196612
  49.8 7.3 %copy-start.6 = (f32[64,256]{1,0:T(8,128)S(1)}, f32[64,256]{1,0:T(8,128)}, u32[]{:S(2)}) copy-start(f32[64,256]{1,0:T(8,128)} %gate_ref.1) | copy-start | bytes 196612
  57.1 0.7 copy-start.9
  60.5 18.9 %all-to-all-start.2 = ((f32[16,24,128]{2,1,0:T(8,128)}), f32[16,24,128]{2,1,0:T(8,128)S(1)}, u32[]{:S(2)}, u32[]{:S(2)}) async-start(f32[16,24,128]{2,1,0:T(8,128)} %get-tuple-element.17), calls=%async_computation.2 | async-start | bytes 393216 | tf_op jit(solution)/shard_map/all_to_all | solution.py:269
  70.6 0.7 collective-permute-start
  104.0 14.2 %copy-start = (f32[24,48,128]{2,1,0:T(8,128)S(1)}, f32[24,48,128]{2,1,0:T(8,128)}, u32[]{:S(2)}) copy-start(f32[24,48,128]{2,1,0:T(8,128)} %state_ref.1) | copy-start | bytes 1769476
  104.0 14.2 %copy-start.1 = (f32[1024,128]{1,0:T(8,128)S(1)}, f32[1024,128]{1,0:T(8,128)}, u32[]{:S(2)}) copy-start(f32[1024,128]{1,0:T(8,128)} %outer_ref.1) | copy-start | bytes 1572868
  118.2 0.7 copy-start.8

commit v3 on v1

v3 whole, which is shorter than its diff:
```python
import functools

import jax
import jax.numpy as jnp
from jax import lax
from jax.experimental import pallas as pl
from jax.experimental.pallas import tpu as pltpu
from jax.sharding import Mesh, PartitionSpec as P

F32 = jnp.float32
BF16 = jnp.bfloat16
ROW = ("y", "zh", "core")
COL = ("zl", "x")
ALL = ROW + COL
LANES = 128
HALVES = (slice(0, 64), slice(64, 128))


def split(value):
    high = value.astype(BF16)
    low = (value - high.astype(F32)).astype(BF16)
    return high, low


def dot(a, b):
    return jnp.dot(a, b, preferred_element_type=F32)


def dot3(a, b):
    ah, al = split(a)
    bh, bl = split(b)
    return dot(ah, bh) + (dot(ah, bl) + dot(al, bh))


def normalize(features, gain):
    mean = jnp.mean(features, axis=-1, keepdims=True)
    centered = features - mean
    spread = jnp.mean(centered * centered, axis=-1, keepdims=True)
    return centered * lax.rsqrt(spread + 1e-05) * gain


def twice(weight):
    zeros = jnp.zeros_like(weight)
    return jnp.concatenate(
        [jnp.concatenate([weight, zeros], 1), jnp.concatenate([zeros, weight], 1)], 0
    )


def fill(ref, value):
    if len(ref.shape) == 2:
        ref[...] = value
    else:
        for k in range(ref.shape[0]):
            ref[k] = value


def features_kernel(align_ref, gain_ref, normed_ref):
    parts = [normalize(align_ref[:, s, :], gain_ref[...]) for s in range(4)]
    features = jnp.concatenate(
        [jnp.concatenate(parts[0:2], axis=1), jnp.concatenate(parts[2:4], axis=1)], axis=0
    )
    fill(normed_ref, features)


def weights_kernel(pair_w_ref, weights_ref):
    heads, rows, columns = pair_w_ref.shape
    turned = pair_w_ref[...].reshape(heads * rows, columns).T
    half = columns // 2
    tail = turned[:, LANES:]
    tail = jnp.concatenate([tail[:half], tail[half:]], axis=1)
    fill(weights_ref, jnp.concatenate([turned[:, :LANES], tail], axis=0))


def dot3_turned(a, b):
    ah, al = split(a)
    bh, bl = split(b)

    def one(x, y):
        return lax.dot_general(x, y, (((1,), (1,)), ((), ())), preferred_element_type=F32)

    return one(ah, bh) + (one(ah, bl) + one(al, bh))


def landed(row):
    y, zh, core = row // 8, row // 2 % 4, row % 2
    return (y * 2 + core) * 4 + zh


def average_kernel(
    weights_ref,
    gathered_ref,
    align_hbm,
    value_hbm,
    gate_hbm,
    output_hbm,
    left_hbm,
    right_hbm,
    align_gain_hbm,
    outer_gain_hbm,
    out_ref,
    left_ref,
    right_ref,
    align_ref,
    value_ref,
    gate_ref,
    output_ref,
    left_w_ref,
    right_w_ref,
    align_gain_ref,
    outer_gain_ref,
    left_tmp,
    right_tmp,
    arrived,
):
    fetches = [
        pltpu.make_async_copy(source, target, arrived.at[n])
        for n, (source, target) in enumerate(
            [
                (value_hbm, value_ref),
                (align_hbm, align_ref),
                (align_gain_hbm, align_gain_ref),
                (gate_hbm, gate_ref),
                (output_hbm, output_ref),
                (left_hbm, left_w_ref),
                (right_hbm, right_w_ref),
                (outer_gain_hbm, outer_gain_ref),
            ]
        )
    ]
    for fetch in fetches:
        fetch.start()
    rows = align_ref.shape[0]
    columns = 2 * rows
    heads = 8
    first = weights_ref[:, 0:columns, :].reshape(-1, LANES)
    tails = [weights_ref[k, columns:, :] for k in range(16)]
    second = jnp.concatenate([t[:, half] for t in tails for half in HALVES], axis=0)
    weights = jnp.concatenate([first.T, second.T], axis=0)
    wh, wl = split(weights)
    mixed = []
    for p in range(2):
        blocks = [
            gathered_ref[landed(r), p * rows : (p + 1) * rows, :] for r in range(32)
        ]
        fh, fl = split(jnp.concatenate(blocks, axis=0))
        mixed.append(dot(wh, fh) + (dot(wh, fl) + dot(wl, fh)))
    for fetch in fetches:
        fetch.wait()
    lane = lax.broadcasted_iota(jnp.int32, (rows, 512), 1)
    lane_head = lax.rem(lax.div(lane, 32), heads)
    vh, vl = split(twice(value_ref[...]))
    gate2 = twice(gate_ref[...])
    own = [normalize(align_ref[:, s, :], align_gain_ref[...]) for s in range(4)]
    gated = []
    for p in range(2):
        mh, ml = split(mixed[p])
        by_head = dot(mh, vh) + (dot(mh, vl) + dot(ml, vh))
        averaged = jnp.zeros((rows, 512), F32)
        for h in range(heads):
            averaged += jnp.where(lane_head == h, by_head[h * rows : (h + 1) * rows], 0.0)
        gate = jax.nn.sigmoid(dot3(jnp.concatenate(own[2 * p : 2 * p + 2], axis=1), gate2))
        product = gate * averaged
        gated += [product[:, :256], product[:, 256:]]
    update = dot3_turned(jnp.concatenate(gated, axis=0), output_ref[...])
    aligned = jnp.concatenate([align_ref[:, s, :] for s in range(4)], axis=0) + update
    for s in range(4):
        out_ref[:, s, :] = aligned[s * rows : (s + 1) * rows]
    normed = normalize(aligned, outer_gain_ref[...])
    left_tmp[:, 0:32] = dot3_turned(normed, left_w_ref[...])
    right_tmp[:, 0:32] = dot3_turned(normed, right_w_ref[...])
    left = jnp.concatenate(
        [left_tmp[pl.ds(k, rows, stride=4), 0:32] for k in range(4)], axis=1
    )
    right = jnp.concatenate(
        [right_tmp[pl.ds(k, rows, stride=4), 0:32] for k in range(4)], axis=1
    )
    fill(left_ref, left)
    fill(right_ref, right)


CHUNK = 8


def outer_kernel(
    left_ref,
    right_ref,
    state_ref,
    outer_ref,
    bias_hbm,
    out_ref,
    turned,
    spread_h,
    spread_l,
    total,
    bias_ref,
    arrived,
):
    fetch = pltpu.make_async_copy(bias_hbm, bias_ref, arrived)
    fetch.start()
    lefts = [left_ref[pl.ds(g, 64, stride=6), :] * (1.0 / 64.0) for g in range(6)]
    lh, ll = split(jnp.concatenate(lefts, axis=1))
    left4 = jnp.concatenate([lh, lh, ll, ll], axis=0)
    for core in range(2):
        for g in range(6):
            block = right_ref[pl.ds(core * 384 + g, 64, stride=6), :]
            high = block.astype(BF16).astype(F32)
            stacked = jnp.concatenate([high, block - high], axis=0)
            turned[(core * 6 + g) * LANES : (core * 6 + g + 1) * LANES, :] = stacked.T
    spread_h[...] = jnp.zeros_like(spread_h)
    spread_l[...] = jnp.zeros_like(spread_l)
    low_lanes = lax.broadcasted_iota(jnp.int32, (48, LANES), 1) < 64
    for t in range(32 // CHUNK):
        rights = []
        for e in range(CHUNK):
            d = t * CHUNK + e
            right = turned[pl.ds(d, 48, stride=32), :].astype(BF16)
            rights.append(jnp.concatenate([right, right], axis=1))
            wh, wl = split(outer_ref[pl.ds(d, 32, stride=32), :])
            for k in range(2):
                at = (pl.ds(e * 64 + 32 * k, 32), pl.ds(k * LANES, LANES))
                spread_h[at] = wh
                spread_l[at] = wl
        product = dot(jnp.concatenate(rights, axis=0), left4)
        rows = []
        for g in range(6):
            halves = [[], []]
            for e in range(0, CHUNK, 2):
                lanes = slice(g * LANES, (g + 1) * LANES)
                first = product[e * 48 : (e + 1) * 48, lanes]
                second = product[(e + 1) * 48 : (e + 2) * 48, lanes]
                halves[0].append(jnp.where(low_lanes, first, pltpu.roll(second, 64, 1)))
                halves[1].append(jnp.where(low_lanes, pltpu.roll(first, 64, 1), second))
            rows += [jnp.concatenate(half, axis=1) for half in halves]
        ah, al = split(jnp.concatenate(rows, axis=0))
        bh, bl = spread_h[...], spread_l[...]
        step = dot(
            jnp.concatenate([ah, ah, al], axis=1), jnp.concatenate([bh, bl, bh], axis=0)
        )
        if t == 0:
            total[...] = step
        else:
            total[...] += step
    fetch.wait()
    for g in range(6):
        for k in range(4):
            start = (g * 2 + k // 2) * 48
            out_ref[g * 4 + k] = (
                state_ref[g * 4 + k]
                + total[start : start + 48, (k % 2) * LANES : (k % 2 + 1) * LANES]
                + bias_ref[...]
            )


def copies(value, axis):
    return jnp.broadcast_to(value[None], (lax.axis_size(axis), *value.shape))


def everyone(value, axis):
    return lax.all_to_all(copies(value, axis), axis, 0, 0, tiled=True)


def mirrored():
    sides = [((a, b), (b, a)) for a in range(4) for b in range(a + 1, 4)]
    sides += [((a, a), (a + 1, a + 1)) for a in (0, 2)]

    def index(y, zh, core, zl, x):
        return (((y * 4 + zh) * 2 + core) * 4 + zl) * 4 + x

    return [
        [index(y, zh, core, zl, x) for y, zl in pair for zh in range(4)]
        for core in range(2)
        for x in range(4)
        for pair in sides
    ]


VMEM = pl.BlockSpec(memory_space=pltpu.VMEM)
HBM = pl.BlockSpec(memory_space=pltpu.HBM)
PREPARE = pltpu.CompilerParams(vmem_limit_bytes=62 * 1024 * 1024)
PARAMS = pltpu.CompilerParams(vmem_limit_bytes=48 * 1024 * 1024)


def shape(*dims):
    return jax.ShapeDtypeStruct(dims, F32)


def first_exchange(alignment, pair_weights, align_gain):
    normed = pl.pallas_call(
        features_kernel, out_shape=shape(4, 48, 128), compiler_params=PREPARE
    )(alignment, align_gain)
    packed = pl.pallas_call(
        weights_kernel, out_shape=shape(16, 72, 128), compiler_params=PREPARE
    )(pair_weights)
    near = lax.all_to_all(normed, "zh", 0, 0, tiled=True).reshape(192, 128)
    near, packed = lax.optimization_barrier((near, packed))
    weights = lax.all_to_all(packed, COL, 0, 0, tiled=True)
    gathered = lax.all_gather(near, ("y", "core"), axis=0, tiled=True).reshape(32, 48, 128)
    return gathered, weights


def on_device(
    alignment,
    pair_state,
    pair_weights,
    align_gain,
    value_weight,
    gate_weight,
    output_weight,
    outer_gain,
    left_weight,
    right_weight,
    outer_weight,
    outer_bias,
):
    align_gain, outer_gain = align_gain[None], outer_gain[None]
    gathered, weights = first_exchange(alignment, pair_weights, align_gain)
    params = (
        alignment,
        value_weight,
        gate_weight,
        output_weight.T,
        left_weight.T,
        right_weight.T,
        align_gain,
        outer_gain,
    )
    alignment_out, left, right = pl.pallas_call(
        average_kernel,
        in_specs=[VMEM, VMEM] + [HBM] * len(params),
        out_specs=[VMEM] * 3,
        out_shape=(shape(24, 4, 64), shape(16, 24, 128), shape(8, 24, 128)),
        scratch_shapes=[pltpu.VMEM(p.shape, F32) for p in params]
        + [
            pltpu.VMEM((96, 128), F32),
            pltpu.VMEM((96, 128), F32),
            pltpu.SemaphoreType.DMA((len(params),)),
        ],
        compiler_params=PARAMS,
    )(weights, gathered, *params)
    right = lax.all_to_all(right, ALL, 0, 0, axis_index_groups=mirrored(), tiled=True)
    y, zl = lax.axis_index("y"), lax.axis_index("zl")
    side = jnp.where(y == zl, y % 2, jnp.where(y < zl, 1, 0))
    right = lax.dynamic_slice_in_dim(right, side * 4, 4, axis=0)
    right = jnp.broadcast_to(right[None], (4, *right.shape)).reshape(16, 24, 128)
    right = lax.all_to_all(right, ("y", "x"), 0, 0, tiled=True).reshape(384, 128)
    right, left = lax.optimization_barrier((right, left))
    left_all = lax.all_to_all(left, COL, 0, 0, tiled=True).reshape(384, 128)
    right_all = lax.all_gather(right, "core", axis=0, tiled=True)
    pair_out = pl.pallas_call(
        outer_kernel,
        in_specs=[VMEM] * 4 + [HBM],
        out_specs=VMEM,
        out_shape=shape(24, 48, 128),
        scratch_shapes=[
            pltpu.VMEM((1536, 128), F32),
            pltpu.VMEM((CHUNK * 64, 256), BF16),
            pltpu.VMEM((CHUNK * 64, 256), BF16),
            pltpu.VMEM((576, 256), F32),
            pltpu.VMEM((1, 128), F32),
            pltpu.SemaphoreType.DMA(()),
        ],
        compiler_params=PARAMS,
    )(left_all, right_all, pair_state, outer_weight, outer_bias[None])
    return alignment_out, pair_out


def solution(mesh):
    torus = Mesh(mesh.devices.reshape(4, 4, 2, 4, 4), ALL)
    return jax.shard_map(
        on_device,
        mesh=torus,
        in_specs=(P(ROW, COL, None), P(ROW, COL, None), P(None, ROW, COL)) + (P(),) * 9,
        out_specs=(P(ROW, COL, None), P(ROW, COL, None)),
        check_vma=False,
    )
```

time: 129 us -> 111 us (0.86)
  blocking collectives: 73.7 us -> 32 us
  waiting for transfers between devices: 18.5 us -> 32.3 us
  starting transfers between devices: 19.9 us -> 31.5 us
  local copies, waits for them, and re-layouts: 5.22 us -> 1.33 us
  Pallas kernels: 10.3 us -> 12.4 us
    all_to_all x3 -> x1, blocking collectives: 43.4 us -> 15.8 us  [on_device(): lax.all_to_all(right, ('y', 'x'), 0, 0, tiled=True).reshape(384, 128)]
    all_to_all x1 -> x3, waiting for transfers between devices: 7.27 us -> 26.3 us  [the longest x1 13.8 us: on_device(): lax.all_to_all(right, ALL, 0, 0, axis_index_groups=mirrored(), tiled=True)]
    all_to_all x1 -> x3, starting transfers between devices: 6.34 us -> 25 us  [the longest x1 15.1 us: first_exchange(): near = lax.all_to_all(normed, 'zh', 0, 0, tiled=True).reshape(192, 128)]
    all_gather x2 -> x1, blocking collectives: 28.3 us -> 14.1 us  [first_exchange(): lax.all_gather(near, ('y', 'core'), axis=0, tiled=True).reshape(32, 48, 128)]
    ppermute x1 -> x0, starting transfers between devices: 5.19 us -> none  [on_device(): right = lax.ppermute(right, ALL, to_columns())]
    ppermute x1 -> x0, waiting for transfers between devices: 5.18 us -> none  [on_device(): right = lax.ppermute(right, ALL, to_columns())]
    unnamed x29 -> x22, local copies, waits for them, and re-layouts: 5.17 us -> 1.31 us
    pallas_call x3 -> x4, Pallas kernels: 10.3 us -> 12.4 us  [the longest x1 5.62 us: on_device(): pl.pallas_call(outer_kernel, in_specs=[VMEM] * 4 + [HBM], out_specs=VMEM,...]
  transfers between devices with their start and end apart: 3 -> 4, of which waited for: 3 -> 3; matrix products, arithmetic and copies ran while one was open for 0% -> 0% of each run, Pallas kernels for 0% -> 2%
where the time goes in v3:
time: 111 us; the launch traced here: 110 us
  waiting for transfers between devices  32.3 us (29%)
  blocking collectives  32 us (29%)
  starting transfers between devices  31.5 us (28%)
  Pallas kernels  12.4 us (11%)
  local copies, waits for them, and re-layouts  1.33 us (1%)
    all_to_all x1, blocking collectives, on_device(): lax.all_to_all(right, ('y', 'x'), 0, 0, tiled=True).reshape(384, 128)  15.8 us
    all_to_all x1, starting transfers between devices, first_exchange(): near = lax.all_to_all(normed, 'zh', 0, 0, tiled=True).reshape(192, 128)  15.1 us
    all_gather x1, blocking collectives, first_exchange(): lax.all_gather(near, ('y', 'core'), axis=0, tiled=True).reshape(32, 48, 128)  14.1 us
    all_to_all x1, waiting for transfers between devices, on_device(): lax.all_to_all(right, ALL, 0, 0, axis_index_groups=mirrored(), tiled=True)  13.8 us
    all_to_all x1, waiting for transfers between devices, first_exchange(): near = lax.all_to_all(normed, 'zh', 0, 0, tiled=True).reshape(192, 128)  12.5 us
    all_to_all x1, starting transfers between devices, on_device(): left_all = lax.all_to_all(left, COL, 0, 0, tiled=True).reshape(384, 128)  6.46 us
    all_to_all x1, starting transfers between devices, first_exchange(): weights = lax.all_to_all(packed, COL, 0, 0, tiled=True)  6.21 us
    all_to_all x1, waiting for transfers between devices, on_device(): left_all = lax.all_to_all(left, COL, 0, 0, tiled=True).reshape(384, 128)  6.02 us
  transfers between devices with their start and end apart: 4, of which 3 were waited for; matrix products, arithmetic and copies ran while one was open for 0% of the time, Pallas kernels for 2%

profile of v3, /device:TPU:2, one launch (start us, length us, event | category | flops | bytes accessed | tf_op | source)
XLA Modules:
  0.0 110.3 jit_solution(17001982442795546094)
XLA Ops:
  0.6 1.7 %shard_map.131 = f32[4,48,128]{2,1,0:T(8,128)} custom-call(f32[24,4,64]{2,1,0:T(4,128)} %align_hbm.1, f32[1,64]{1,0:T(1,128)} %bitcast.16), custom_call_target="tpu_custom_call" | custom-call | tf_op jit(solution)/shard_map/pallas_call | solution.py:288
  2.3 15.1 %all-to-all-start = ((f32[4,48,128]{2,1,0:T(8,128)}), f32[4,48,128]{2,1,0:T(8,128)S(1)}, u32[]{:S(2)}, u32[]{:S(2)}) async-start(f32[4,48,128]{2,1,0:T(8,128)} %shard_map.131), calls=%async_computation | async-start | bytes 196608 | tf_op jit(solution)/shard_map/all_to_all | solution.py:294
  17.4 1.9 %shard_map.132 = f32[16,72,128]{2,1,0:T(8,128)} custom-call(f32[8,24,48]{2,1,0:T(8,128)} %pair_w_ref.1), custom_call_target="tpu_custom_call" | custom-call | tf_op jit(solution)/shard_map/pallas_call | solution.py:291
  19.3 12.5 %all-to-all-done = f32[4,48,128]{2,1,0:T(8,128)S(1)} async-done(((f32[4,48,128]{2,1,0:T(8,128)}), f32[4,48,128]{2,1,0:T(8,128)S(1)}, u32[]{:S(2)}, u32[]{:S(2)}) %all-to-all-start) | async-done | bytes 98336 | tf_op jit(solution)/shard_map/all_to_all | solution.py:294
  31.8 6.2 %all-to-all-start.1 = ((f32[16,72,128]{2,1,0:T(8,128)}), f32[16,72,128]{2,1,0:T(8,128)S(1)}, u32[]{:S(2)}, u32[]{:S(2)}) async-start(f32[16,72,128]{2,1,0:T(8,128)} %shard_map.132), calls=%async_computation.1 | async-start | bytes 1179648 | tf_op jit(solution)/shard_map/all_to_all | solution.py:296
  38.0 0.0 copy-start.2
  38.0 0.0 copy-start.3
  38.0 0.0 copy-start.4
  38.1 0.0 copy-start.5
  38.1 0.0 copy-start.6
  38.1 0.0 copy-start.7
  38.1 14.1 %all_gather.6 = f32[1536,128]{1,0:T(8,128)S(1)} all-gather(f32[192,128]{1,0:T(8,128)S(1)} %bitcast.22), channel_id=1, replica_groups=mesh['y'=4,'zh'=4,'core'=2,'zl'=4,'x'=4] {'y','core'}, dimensions={0}, use_global_device_ids=true | all-gather | bytes 884736 | tf_op jit(solution)/shard_map/all_gather | solution.py:297
  52.2 0.0 all-to-all-done.1.weights_ref
  52.2 0.0 copy-start.8
  52.2 0.0 copy-start.9
  52.2 0.0 copy-done.2
  52.2 0.0 copy-done.3
  52.2 0.0 copy-done.4
  52.2 0.0 copy-done.5
  52.3 0.0 copy-done.6
  52.3 0.0 copy-done.7
  52.3 0.6 copy-done.8
  52.9 0.0 copy-done.9
  52.9 3.2 %shard_map.133 = (f32[24,4,64]{2,1,0:T(4,128)}, f32[16,24,128]{2,1,0:T(8,128)}, f32[8,24,128]{2,1,0:T(8,128)}) custom-call(f32[16,72,128]{2,1,0:T(8,128)S(1)} %all-to-all-done.1.weights_ref, f32[32,48,128]{2,1,0:T(8,128)S(1)} %bitcast.11, f32[24,4,64]{2,1,0:T(4,128)S(1)} %copy-done.2, f32[64,256]{1,0:T(8,128)S(1)} %copy-done.3, f32[64,256]{1,0:T(8,128)S(1)} %copy-done.4, ...), custom_call_target="tpu_custom_call" | custom-call | tf_op jit(solution)/shard_map/pallas_call | solution.py:327
  56.1 3.7 %all-to-all-start.2 = ((f32[8,24,128]{2,1,0:T(8,128)}), f32[8,24,128]{2,1,0:T(8,128)S(1)}, u32[]{:S(2)}, u32[]{:S(2)}) async-start(f32[8,24,128]{2,1,0:T(8,128)} %get-tuple-element.12), calls=%async_computation.2 | async-start | bytes 196608 | tf_op jit(solution)/shard_map/all_to_all | solution.py:340
  59.8 13.8 %all-to-all-done.2 = f32[8,24,128]{2,1,0:T(8,128)S(1)} async-done(((f32[8,24,128]{2,1,0:T(8,128)}), f32[8,24,128]{2,1,0:T(8,128)S(1)}, u32[]{:S(2)}, u32[]{:S(2)}) %all-to-all-start.2) | async-done | bytes 98336 | tf_op jit(solution)/shard_map/all_to_all | solution.py:340
  73.6 0.0 copy-start.1
  73.7 15.8 %all_to_all.25 = f32[16,24,128]{2,1,0:T(8,128)S(1)} all-to-all(f32[16,24,128]{2,1,0:T(8,128)S(1)} %bitcast.21), channel_id=1, replica_groups=mesh['y'=4,'zh'=4,'core'=2,'zl'=4,'x'=4] {'y','x'}, dimensions={0} | all-to-all | bytes 393216 | tf_op jit(solution)/shard_map/all_to_all | solution.py:345
  89.4 0.0 copy-start
  89.4 6.5 %all-to-all-start.4 = ((f32[16,24,128]{2,1,0:T(8,128)}), f32[16,24,128]{2,1,0:T(8,128)S(1)}, u32[]{:S(2)}, u32[]{:S(2)}) async-start(f32[16,24,128]{2,1,0:T(8,128)} %get-tuple-element.14), calls=%async_computation.4 | async-start | bytes 393216 | tf_op jit(solution)/shard_map/all_to_all | solution.py:347
  95.9 2.1 %all_gather.7.right_ref = f32[768,128]{1,0:T(8,128)S(1)} all-gather(f32[384,128]{1,0:T(8,128)S(1)} %bitcast.20), channel_id=1, replica_groups=mesh['y'=4,'zh'=4,'core'=2,'zl'=4,'x'=4] {'core'}, dimensions={0}, use_global_device_ids=true | all-gather | bytes 589824 | tf_op jit(solution)/shard_map/all_gather | solution.py:348
  98.0 6.0 %all-to-all-done.4 = f32[16,24,128]{2,1,0:T(8,128)S(1)} async-done(((f32[16,24,128]{2,1,0:T(8,128)}), f32[16,24,128]{2,1,0:T(8,128)S(1)}, u32[]{:S(2)}, u32[]{:S(2)}) %all-to-all-start.4) | async-done | bytes 196640 | tf_op jit(solution)/shard_map/all_to_all | solution.py:347
  104.0 0.0 copy-start.10
  104.0 0.0 copy-done.1
  104.0 0.0 copy-done
  104.0 0.6 copy-done.10
  104.6 5.6 %shard_map.134 = f32[24,48,128]{2,1,0:T(8,128)} custom-call(f32[384,128]{1,0:T(8,128)S(1)} %bitcast.12, f32[768,128]{1,0:T(8,128)S(1)} %all_gather.7.right_ref, f32[24,48,128]{2,1,0:T(8,128)S(1)} %copy-done, f32[1024,128]{1,0:T(8,128)S(1)} %copy-done.1, f32[1,128]{1,0:T(1,128)S(1)} %bitcast.19), custom_call_target="tpu_custom_call" | custom-call | tf_op jit(solution)/shard_map/pallas_call | solution.py:349
  (2 shorter events, 0.0 us)
Async XLA Ops:
  2.3 29.5 %all-to-all-start = ((f32[4,48,128]{2,1,0:T(8,128)}), f32[4,48,128]{2,1,0:T(8,128)S(1)}, u32[]{:S(2)}, u32[]{:S(2)}) async-start(f32[4,48,128]{2,1,0:T(8,128)} %shard_map.131), calls=%async_computation | async-start | bytes 196608 | tf_op jit(solution)/shard_map/all_to_all | solution.py:294
  31.8 20.4 %all-to-all-start.1 = ((f32[16,72,128]{2,1,0:T(8,128)}), f32[16,72,128]{2,1,0:T(8,128)S(1)}, u32[]{:S(2)}, u32[]{:S(2)}) async-start(f32[16,72,128]{2,1,0:T(8,128)} %shard_map.132), calls=%async_computation.1 | async-start | bytes 1179648 | tf_op jit(solution)/shard_map/all_to_all | solution.py:296
  38.0 14.2 %copy-start.2 = (f32[24,4,64]{2,1,0:T(4,128)S(1)}, f32[24,4,64]{2,1,0:T(4,128)}, u32[]{:S(2)}) copy-start(f32[24,4,64]{2,1,0:T(4,128)} %align_hbm.1) | copy-start | bytes 73732
  38.0 14.2 %copy-start.3 = (f32[64,256]{1,0:T(8,128)S(1)}, f32[64,256]{1,0:T(8,128)}, u32[]{:S(2)}) copy-start(f32[64,256]{1,0:T(8,128)} %value_hbm.1) | copy-start | bytes 196612
  38.0 14.2 %copy-start.4 = (f32[64,256]{1,0:T(8,128)S(1)}, f32[64,256]{1,0:T(8,128)}, u32[]{:S(2)}) copy-start(f32[64,256]{1,0:T(8,128)} %gate_hbm.1) | copy-start | bytes 196612
  38.1 14.2 %copy-start.5 = (f32[256,64]{0,1:T(8,128)S(1)}, f32[256,64]{0,1:T(8,128)}, u32[]{:S(2)}) copy-start(f32[256,64]{0,1:T(8,128)} %param.18) | copy-start | bytes 196612
  38.1 14.2 %copy-start.6 = (f32[64,32]{0,1:T(8,128)S(1)}, f32[64,32]{0,1:T(8,128)}, u32[]{:S(2)}) copy-start(f32[64,32]{0,1:T(8,128)} %param.20) | copy-start | bytes 24580
  38.1 14.2 %copy-start.7 = (f32[64,32]{0,1:T(8,128)S(1)}, f32[64,32]{0,1:T(8,128)}, u32[]{:S(2)}) copy-start(f32[64,32]{0,1:T(8,128)} %param.21) | copy-start | bytes 24580
  52.2 0.7 copy-start.8
  52.2 0.7 copy-start.9
  56.1 17.5 %all-to-all-start.2 = ((f32[8,24,128]{2,1,0:T(8,128)}), f32[8,24,128]{2,1,0:T(8,128)S(1)}, u32[]{:S(2)}, u32[]{:S(2)}) async-start(f32[8,24,128]{2,1,0:T(8,128)} %get-tuple-element.12), calls=%async_computation.2 | async-start | bytes 196608 | tf_op jit(solution)/shard_map/all_to_all | solution.py:340
  73.6 30.3 %copy-start.1 = (f32[1024,128]{1,0:T(8,128)S(1)}, f32[1024,128]{1,0:T(8,128)}, u32[]{:S(2)}) copy-start(f32[1024,128]{1,0:T(8,128)} %outer_ref.1) | copy-start | bytes 1572868
  89.4 14.6 %copy-start = (f32[24,48,128]{2,1,0:T(8,128)S(1)}, f32[24,48,128]{2,1,0:T(8,128)}, u32[]{:S(2)}) copy-start(f32[24,48,128]{2,1,0:T(8,128)} %state_ref.1) | copy-start | bytes 1769476
  89.4 14.5 %all-to-all-start.4 = ((f32[16,24,128]{2,1,0:T(8,128)}), f32[16,24,128]{2,1,0:T(8,128)S(1)}, u32[]{:S(2)}, u32[]{:S(2)}) async-start(f32[16,24,128]{2,1,0:T(8,128)} %get-tuple-element.14), calls=%async_computation.4 | async-start | bytes 393216 | tf_op jit(solution)/shard_map/all_to_all | solution.py:347
  104.0 0.7 copy-start.10

commit v4 on v3

--- a/solution.py
+++ b/solution.py
@@ -62,13 +62,16 @@
     fill(normed_ref, features)
 
 
-def weights_kernel(pair_w_ref, weights_ref):
+def weights_kernel(pair_w_ref, align_gain_ref, outer_gain_ref, bias_ref, weights_ref, small_ref):
     heads, rows, columns = pair_w_ref.shape
     turned = pair_w_ref[...].reshape(heads * rows, columns).T
     half = columns // 2
     tail = turned[:, LANES:]
     tail = jnp.concatenate([tail[:half], tail[half:]], axis=1)
     fill(weights_ref, jnp.concatenate([turned[:, :LANES], tail], axis=0))
+    small_ref[0:1, 0:64] = align_gain_ref[...]
+    small_ref[1:2, 0:64] = outer_gain_ref[...]
+    small_ref[2:3, :] = bias_ref[...]
 
 
 def dot3_turned(a, b):
@@ -89,14 +92,13 @@
 def average_kernel(
     weights_ref,
     gathered_ref,
+    small_ref,
     align_hbm,
     value_hbm,
     gate_hbm,
     output_hbm,
     left_hbm,
     right_hbm,
-    align_gain_hbm,
-    outer_gain_hbm,
     out_ref,
     left_ref,
     right_ref,
@@ -106,8 +108,6 @@
     output_ref,
     left_w_ref,
     right_w_ref,
-    align_gain_ref,
-    outer_gain_ref,
     left_tmp,
     right_tmp,
     arrived,
@@ -118,12 +118,10 @@
             [
                 (value_hbm, value_ref),
                 (align_hbm, align_ref),
-                (align_gain_hbm, align_gain_ref),
                 (gate_hbm, gate_ref),
                 (output_hbm, output_ref),
                 (left_hbm, left_w_ref),
                 (right_hbm, right_w_ref),
-                (outer_gain_hbm, outer_gain_ref),
             ]
         )
     ]
@@ -150,7 +148,7 @@
     lane_head = lax.rem(lax.div(lane, 32), heads)
     vh, vl = split(twice(value_ref[...]))
     gate2 = twice(gate_ref[...])
-    own = [normalize(align_ref[:, s, :], align_gain_ref[...]) for s in range(4)]
+    own = [normalize(align_ref[:, s, :], small_ref[0:1, 0:64]) for s in range(4)]
     gated = []
     for p in range(2):
         mh, ml = split(mixed[p])
@@ -165,7 +163,7 @@
     aligned = jnp.concatenate([align_ref[:, s, :] for s in range(4)], axis=0) + update
     for s in range(4):
         out_ref[:, s, :] = aligned[s * rows : (s + 1) * rows]
-    normed = normalize(aligned, outer_gain_ref[...])
+    normed = normalize(aligned, small_ref[1:2, 0:64])
     left_tmp[:, 0:32] = dot3_turned(normed, left_w_ref[...])
     right_tmp[:, 0:32] = dot3_turned(normed, right_w_ref[...])
     left = jnp.concatenate(
@@ -186,23 +184,25 @@
     right_ref,
     state_ref,
     outer_ref,
-    bias_hbm,
+    small_ref,
     out_ref,
     turned,
     spread_h,
     spread_l,
     total,
-    bias_ref,
-    arrived,
 ):
-    fetch = pltpu.make_async_copy(bias_hbm, bias_ref, arrived)
-    fetch.start()
     lefts = [left_ref[pl.ds(g, 64, stride=6), :] * (1.0 / 64.0) for g in range(6)]
     lh, ll = split(jnp.concatenate(lefts, axis=1))
     left4 = jnp.concatenate([lh, lh, ll, ll], axis=0)
     for core in range(2):
         for g in range(6):
-            block = right_ref[pl.ds(core * 384 + g, 64, stride=6), :]
+            block = jnp.concatenate(
+                [
+                    right_ref[pl.ds((y * 2 + core) * 96 + g, 16, stride=6), :]
+                    for y in range(4)
+                ],
+                axis=0,
+            )
             high = block.astype(BF16).astype(F32)
             stacked = jnp.concatenate([high, block - high], axis=0)
             turned[(core * 6 + g) * LANES : (core * 6 + g + 1) * LANES, :] = stacked.T
@@ -240,14 +240,13 @@
             total[...] = step
         else:
             total[...] += step
-    fetch.wait()
     for g in range(6):
         for k in range(4):
             start = (g * 2 + k // 2) * 48
             out_ref[g * 4 + k] = (
                 state_ref[g * 4 + k]
                 + total[start : start + 48, (k % 2) * LANES : (k % 2 + 1) * LANES]
-                + bias_ref[...]
+                + small_ref[2:3, :]
             )
 
 
@@ -284,18 +283,18 @@
     return jax.ShapeDtypeStruct(dims, F32)
 
 
-def first_exchange(alignment, pair_weights, align_gain):
+def first_exchange(alignment, pair_weights, align_gain, outer_gain, outer_bias):
     normed = pl.pallas_call(
         features_kernel, out_shape=shape(4, 48, 128), compiler_params=PREPARE
     )(alignment, align_gain)
-    packed = pl.pallas_call(
-        weights_kernel, out_shape=shape(16, 72, 128), compiler_params=PREPARE
-    )(pair_weights)
+    packed, small = pl.pallas_call(
+        weights_kernel, out_shape=(shape(16, 72, 128), shape(8, 128)), compiler_params=PARAMS
+    )(pair_weights, align_gain, outer_gain, outer_bias)
     near = lax.all_to_all(normed, "zh", 0, 0, tiled=True).reshape(192, 128)
     near, packed = lax.optimization_barrier((near, packed))
     weights = lax.all_to_all(packed, COL, 0, 0, tiled=True)
     gathered = lax.all_gather(near, ("y", "core"), axis=0, tiled=True).reshape(32, 48, 128)
-    return gathered, weights
+    return gathered, weights, small
 
 
 def on_device(
@@ -313,7 +312,9 @@
     outer_bias,
 ):
     align_gain, outer_gain = align_gain[None], outer_gain[None]
-    gathered, weights = first_exchange(alignment, pair_weights, align_gain)
+    gathered, weights, small = first_exchange(
+        alignment, pair_weights, align_gain, outer_gain, outer_bias[None]
+    )
     params = (
         alignment,
         value_weight,
@@ -321,14 +322,12 @@
         output_weight.T,
         left_weight.T,
         right_weight.T,
-        align_gain,
-        outer_gain,
     )
     alignment_out, left, right = pl.pallas_call(
         average_kernel,
-        in_specs=[VMEM, VMEM] + [HBM] * len(params),
+        in_specs=[VMEM] * 3 + [HBM] * len(params),
         out_specs=[VMEM] * 3,
-        out_shape=(shape(24, 4, 64), shape(16, 24, 128), shape(8, 24, 128)),
+        out_shape=(shape(24, 4, 64), shape(24, 128), shape(8, 24, 128)),
         scratch_shapes=[pltpu.VMEM(p.shape, F32) for p in params]
         + [
             pltpu.VMEM((96, 128), F32),
@@ -336,31 +335,28 @@
             pltpu.SemaphoreType.DMA((len(params),)),
         ],
         compiler_params=PARAMS,
-    )(weights, gathered, *params)
+    )(weights, gathered, small, *params)
     right = lax.all_to_all(right, ALL, 0, 0, axis_index_groups=mirrored(), tiled=True)
+    left = lax.all_gather(left, "x", axis=0, tiled=True)
+    right, left = lax.optimization_barrier((right, left))
     y, zl = lax.axis_index("y"), lax.axis_index("zl")
     side = jnp.where(y == zl, y % 2, jnp.where(y < zl, 1, 0))
     right = lax.dynamic_slice_in_dim(right, side * 4, 4, axis=0)
-    right = jnp.broadcast_to(right[None], (4, *right.shape)).reshape(16, 24, 128)
-    right = lax.all_to_all(right, ("y", "x"), 0, 0, tiled=True).reshape(384, 128)
-    right, left = lax.optimization_barrier((right, left))
-    left_all = lax.all_to_all(left, COL, 0, 0, tiled=True).reshape(384, 128)
-    right_all = lax.all_gather(right, "core", axis=0, tiled=True)
+    right = jnp.broadcast_to(right[None], (8, *right.shape)).reshape(32, 24, 128)
+    right_all = lax.all_to_all(right, ("y", "core", "x"), 0, 0, tiled=True)
+    right_all = right_all.reshape(768, 128)
+    left_all = lax.all_gather(left, "zl", axis=0, tiled=True)
     pair_out = pl.pallas_call(
         outer_kernel,
-        in_specs=[VMEM] * 4 + [HBM],
-        out_specs=VMEM,
         out_shape=shape(24, 48, 128),
         scratch_shapes=[
             pltpu.VMEM((1536, 128), F32),
             pltpu.VMEM((CHUNK * 64, 256), BF16),
             pltpu.VMEM((CHUNK * 64, 256), BF16),
             pltpu.VMEM((576, 256), F32),
-            pltpu.VMEM((1, 128), F32),
-            pltpu.SemaphoreType.DMA(()),
         ],
         compiler_params=PARAMS,
-    )(left_all, right_all, pair_state, outer_weight, outer_bias[None])
+    )(left_all, right_all, pair_state, outer_weight, small)
     return alignment_out, pair_out
 
 

time: 111 us -> 103 us (0.928)
  waiting for transfers between devices: 32.3 us -> 14.3 us
  blocking collectives: 32 us -> 39.7 us
  starting transfers between devices: 31.5 us -> 34.6 us
    all_gather x1 -> x2, blocking collectives: 2.07 us -> 25.6 us  [the longest x1 13.7 us: on_device(): left_all = lax.all_gather(left, 'zl', axis=0, tiled=True)]
    all_to_all x1 -> x0, blocking collectives: 15.8 us -> none  [on_device(): lax.all_to_all(right, ('y', 'x'), 0, 0, tiled=True).reshape(384, 128)]
    all_to_all x1, waiting for transfers between devices: 13.8 us -> 1.62 us  [on_device(): lax.all_to_all(right, ALL, 0, 0, axis_index_groups=mirrored(), tiled=True)]
    all_to_all x1, waiting for transfers between devices: 6.02 us -> 0.01 us  [on_device(): right_all = lax.all_to_all(right, ('y', 'core', 'x'), 0, 0, tiled=True)]
    all_to_all x1, starting transfers between devices: 6.46 us -> 9.43 us  [on_device(): right_all = lax.all_to_all(right, ('y', 'core', 'x'), 0, 0, tiled=True)]
  transfers between devices with their start and end apart: 4 -> 4, of which waited for: 3 -> 2; matrix products, arithmetic and copies ran while one was open for 0% -> 0% of each run, Pallas kernels for 2% -> 1%
where the time goes in v4:
time: 103 us; the launch traced here: 102 us
  blocking collectives  39.7 us (39%)
  starting transfers between devices  34.6 us (34%)
  waiting for transfers between devices  14.3 us (14%)
  Pallas kernels  11.5 us (11%)
  local copies, waits for them, and re-layouts  1.5 us (1%)
    all_to_all x1, starting transfers between devices, first_exchange(): near = lax.all_to_all(normed, 'zh', 0, 0, tiled=True).reshape(192, 128)  15.2 us
    all_gather x1, blocking collectives, first_exchange(): lax.all_gather(near, ('y', 'core'), axis=0, tiled=True).reshape(32, 48, 128)  14.1 us
    all_gather x1, blocking collectives, on_device(): left_all = lax.all_gather(left, 'zl', axis=0, tiled=True)  13.7 us
    all_to_all x1, waiting for transfers between devices, first_exchange(): near = lax.all_to_all(normed, 'zh', 0, 0, tiled=True).reshape(192, 128)  12.7 us
    all_gather x1, blocking collectives, on_device(): left = lax.all_gather(left, 'x', axis=0, tiled=True)  11.9 us
    all_to_all x1, starting transfers between devices, on_device(): right_all = lax.all_to_all(right, ('y', 'core', 'x'), 0, 0, tiled=True)  9.43 us
    all_to_all x1, starting transfers between devices, first_exchange(): weights = lax.all_to_all(packed, COL, 0, 0, tiled=True)  6.21 us
    pallas_call x1, Pallas kernels, on_device(): pl.pallas_call(outer_kernel, out_shape=shape(24, 48, 128), scratch_shapes...  5.63 us
  transfers between devices with their start and end apart: 4, of which 2 were waited for; matrix products, arithmetic and copies ran while one was open for 0% of the time, Pallas kernels for 1%

profile of v4, /device:TPU:2, one launch (start us, length us, event | category | flops | bytes accessed | tf_op | source)
XLA Modules:
  0.0 102.4 jit_solution(10379310001517018306)
XLA Ops:
  0.6 1.7 %shard_map.131 = f32[4,48,128]{2,1,0:T(8,128)} custom-call(f32[24,4,64]{2,1,0:T(4,128)} %align_hbm.1, f32[1,64]{1,0:T(1,128)} %bitcast.15), custom_call_target="tpu_custom_call" | custom-call | tf_op jit(solution)/shard_map/pallas_call | solution.py:287
  2.3 0.0 copy-start.3
  2.3 15.2 %all-to-all-start = ((f32[4,48,128]{2,1,0:T(8,128)}), f32[4,48,128]{2,1,0:T(8,128)S(1)}, u32[]{:S(2)}, u32[]{:S(2)}) async-start(f32[4,48,128]{2,1,0:T(8,128)} %shard_map.131), calls=%async_computation | async-start | bytes 196608 | tf_op jit(solution)/shard_map/all_to_all | solution.py:293
  17.5 0.0 copy-start.9
  17.5 0.0 copy-start.10
  17.5 0.0 copy-start.11
  17.5 0.0 copy-done.3
  17.6 0.6 copy-done.9
  18.2 0.0 copy-done.10
  18.2 0.0 copy-done.11
  18.2 1.0 shard_map.132
  19.2 12.7 %all-to-all-done = f32[4,48,128]{2,1,0:T(8,128)S(1)} async-done(((f32[4,48,128]{2,1,0:T(8,128)}), f32[4,48,128]{2,1,0:T(8,128)S(1)}, u32[]{:S(2)}, u32[]{:S(2)}) %all-to-all-start) | async-done | bytes 98336 | tf_op jit(solution)/shard_map/all_to_all | solution.py:293
  32.0 6.2 %all-to-all-start.1 = ((f32[16,72,128]{2,1,0:T(8,128)}), f32[16,72,128]{2,1,0:T(8,128)S(1)}, u32[]{:S(2)}, u32[]{:S(2)}) async-start(f32[16,72,128]{2,1,0:T(8,128)} %get-tuple-element.12), calls=%async_computation.1 | async-start | bytes 1179648 | tf_op jit(solution)/shard_map/all_to_all | solution.py:295
  38.2 0.0 copy-start.2
  38.2 0.0 copy-start.4
  38.2 0.0 copy-start.5
  38.2 0.0 copy-start.6
  38.2 0.0 copy-start.7
  38.2 0.0 copy-start.8
  38.2 14.1 %all_gather.9 = f32[1536,128]{1,0:T(8,128)S(1)} all-gather(f32[192,128]{1,0:T(8,128)S(1)} %bitcast.19), channel_id=1, replica_groups=mesh['y'=4,'zh'=4,'core'=2,'zl'=4,'x'=4] {'y','core'}, dimensions={0}, use_global_device_ids=true | all-gather | bytes 884736 | tf_op jit(solution)/shard_map/all_gather | solution.py:296
  52.4 0.0 all-to-all-done.1.weights_ref
  52.4 0.0 copy-done.2
  52.4 0.0 copy-done.4
  52.4 0.0 copy-done.5
  52.4 0.0 copy-done.6
  52.4 0.0 copy-done.7
  52.4 0.0 copy-done.8
  52.4 3.2 %shard_map.133 = (f32[24,4,64]{2,1,0:T(4,128)}, f32[24,128]{1,0:T(8,128)S(1)}, f32[8,24,128]{2,1,0:T(8,128)}) custom-call(f32[16,72,128]{2,1,0:T(8,128)S(1)} %all-to-all-done.1.weights_ref, f32[32,48,128]{2,1,0:T(8,128)S(1)} %bitcast.10, f32[8,128]{1,0:T(8,128)S(1)} %get-tuple-element.14.small_ref, f32[24,4,64]{2,1,0:T(4,128)S(1)} %copy-done.2, ...), custom_call_target="tpu_custom_call" | custom-call | tf_op jit(solution)/shard_map/pallas_call | solution.py:326
  55.6 3.7 %all-to-all-start.2 = ((f32[8,24,128]{2,1,0:T(8,128)}), f32[8,24,128]{2,1,0:T(8,128)S(1)}, u32[]{:S(2)}, u32[]{:S(2)}) async-start(f32[8,24,128]{2,1,0:T(8,128)} %get-tuple-element.16), calls=%async_computation.2 | async-start | bytes 196608 | tf_op jit(solution)/shard_map/all_to_all | solution.py:339
  59.3 11.9 %all_gather.10 = f32[96,128]{1,0:T(8,128)S(1)} all-gather(f32[24,128]{1,0:T(8,128)S(1)} %get-tuple-element.17), channel_id=1, replica_groups=mesh['y'=4,'zh'=4,'core'=2,'zl'=4,'x'=4] {'x'}, dimensions={0}, use_global_device_ids=true | all-gather | bytes 61440 | tf_op jit(solution)/shard_map/all_gather | solution.py:340
  71.2 1.6 %all-to-all-done.2 = f32[8,24,128]{2,1,0:T(8,128)S(1)} async-done(((f32[8,24,128]{2,1,0:T(8,128)}), f32[8,24,128]{2,1,0:T(8,128)S(1)}, u32[]{:S(2)}, u32[]{:S(2)}) %all-to-all-start.2) | async-done | bytes 98336 | tf_op jit(solution)/shard_map/all_to_all | solution.py:339
  72.8 0.0 copy-start.1
  72.8 0.8 broadcast_in_dim.18
  73.6 0.0 copy-start
  73.6 9.4 %all-to-all-start.3 = ((f32[32,24,128]{2,1,0:T(8,128)}), f32[32,24,128]{2,1,0:T(8,128)S(1)}, u32[]{:S(2)}, u32[]{:S(2)}) async-start(f32[32,24,128]{2,1,0:T(8,128)} %bitcast.8), calls=%async_computation.3 | async-start | bytes 786432 | tf_op jit(solution)/shard_map/all_to_all | solution.py:346
  83.0 13.7 %all_gather.11.left_ref = f32[384,128]{1,0:T(8,128)S(1)} all-gather(f32[96,128]{1,0:T(8,128)S(1)} %all_gather.10), channel_id=1, replica_groups=mesh['y'=4,'zh'=4,'core'=2,'zl'=4,'x'=4] {'zl'}, dimensions={0}, use_global_device_ids=true | all-gather | bytes 245760 | tf_op jit(solution)/shard_map/all_gather | solution.py:348
  96.7 0.0 all-to-all-done.3
  96.7 0.0 copy-done.1
  96.7 0.0 copy-done
  96.7 5.6 %shard_map.134 = f32[24,48,128]{2,1,0:T(8,128)} custom-call(f32[384,128]{1,0:T(8,128)S(1)} %all_gather.11.left_ref, f32[768,128]{1,0:T(8,128)S(1)} %bitcast.11, f32[24,48,128]{2,1,0:T(8,128)S(1)} %copy-done, f32[1024,128]{1,0:T(8,128)S(1)} %copy-done.1, f32[8,128]{1,0:T(8,128)S(1)} %get-tuple-element.14.small_ref), custom_call_target="tpu_custom_call" | custom-call | tf_op jit(solution)/shard_map/pallas_call | solution.py:349
  (1 shorter events, 0.0 us)
Async XLA Ops:
  2.3 15.2 %copy-start.3 = (f32[8,24,48]{2,1,0:T(8,128)S(1)}, f32[8,24,48]{2,1,0:T(8,128)}, u32[]{:S(2)}) copy-start(f32[8,24,48]{2,1,0:T(8,128)} %pair_w_ref.1) | copy-start | bytes 110596
  2.3 29.6 %all-to-all-start = ((f32[4,48,128]{2,1,0:T(8,128)}), f32[4,48,128]{2,1,0:T(8,128)S(1)}, u32[]{:S(2)}, u32[]{:S(2)}) async-start(f32[4,48,128]{2,1,0:T(8,128)} %shard_map.131), calls=%async_computation | async-start | bytes 196608 | tf_op jit(solution)/shard_map/all_to_all | solution.py:293
  17.5 0.7 copy-start.9
  17.5 0.7 copy-start.10
  17.5 0.7 copy-start.11
  32.0 20.4 %all-to-all-start.1 = ((f32[16,72,128]{2,1,0:T(8,128)}), f32[16,72,128]{2,1,0:T(8,128)S(1)}, u32[]{:S(2)}, u32[]{:S(2)}) async-start(f32[16,72,128]{2,1,0:T(8,128)} %get-tuple-element.12), calls=%async_computation.1 | async-start | bytes 1179648 | tf_op jit(solution)/shard_map/all_to_all | solution.py:295
  38.2 14.2 %copy-start.2 = (f32[24,4,64]{2,1,0:T(4,128)S(1)}, f32[24,4,64]{2,1,0:T(4,128)}, u32[]{:S(2)}) copy-start(f32[24,4,64]{2,1,0:T(4,128)} %align_hbm.1) | copy-start | bytes 73732
  38.2 14.2 %copy-start.4 = (f32[64,256]{1,0:T(8,128)S(1)}, f32[64,256]{1,0:T(8,128)}, u32[]{:S(2)}) copy-start(f32[64,256]{1,0:T(8,128)} %value_hbm.1) | copy-start | bytes 196612
  38.2 14.2 %copy-start.5 = (f32[64,256]{1,0:T(8,128)S(1)}, f32[64,256]{1,0:T(8,128)}, u32[]{:S(2)}) copy-start(f32[64,256]{1,0:T(8,128)} %gate_hbm.1) | copy-start | bytes 196612
  38.2 14.2 %copy-start.6 = (f32[256,64]{0,1:T(8,128)S(1)}, f32[256,64]{0,1:T(8,128)}, u32[]{:S(2)}) copy-start(f32[256,64]{0,1:T(8,128)} %param.18) | copy-start | bytes 196612
  38.2 14.2 %copy-start.7 = (f32[64,32]{0,1:T(8,128)S(1)}, f32[64,32]{0,1:T(8,128)}, u32[]{:S(2)}) copy-start(f32[64,32]{0,1:T(8,128)} %param.20) | copy-start | bytes 24580
  38.2 14.2 %copy-start.8 = (f32[64,32]{0,1:T(8,128)S(1)}, f32[64,32]{0,1:T(8,128)}, u32[]{:S(2)}) copy-start(f32[64,32]{0,1:T(8,128)} %param.21) | copy-start | bytes 24580
  55.6 17.2 %all-to-all-start.2 = ((f32[8,24,128]{2,1,0:T(8,128)}), f32[8,24,128]{2,1,0:T(8,128)S(1)}, u32[]{:S(2)}, u32[]{:S(2)}) async-start(f32[8,24,128]{2,1,0:T(8,128)} %get-tuple-element.16), calls=%async_computation.2 | async-start | bytes 196608 | tf_op jit(solution)/shard_map/all_to_all | solution.py:339
  72.8 23.9 %copy-start.1 = (f32[1024,128]{1,0:T(8,128)S(1)}, f32[1024,128]{1,0:T(8,128)}, u32[]{:S(2)}) copy-start(f32[1024,128]{1,0:T(8,128)} %outer_ref.1) | copy-start | bytes 1572868
  73.6 23.1 %copy-start = (f32[24,48,128]{2,1,0:T(8,128)S(1)}, f32[24,48,128]{2,1,0:T(8,128)}, u32[]{:S(2)}) copy-start(f32[24,48,128]{2,1,0:T(8,128)} %state_ref.1) | copy-start | bytes 1769476
  73.6 23.1 %all-to-all-start.3 = ((f32[32,24,128]{2,1,0:T(8,128)}), f32[32,24,128]{2,1,0:T(8,128)S(1)}, u32[]{:S(2)}, u32[]{:S(2)}) async-start(f32[32,24,128]{2,1,0:T(8,128)} %bitcast.8), calls=%async_computation.3 | async-start | bytes 786432 | tf_op jit(solution)/shard_map/all_to_all | solution.py:346

commit v5 on v4

v5 whole, which is shorter than its diff:
```python
import functools

import jax
import jax.numpy as jnp
from jax import lax
from jax.experimental import pallas as pl
from jax.experimental.pallas import tpu as pltpu
from jax.sharding import Mesh, PartitionSpec as P

F32 = jnp.float32
BF16 = jnp.bfloat16
ROW = ("y", "zh", "core")
COL = ("zl", "x")
ALL = ROW + COL
LANES = 128
HALVES = (slice(0, 64), slice(64, 128))


def split(value):
    high = value.astype(BF16)
    low = (value - high.astype(F32)).astype(BF16)
    return high, low


def dot(a, b):
    return jnp.dot(a, b, preferred_element_type=F32)


def dot3(a, b):
    ah, al = split(a)
    bh, bl = split(b)
    return dot(ah, bh) + (dot(ah, bl) + dot(al, bh))


def normalize(features, gain):
    mean = jnp.mean(features, axis=-1, keepdims=True)
    centered = features - mean
    spread = jnp.mean(centered * centered, axis=-1, keepdims=True)
    return centered * lax.rsqrt(spread + 1e-05) * gain


def twice(weight):
    zeros = jnp.zeros_like(weight)
    return jnp.concatenate(
        [jnp.concatenate([weight, zeros], 1), jnp.concatenate([zeros, weight], 1)], 0
    )


def fill(ref, value):
    if len(ref.shape) == 2:
        ref[...] = value
    else:
        for k in range(ref.shape[0]):
            ref[k] = value


def features_kernel(align_ref, gain_ref, normed_ref):
    parts = [normalize(align_ref[:, s, :], gain_ref[...]) for s in range(4)]
    features = jnp.concatenate(
        [jnp.concatenate(parts[0:2], axis=1), jnp.concatenate(parts[2:4], axis=1)], axis=0
    )
    fill(normed_ref, features)


def early_kernel(
    pair_w_ref,
    align_ref,
    gate_w_ref,
    outer_ref,
    align_gain_ref,
    outer_gain_ref,
    bias_ref,
    weights_ref,
    gate_ref,
    spread_ref,
    small_ref,
):
    heads, rows, columns = pair_w_ref.shape
    turned = pair_w_ref[...].reshape(heads * rows, columns).T
    half = columns // 2
    tail = turned[:, LANES:]
    tail = jnp.concatenate([tail[:half], tail[half:]], axis=1)
    fill(weights_ref, jnp.concatenate([turned[:, :LANES], tail], axis=0))
    small_ref[0:1, 0:64] = outer_gain_ref[...]
    small_ref[1:2, :] = bias_ref[...]
    own = [normalize(align_ref[:, s, :], align_gain_ref[...]) for s in range(4)]
    logits = dot3(jnp.concatenate(own, axis=0), gate_w_ref[...])
    for s in range(4):
        gate_ref[:, s * 256 : (s + 1) * 256] = jax.nn.sigmoid(logits[s * rows : (s + 1) * rows])
    for d in range(32):
        wh, wl = split(outer_ref[pl.ds(d, 32, stride=32), :])
        both = jnp.concatenate([wh, wl], axis=1)
        spread_ref[pl.ds(d * 32, 32), :] = both
        spread_ref[pl.ds(1024 + d * 32, 32), :] = both


def copies_kernel(blocks_ref, out_ref):
    block = blocks_ref[0:4] + blocks_ref[4:8]
    for k in range(8):
        out_ref[4 * k : 4 * k + 4] = block


def dot3_turned(a, b):
    ah, al = split(a)
    bh, bl = split(b)

    def one(x, y):
        return lax.dot_general(x, y, (((1,), (1,)), ((), ())), preferred_element_type=F32)

    return one(ah, bh) + (one(ah, bl) + one(al, bh))


def landed(row):
    y, zh, core = row // 8, row // 2 % 4, row % 2
    return (y * 2 + core) * 4 + zh


def average_kernel(
    weights_ref,
    gathered_ref,
    gate_ref,
    small_ref,
    align_ref,
    value_ref,
    output_ref,
    left_w_ref,
    right_w_ref,
    out_ref,
    left_ref,
    right_ref,
    left_tmp,
    right_tmp,
):
    rows = align_ref.shape[0]
    columns = 2 * rows
    heads = 8
    first = weights_ref[:, 0:columns, :].reshape(-1, LANES)
    tails = [weights_ref[k, columns:, :] for k in range(16)]
    second = jnp.concatenate([t[:, half] for t in tails for half in HALVES], axis=0)
    weights = jnp.concatenate([first.T, second.T], axis=0)
    wh, wl = split(weights)
    mixed = []
    for p in range(2):
        blocks = [
            gathered_ref[landed(r), p * rows : (p + 1) * rows, :] for r in range(32)
        ]
        fh, fl = split(jnp.concatenate(blocks, axis=0))
        mixed.append(dot(wh, fh) + (dot(wh, fl) + dot(wl, fh)))
    lane = lax.broadcasted_iota(jnp.int32, (rows, 512), 1)
    lane_head = lax.rem(lax.div(lane, 32), heads)
    vh, vl = split(twice(value_ref[...]))
    gated = []
    for p in range(2):
        mh, ml = split(mixed[p])
        by_head = dot(mh, vh) + (dot(mh, vl) + dot(ml, vh))
        averaged = jnp.zeros((rows, 512), F32)
        for h in range(heads):
            averaged += jnp.where(lane_head == h, by_head[h * rows : (h + 1) * rows], 0.0)
        product = gate_ref[:, p * 512 : (p + 1) * 512] * averaged
        gated += [product[:, :256], product[:, 256:]]
    update = dot3_turned(jnp.concatenate(gated, axis=0), output_ref[...])
    aligned = jnp.concatenate([align_ref[:, s, :] for s in range(4)], axis=0) + update
    for s in range(4):
        out_ref[:, s, :] = aligned[s * rows : (s + 1) * rows]
    normed = normalize(aligned, small_ref[0:1, 0:64])
    left_tmp[:, 0:32] = dot3_turned(normed, left_w_ref[...])
    right_tmp[:, 0:32] = dot3_turned(normed, right_w_ref[...])
    left = jnp.concatenate(
        [left_tmp[pl.ds(k, rows, stride=4), 0:32] for k in range(4)], axis=1
    )
    right = jnp.concatenate(
        [right_tmp[pl.ds(k, rows, stride=4), 0:32] for k in range(4)], axis=1
    )
    fill(left_ref, left)
    y, zl = lax.axis_index("y"), lax.axis_index("zl")
    side = jnp.where(y == zl, lax.rem(y, 2), jnp.where(y < zl, 1, 0))
    for k in range(8):
        right_ref[k] = jnp.where(side == k // 4, right, 0.0)


CHUNK = 8


def outer_kernel(
    left_ref, right_ref, state_ref, spread_ref, small_ref, out_ref, turned
):
    lefts = [left_ref[pl.ds(g, 64, stride=6), :] * (1.0 / 64.0) for g in range(6)]
    lh, ll = split(jnp.concatenate(lefts, axis=1))
    left4 = jnp.concatenate([lh, lh, ll, ll], axis=0)
    for core in range(2):
        for g in range(6):
            block = jnp.concatenate(
                [
                    right_ref[pl.ds((y * 2 + core) * 96 + g, 16, stride=6), :]
                    for y in range(4)
                ],
                axis=0,
            )
            high = block.astype(BF16).astype(F32)
            stacked = jnp.concatenate([high, block - high], axis=0)
            turned[(core * 6 + g) * LANES : (core * 6 + g + 1) * LANES, :] = stacked.T
    rights = []
    for d in range(32):
        right = turned[pl.ds(d, 48, stride=32), :].astype(BF16)
        rights.append(jnp.concatenate([right, right], axis=1))
    right4 = jnp.concatenate(rights, axis=0)
    lane = lax.broadcasted_iota(jnp.int32, (48, LANES), 1)
    low_half = lane < 64
    even = lax.rem(lax.div(lane, 32), 2) == 0

    def exchange(a, b, shift, keep):
        return (
            jnp.where(keep, a, pltpu.roll(b, shift, 1)),
            jnp.where(keep, pltpu.roll(a, LANES - shift, 1), b),
        )

    for pair in range(6 // 6):
        product = dot(right4, left4[:, pair * 6 * LANES : (pair + 1) * 6 * LANES])
        rows = []
        for g in range(6):
            lanes = slice(g * LANES, (g + 1) * LANES)
            pieces = [[], [], [], []]
            for t in range(0, 32, 4):
                p0, p1, p2, p3 = (
                    product[(t + e) * 48 : (t + e + 1) * 48, lanes] for e in range(4)
                )
                a0, a2 = exchange(p0, p2, 64, low_half)
                a1, a3 = exchange(p1, p3, 64, low_half)
                k0, k1 = exchange(a0, a1, 32, even)
                k2, k3 = exchange(a2, a3, 32, even)
                for k, piece in enumerate((k0, k1, k2, k3)):
                    pieces[k].append(piece)
            rows += [jnp.concatenate(piece, axis=1) for piece in pieces]
        ah, al = split(jnp.concatenate(rows, axis=0))
        update = dot(jnp.concatenate([ah, al], axis=1), spread_ref[...])
        for n in range(4 * 6):
            i = pair * 4 * 6 + n
            part = update[n * 48 : (n + 1) * 48]
            out_ref[i] = (
                state_ref[i] + (part[:, :LANES] + part[:, LANES:]) + small_ref[1:2, :]
            )


def mirrored():
    sides = [((a, b), (b, a)) for a in range(4) for b in range(a + 1, 4)]
    sides += [((a, a), (a + 1, a + 1)) for a in (0, 2)]

    def index(y, zh, core, zl, x):
        return (((y * 4 + zh) * 2 + core) * 4 + zl) * 4 + x

    return [
        [index(y, zh, core, zl, x) for y, zl in pair for zh in range(4)]
        for core in range(2)
        for x in range(4)
        for pair in sides
    ]


PREPARE = pltpu.CompilerParams(vmem_limit_bytes=62 * 1024 * 1024)
PARAMS = pltpu.CompilerParams(vmem_limit_bytes=48 * 1024 * 1024)


OUTER_SCRATCH = [pltpu.VMEM((1536, 128), F32)]


def shape(*dims):
    return jax.ShapeDtypeStruct(dims, F32)


def on_device(
    alignment,
    pair_state,
    pair_weights,
    align_gain,
    value_weight,
    gate_weight,
    output_weight,
    outer_gain,
    left_weight,
    right_weight,
    outer_weight,
    outer_bias,
):
    align_gain, outer_gain = align_gain[None], outer_gain[None]
    normed = pl.pallas_call(
        features_kernel, out_shape=shape(4, 48, 128), compiler_params=PREPARE
    )(alignment, align_gain)
    packed, gate, spread, small = pl.pallas_call(
        early_kernel,
        out_shape=(
            shape(16, 72, 128),
            shape(24, 1024),
            jax.ShapeDtypeStruct((2048, 256), BF16),
            shape(8, 128),
        ),
        compiler_params=PARAMS,
    )(
        pair_weights,
        alignment,
        gate_weight,
        outer_weight,
        align_gain,
        outer_gain,
        outer_bias[None],
    )
    near = lax.all_to_all(normed, "zh", 0, 0, tiled=True).reshape(192, 128)
    near, packed = lax.optimization_barrier((near, packed))
    weights = lax.all_to_all(packed, COL, 0, 0, tiled=True)
    gathered = lax.all_gather(near, ("y", "core"), axis=0, tiled=True).reshape(32, 48, 128)
    alignment_out, left, right = pl.pallas_call(
        average_kernel,
        out_shape=(shape(24, 4, 64), shape(24, 128), shape(8, 24, 128)),
        scratch_shapes=[pltpu.VMEM((96, 128), F32), pltpu.VMEM((96, 128), F32)],
        compiler_params=PARAMS,
    )(
        weights,
        gathered,
        gate,
        small,
        alignment,
        value_weight,
        output_weight.T,
        left_weight.T,
        right_weight.T,
    )
    right = lax.all_to_all(right, ALL, 0, 0, axis_index_groups=mirrored(), tiled=True)
    left = lax.all_gather(left, "x", axis=0, tiled=True)
    right, left = lax.optimization_barrier((right, left))
    right = pl.pallas_call(
        copies_kernel, out_shape=shape(32, 24, 128), compiler_params=PARAMS
    )(right)
    right_all = lax.all_to_all(right, ("y", "core", "x"), 0, 0, tiled=True)
    right_all = right_all.reshape(768, 128)
    left_all = lax.all_gather(left, "zl", axis=0, tiled=True)
    pair_out = pl.pallas_call(
        outer_kernel,
        out_shape=shape(24, 48, 128),
        scratch_shapes=OUTER_SCRATCH,
        compiler_params=PARAMS,
    )(left_all, right_all, pair_state, spread, small)
    return alignment_out, pair_out


def solution(mesh):
    torus = Mesh(mesh.devices.reshape(4, 4, 2, 4, 4), ALL)
    return jax.shard_map(
        on_device,
        mesh=torus,
        in_specs=(P(ROW, COL, None), P(ROW, COL, None), P(None, ROW, COL)) + (P(),) * 9,
        out_specs=(P(ROW, COL, None), P(ROW, COL, None)),
        check_vma=False,
    )
```

time: 103 us -> 101 us (0.981)
  waiting for transfers between devices: 14.3 us -> 13.2 us
    all_to_all x2, waiting for transfers between devices: 12.7 us -> 11.3 us  [the longest x1 11.3 us: on_device(): near = lax.all_to_all(normed, 'zh', 0, 0, tiled=True).reshape(192, 128)]
    pallas_call x3 -> x4, Pallas kernels: 5.89 us -> 6.29 us  [the longest x1 2.37 us: on_device(): pl.pallas_call(average_kernel, out_shape=(shape(24, 4, 64), shape(24, 128...]
where the time goes in v5:
time: 101 us
  blocking collectives  39.7 us (39%)
  starting transfers between devices  34.3 us (34%)
  waiting for transfers between devices  13.2 us (13%)
  Pallas kernels  11.2 us (11%)
  local copies, waits for them, and re-layouts  1.73 us (2%)
    all_to_all x1, starting transfers between devices, on_device(): near = lax.all_to_all(normed, 'zh', 0, 0, tiled=True).reshape(192, 128)  15.2 us
    all_gather x1, blocking collectives, on_device(): lax.all_gather(near, ('y', 'core'), axis=0, tiled=True).reshape(32, 48, 128)  14.1 us
    all_gather x1, blocking collectives, on_device(): left_all = lax.all_gather(left, 'zl', axis=0, tiled=True)  13.7 us
    all_gather x1, blocking collectives, on_device(): left = lax.all_gather(left, 'x', axis=0, tiled=True)  11.9 us
    all_to_all x1, waiting for transfers between devices, on_device(): near = lax.all_to_all(normed, 'zh', 0, 0, tiled=True).reshape(192, 128)  11.3 us
    all_to_all x1, starting transfers between devices, on_device(): right_all = lax.all_to_all(right, ('y', 'core', 'x'), 0, 0, tiled=True)  9.15 us
    all_to_all x1, starting transfers between devices, on_device(): weights = lax.all_to_all(packed, COL, 0, 0, tiled=True)  6.21 us
    pallas_call x1, Pallas kernels, on_device(): pl.pallas_call(outer_kernel, out_shape=shape(24, 48, 128), scratch_shapes...  4.95 us
  transfers between devices with their start and end apart: 4, of which 2 were waited for; matrix products, arithmetic and copies ran while one was open for 0% of the time, Pallas kernels for 1%

profile of v5, /device:TPU:2, one launch (start us, length us, event | category | flops | bytes accessed | tf_op | source)
XLA Modules:
  0.0 100.8 jit_solution(16572936501567204248)
XLA Ops:
  0.6 0.0 copy-start.4
  0.6 1.7 %shard_map.131 = f32[4,48,128]{2,1,0:T(8,128)} custom-call(f32[24,4,64]{2,1,0:T(4,128)} %align_ref.5, f32[1,64]{1,0:T(1,128)} %bitcast.14), custom_call_target="tpu_custom_call" | custom-call | tf_op jit(solution)/shard_map/pallas_call | solution.py:285
  2.4 0.0 copy-start.2
  2.4 0.0 copy-start.3
  2.4 15.2 %all-to-all-start = ((f32[4,48,128]{2,1,0:T(8,128)}), f32[4,48,128]{2,1,0:T(8,128)S(1)}, u32[]{:S(2)}, u32[]{:S(2)}) async-start(f32[4,48,128]{2,1,0:T(8,128)} %shard_map.131), calls=%async_computation | async-start | bytes 196608 | tf_op jit(solution)/shard_map/all_to_all | solution.py:306
  17.6 0.0 copy-start.9
  17.6 0.0 copy-start.10
  17.6 0.0 copy-start.11
  17.6 0.0 copy-done.4
  17.6 0.0 copy-done.2
  17.6 0.0 copy-done.3
  17.6 0.6 copy-done.9
  18.2 0.0 copy-done.10
  18.3 0.0 copy-done.11
  18.3 0.0 copy-start.1
  18.3 1.0 %copy-done.1 = f32[1024,128]{1,0:T(8,128)S(1)} copy-done((f32[1024,128]{1,0:T(8,128)S(1)}, f32[1024,128]{1,0:T(8,128)}, u32[]{:S(2)}) %copy-start.1) | copy-done | bytes 524312
  19.3 1.4 %shard_map.132 = (f32[16,72,128]{2,1,0:T(8,128)}, f32[24,1024]{1,0:T(8,128)S(1)}, bf16[2048,256]{1,0:T(8,128)(2,1)S(1)}, f32[8,128]{1,0:T(8,128)S(1)}) custom-call(f32[8,24,48]{2,1,0:T(8,128)S(1)} %copy-done.3, f32[24,4,64]{2,1,0:T(4,128)S(1)} %copy-done.2, f32[64,256]{1,0:T(8,128)S(1)} %copy-done.4, f32[1024,128]{1,0:T(8,128)S(1)} %copy-done.1, ...), custom_call_target="tpu_custom_call" | custom-call | tf_op jit(solution)/shard_map/pallas_call | solution.py:288
  20.7 11.3 %all-to-all-done = f32[4,48,128]{2,1,0:T(8,128)S(1)} async-done(((f32[4,48,128]{2,1,0:T(8,128)}), f32[4,48,128]{2,1,0:T(8,128)S(1)}, u32[]{:S(2)}, u32[]{:S(2)}) %all-to-all-start) | async-done | bytes 98336 | tf_op jit(solution)/shard_map/all_to_all | solution.py:306
  32.0 6.2 %all-to-all-start.1 = ((f32[16,72,128]{2,1,0:T(8,128)}), f32[16,72,128]{2,1,0:T(8,128)S(1)}, u32[]{:S(2)}, u32[]{:S(2)}) async-start(f32[16,72,128]{2,1,0:T(8,128)} %get-tuple-element.14), calls=%async_computation.1 | async-start | bytes 1179648 | tf_op jit(solution)/shard_map/all_to_all | solution.py:308
  38.2 0.0 copy-start.5
  38.2 0.0 copy-start.6
  38.2 0.0 copy-start.7
  38.2 0.0 copy-start.8
  38.2 14.1 %all_gather.9 = f32[1536,128]{1,0:T(8,128)S(1)} all-gather(f32[192,128]{1,0:T(8,128)S(1)} %bitcast.18), channel_id=1, replica_groups=mesh['y'=4,'zh'=4,'core'=2,'zl'=4,'x'=4] {'y','core'}, dimensions={0}, use_global_device_ids=true | all-gather | bytes 884736 | tf_op jit(solution)/shard_map/all_gather | solution.py:309
  52.4 0.0 all-to-all-done.1.weights_ref
  52.4 0.0 copy-done.5
  52.4 0.0 copy-done.6
  52.4 0.0 copy-done.7
  52.4 0.0 copy-done.8
  52.4 2.4 %shard_map.133 = (f32[24,4,64]{2,1,0:T(4,128)}, f32[24,128]{1,0:T(8,128)S(1)}, f32[8,24,128]{2,1,0:T(8,128)}) custom-call(f32[16,72,128]{2,1,0:T(8,128)S(1)} %all-to-all-done.1.weights_ref, f32[32,48,128]{2,1,0:T(8,128)S(1)} %bitcast.9, f32[24,1024]{1,0:T(8,128)S(1)} %get-tuple-element.16.gate_ref, f32[8,128]{1,0:T(8,128)S(1)} %get-tuple-element.17.small_ref, ...), custom_call_target="tpu_custom_call" | custom-call | tf_op jit(solution)/shard_map/pallas_call | solution.py:310
  54.8 3.7 %all-to-all-start.2 = ((f32[8,24,128]{2,1,0:T(8,128)}), f32[8,24,128]{2,1,0:T(8,128)S(1)}, u32[]{:S(2)}, u32[]{:S(2)}) async-start(f32[8,24,128]{2,1,0:T(8,128)} %get-tuple-element.19), calls=%async_computation.2 | async-start | bytes 196608 | tf_op jit(solution)/shard_map/all_to_all | solution.py:326
  58.5 11.9 %all_gather.10 = f32[96,128]{1,0:T(8,128)S(1)} all-gather(f32[24,128]{1,0:T(8,128)S(1)} %get-tuple-element.20), channel_id=1, replica_groups=mesh['y'=4,'zh'=4,'core'=2,'zl'=4,'x'=4] {'x'}, dimensions={0}, use_global_device_ids=true | all-gather | bytes 61440 | tf_op jit(solution)/shard_map/all_gather | solution.py:327
  70.4 1.9 %all-to-all-done.2.blocks_ref = f32[8,24,128]{2,1,0:T(8,128)S(1)} async-done(((f32[8,24,128]{2,1,0:T(8,128)}), f32[8,24,128]{2,1,0:T(8,128)S(1)}, u32[]{:S(2)}, u32[]{:S(2)}) %all-to-all-start.2) | async-done | bytes 98336 | tf_op jit(solution)/shard_map/all_to_all | solution.py:326
  72.3 0.8 shard_map.134
  73.0 0.0 copy-start
  73.0 9.1 %all-to-all-start.3 = ((f32[32,24,128]{2,1,0:T(8,128)}), f32[32,24,128]{2,1,0:T(8,128)S(1)}, u32[]{:S(2)}, u32[]{:S(2)}) async-start(f32[32,24,128]{2,1,0:T(8,128)} %shard_map.134), calls=%async_computation.3 | async-start | bytes 786432 | tf_op jit(solution)/shard_map/all_to_all | solution.py:332
  82.2 13.7 %all_gather.11.left_ref = f32[384,128]{1,0:T(8,128)S(1)} all-gather(f32[96,128]{1,0:T(8,128)S(1)} %all_gather.10), channel_id=1, replica_groups=mesh['y'=4,'zh'=4,'core'=2,'zl'=4,'x'=4] {'zl'}, dimensions={0}, use_global_device_ids=true | all-gather | bytes 245760 | tf_op jit(solution)/shard_map/all_gather | solution.py:334
  95.9 0.0 all-to-all-done.3
  95.9 0.0 copy-done
  95.9 5.0 %shard_map.135 = f32[24,48,128]{2,1,0:T(8,128)} custom-call(f32[384,128]{1,0:T(8,128)S(1)} %all_gather.11.left_ref, f32[768,128]{1,0:T(8,128)S(1)} %bitcast.10, f32[24,48,128]{2,1,0:T(8,128)S(1)} %copy-done, bf16[2048,256]{1,0:T(8,128)(2,1)S(1)} %get-tuple-element.23.spread_ref, f32[8,128]{1,0:T(8,128)S(1)} %get-tuple-element.17.small_ref), custom_call_target="tpu_custom_call" | custom-call | tf_op jit(solution)/shard_map/pallas_call | solution.py:335
Async XLA Ops:
  0.6 17.0 %copy-start.4 = (f32[64,256]{1,0:T(8,128)S(1)}, f32[64,256]{1,0:T(8,128)}, u32[]{:S(2)}) copy-start(f32[64,256]{1,0:T(8,128)} %gate_w_ref.1) | copy-start | bytes 196612
  2.4 15.2 %copy-start.2 = (f32[24,4,64]{2,1,0:T(4,128)S(1)}, f32[24,4,64]{2,1,0:T(4,128)}, u32[]{:S(2)}) copy-start(f32[24,4,64]{2,1,0:T(4,128)} %align_ref.5) | copy-start | bytes 73732
  2.4 15.2 %copy-start.3 = (f32[8,24,48]{2,1,0:T(8,128)S(1)}, f32[8,24,48]{2,1,0:T(8,128)}, u32[]{:S(2)}) copy-start(f32[8,24,48]{2,1,0:T(8,128)} %pair_w_ref.1) | copy-start | bytes 110596
  2.4 29.6 %all-to-all-start = ((f32[4,48,128]{2,1,0:T(8,128)}), f32[4,48,128]{2,1,0:T(8,128)S(1)}, u32[]{:S(2)}, u32[]{:S(2)}) async-start(f32[4,48,128]{2,1,0:T(8,128)} %shard_map.131), calls=%async_computation | async-start | bytes 196608 | tf_op jit(solution)/shard_map/all_to_all | solution.py:306
  17.6 0.7 copy-start.9
  17.6 0.7 copy-start.10
  17.6 0.7 copy-start.11
  18.3 1.0 %copy-start.1 = (f32[1024,128]{1,0:T(8,128)S(1)}, f32[1024,128]{1,0:T(8,128)}, u32[]{:S(2)}) copy-start(f32[1024,128]{1,0:T(8,128)} %outer_ref.1) | copy-start | bytes 1572868
  32.0 20.4 %all-to-all-start.1 = ((f32[16,72,128]{2,1,0:T(8,128)}), f32[16,72,128]{2,1,0:T(8,128)S(1)}, u32[]{:S(2)}, u32[]{:S(2)}) async-start(f32[16,72,128]{2,1,0:T(8,128)} %get-tuple-element.14), calls=%async_computation.1 | async-start | bytes 1179648 | tf_op jit(solution)/shard_map/all_to_all | solution.py:308
  38.2 14.2 %copy-start.5 = (f32[64,256]{1,0:T(8,128)S(1)}, f32[64,256]{1,0:T(8,128)}, u32[]{:S(2)}) copy-start(f32[64,256]{1,0:T(8,128)} %value_ref.1) | copy-start | bytes 196612
  38.2 14.2 %copy-start.6 = (f32[256,64]{0,1:T(8,128)S(1)}, f32[256,64]{0,1:T(8,128)}, u32[]{:S(2)}) copy-start(f32[256,64]{0,1:T(8,128)} %param.18) | copy-start | bytes 196612
  38.2 14.2 %copy-start.7 = (f32[64,32]{0,1:T(8,128)S(1)}, f32[64,32]{0,1:T(8,128)}, u32[]{:S(2)}) copy-start(f32[64,32]{0,1:T(8,128)} %param.20) | copy-start | bytes 24580
  38.2 14.2 %copy-start.8 = (f32[64,32]{0,1:T(8,128)S(1)}, f32[64,32]{0,1:T(8,128)}, u32[]{:S(2)}) copy-start(f32[64,32]{0,1:T(8,128)} %param.21) | copy-start | bytes 24580
  54.8 17.5 %all-to-all-start.2 = ((f32[8,24,128]{2,1,0:T(8,128)}), f32[8,24,128]{2,1,0:T(8,128)S(1)}, u32[]{:S(2)}, u32[]{:S(2)}) async-start(f32[8,24,128]{2,1,0:T(8,128)} %get-tuple-element.19), calls=%async_computation.2 | async-start | bytes 196608 | tf_op jit(solution)/shard_map/all_to_all | solution.py:326
  73.0 22.8 %copy-start = (f32[24,48,128]{2,1,0:T(8,128)S(1)}, f32[24,48,128]{2,1,0:T(8,128)}, u32[]{:S(2)}) copy-start(f32[24,48,128]{2,1,0:T(8,128)} %state_ref.1) | copy-start | bytes 1769476
  73.0 22.8 %all-to-all-start.3 = ((f32[32,24,128]{2,1,0:T(8,128)}), f32[32,24,128]{2,1,0:T(8,128)S(1)}, u32[]{:S(2)}, u32[]{:S(2)}) async-start(f32[32,24,128]{2,1,0:T(8,128)} %shard_map.134), calls=%async_computation.3 | async-start | bytes 786432 | tf_op jit(solution)/shard_map/all_to_all | solution.py:332

commit v6 on v5

--- a/solution.py
+++ b/solution.py
@@ -12,6 +12,9 @@
 ROW = ("y", "zh", "core")
 COL = ("zl", "x")
 ALL = ROW + COL
+FAR = (2, 3, 0, 1)
+RING = (0, 2, 3, 1)
+MIDDLE = (5, *range(5), *range(6, 16))
 LANES = 128
 HALVES = (slice(0, 64), slice(64, 128))
 
@@ -95,9 +98,11 @@
 
 
 def copies_kernel(blocks_ref, out_ref):
-    block = blocks_ref[0:4] + blocks_ref[4:8]
-    for k in range(8):
-        out_ref[4 * k : 4 * k + 4] = block
+    for x in range(4):
+        at = FAR.index(x)
+        block = blocks_ref[at] + blocks_ref[at + 4]
+        for k in range(8):
+            out_ref[4 * k + x] = block
 
 
 def dot3_turned(a, b):
@@ -112,7 +117,7 @@
 
 def landed(row):
     y, zh, core = row // 8, row // 2 % 4, row % 2
-    return (y * 2 + core) * 4 + zh
+    return (y * 2 + core) * 4 + FAR.index(zh)
 
 
 def average_kernel(
@@ -134,8 +139,9 @@
     rows = align_ref.shape[0]
     columns = 2 * rows
     heads = 8
-    first = weights_ref[:, 0:columns, :].reshape(-1, LANES)
-    tails = [weights_ref[k, columns:, :] for k in range(16)]
+    order = [MIDDLE.index(c) for c in range(16)]
+    first = jnp.concatenate([weights_ref[k, 0:columns, :] for k in order], axis=0)
+    tails = [weights_ref[k, columns:, :] for k in order]
     second = jnp.concatenate([t[:, half] for t in tails for half in HALVES], axis=0)
     weights = jnp.concatenate([first.T, second.T], axis=0)
     wh, wl = split(weights)
@@ -192,7 +198,7 @@
             block = jnp.concatenate(
                 [
                     right_ref[pl.ds((y * 2 + core) * 96 + g, 16, stride=6), :]
-                    for y in range(4)
+                    for y in RING
                 ],
                 axis=0,
             )
@@ -249,7 +255,7 @@
         return (((y * 4 + zh) * 2 + core) * 4 + zl) * 4 + x
 
     return [
-        [index(y, zh, core, zl, x) for y, zl in pair for zh in range(4)]
+        [index(y, zh, core, zl, x) for y, zl in pair for zh in FAR]
         for core in range(2)
         for x in range(4)
         for pair in sides
@@ -303,9 +309,11 @@
         outer_gain,
         outer_bias[None],
     )
-    near = lax.all_to_all(normed, "zh", 0, 0, tiled=True).reshape(192, 128)
+    near = lax.all_to_all(
+        normed, "zh", 0, 0, axis_index_groups=[list(FAR)], tiled=True
+    ).reshape(192, 128)
     near, packed = lax.optimization_barrier((near, packed))
-    weights = lax.all_to_all(packed, COL, 0, 0, tiled=True)
+    weights = lax.all_to_all(packed, COL, 0, 0, axis_index_groups=[list(MIDDLE)], tiled=True)
     gathered = lax.all_gather(near, ("y", "core"), axis=0, tiled=True).reshape(32, 48, 128)
     alignment_out, left, right = pl.pallas_call(
         average_kernel,
@@ -331,7 +339,7 @@
     )(right)
     right_all = lax.all_to_all(right, ("y", "core", "x"), 0, 0, tiled=True)
     right_all = right_all.reshape(768, 128)
-    left_all = lax.all_gather(left, "zl", axis=0, tiled=True)
+    left_all = lax.all_gather(left, "zl", axis=0, axis_index_groups=[list(RING)], tiled=True)
     pair_out = pl.pallas_call(
         outer_kernel,
         out_shape=shape(24, 48, 128),

time: 101 us -> 98.7 us (0.977)
  waiting for transfers between devices: 13.2 us -> 2.27 us
  starting transfers between devices: 34.3 us -> 43.3 us
    all_to_all x2, waiting for transfers between devices: 11.3 us -> 2.26 us  [the longest x1 2.26 us: on_device(): lax.all_to_all(normed, 'zh', 0, 0, axis_index_groups=[list(FAR)], tiled=T...]
    all_to_all x1, starting transfers between devices: 3.7 us -> 12.3 us  [on_device(): lax.all_to_all(right, ALL, 0, 0, axis_index_groups=mirrored(), tiled=True)]
    all_to_all x1, waiting for transfers between devices: 1.88 us -> 0.01 us  [on_device(): lax.all_to_all(right, ALL, 0, 0, axis_index_groups=mirrored(), tiled=True)]
    all_gather x1, blocking collectives: 13.7 us -> 11.8 us  [on_device(): lax.all_gather(left, 'zl', axis=0, axis_index_groups=[list(RING)], tiled=...]
    all_to_all x2, starting transfers between devices: 21.4 us -> 22.9 us  [the longest x1 17.6 us: on_device(): lax.all_to_all(normed, 'zh', 0, 0, axis_index_groups=[list(FAR)], tiled=T...]
    all_to_all x1, starting transfers between devices: 9.15 us -> 8.08 us  [on_device(): right_all = lax.all_to_all(right, ('y', 'core', 'x'), 0, 0, tiled=True)]
  transfers between devices with their start and end apart: 4 -> 4, of which waited for: 2 -> 1; matrix products, arithmetic and copies ran while one was open for 0% -> 0% of each run, Pallas kernels for 1% -> 1%
where the time goes in v6:
time: 98.7 us; the launch traced here: 98 us
  starting transfers between devices  43.3 us (44%)
  blocking collectives  38.7 us (39%)
  Pallas kernels  11.2 us (11%)
  waiting for transfers between devices  2.27 us (2%)
  local copies, waits for them, and re-layouts  1.74 us (2%)
    all_to_all x1, starting transfers between devices, on_device(): lax.all_to_all(normed, 'zh', 0, 0, axis_index_groups=[list(FAR)], tiled=T...  17.6 us
    all_gather x1, blocking collectives, on_device(): lax.all_gather(near, ('y', 'core'), axis=0, tiled=True).reshape(32, 48, 128)  14.1 us
    all_gather x1, blocking collectives, on_device(): left = lax.all_gather(left, 'x', axis=0, tiled=True)  12.8 us
    all_to_all x1, starting transfers between devices, on_device(): lax.all_to_all(right, ALL, 0, 0, axis_index_groups=mirrored(), tiled=True)  12.3 us
    all_gather x1, blocking collectives, on_device(): lax.all_gather(left, 'zl', axis=0, axis_index_groups=[list(RING)], tiled=...  11.8 us
    all_to_all x1, starting transfers between devices, on_device(): right_all = lax.all_to_all(right, ('y', 'core', 'x'), 0, 0, tiled=True)  8.08 us
    all_to_all x1, starting transfers between devices, on_device(): lax.all_to_all(packed, COL, 0, 0, axis_index_groups=[list(MIDDLE)], tiled...  5.31 us
    pallas_call x1, Pallas kernels, on_device(): pl.pallas_call(outer_kernel, out_shape=shape(24, 48, 128), scratch_shapes...  4.95 us
  transfers between devices with their start and end apart: 4, of which 1 were waited for; matrix products, arithmetic and copies ran while one was open for 0% of the time, Pallas kernels for 1%

profile of v6, /device:TPU:2, one launch (start us, length us, event | category | flops | bytes accessed | tf_op | source)
XLA Modules:
  0.0 98.0 jit_solution(15801547261198844493)
XLA Ops:
  0.6 0.0 copy-start.4
  0.6 1.7 %shard_map.131 = f32[4,48,128]{2,1,0:T(8,128)} custom-call(f32[24,4,64]{2,1,0:T(4,128)} %align_ref.5, f32[1,64]{1,0:T(1,128)} %bitcast.14), custom_call_target="tpu_custom_call" | custom-call | tf_op jit(solution)/shard_map/pallas_call | solution.py:291
  2.4 0.0 copy-start.2
  2.4 0.0 copy-start.3
  2.4 17.6 %all-to-all-start = ((f32[4,48,128]{2,1,0:T(8,128)}), f32[4,48,128]{2,1,0:T(8,128)S(1)}, u32[]{:S(2)}, u32[]{:S(2)}) async-start(f32[4,48,128]{2,1,0:T(8,128)} %shard_map.131), calls=%async_computation | async-start | bytes 196608 | tf_op jit(solution)/shard_map/all_to_all | solution.py:312
  20.0 0.0 copy-start.9
  20.0 0.0 copy-start.10
  20.0 0.0 copy-start.11
  20.0 0.0 copy-done.4
  20.0 0.0 copy-done.2
  20.0 0.0 copy-done.3
  20.0 0.6 copy-done.9
  20.6 0.0 copy-done.10
  20.6 0.0 copy-done.11
  20.7 0.0 copy-start.1
  20.7 1.0 %copy-done.1 = f32[1024,128]{1,0:T(8,128)S(1)} copy-done((f32[1024,128]{1,0:T(8,128)S(1)}, f32[1024,128]{1,0:T(8,128)}, u32[]{:S(2)}) %copy-start.1) | copy-done | bytes 524312
  21.7 1.4 %shard_map.132 = (f32[16,72,128]{2,1,0:T(8,128)}, f32[24,1024]{1,0:T(8,128)S(1)}, bf16[2048,256]{1,0:T(8,128)(2,1)S(1)}, f32[8,128]{1,0:T(8,128)S(1)}) custom-call(f32[8,24,48]{2,1,0:T(8,128)S(1)} %copy-done.3, f32[24,4,64]{2,1,0:T(4,128)S(1)} %copy-done.2, f32[64,256]{1,0:T(8,128)S(1)} %copy-done.4, f32[1024,128]{1,0:T(8,128)S(1)} %copy-done.1, ...), custom_call_target="tpu_custom_call" | custom-call | tf_op jit(solution)/shard_map/pallas_call | solution.py:294
  23.1 2.3 %all-to-all-done = f32[4,48,128]{2,1,0:T(8,128)S(1)} async-done(((f32[4,48,128]{2,1,0:T(8,128)}), f32[4,48,128]{2,1,0:T(8,128)S(1)}, u32[]{:S(2)}, u32[]{:S(2)}) %all-to-all-start) | async-done | bytes 98336 | tf_op jit(solution)/shard_map/all_to_all | solution.py:312
  25.4 5.3 %all-to-all-start.1 = ((f32[16,72,128]{2,1,0:T(8,128)}), f32[16,72,128]{2,1,0:T(8,128)S(1)}, u32[]{:S(2)}, u32[]{:S(2)}) async-start(f32[16,72,128]{2,1,0:T(8,128)} %get-tuple-element.14), calls=%async_computation.1 | async-start | bytes 1179648 | tf_op jit(solution)/shard_map/all_to_all | solution.py:316
  30.7 0.0 copy-start.5
  30.7 0.0 copy-start.6
  30.7 0.0 copy-start.7
  30.7 0.0 copy-start.8
  30.7 14.1 %all_gather.9 = f32[1536,128]{1,0:T(8,128)S(1)} all-gather(f32[192,128]{1,0:T(8,128)S(1)} %bitcast.18), channel_id=1, replica_groups=mesh['y'=4,'zh'=4,'core'=2,'zl'=4,'x'=4] {'y','core'}, dimensions={0}, use_global_device_ids=true | all-gather | bytes 884736 | tf_op jit(solution)/shard_map/all_gather | solution.py:317
  44.8 0.0 all-to-all-done.1.weights_ref
  44.9 0.0 copy-done.5
  44.9 0.0 copy-done.6
  44.9 0.0 copy-done.7
  44.9 0.0 copy-done.8
  44.9 2.4 %shard_map.133 = (f32[24,4,64]{2,1,0:T(4,128)}, f32[24,128]{1,0:T(8,128)S(1)}, f32[8,24,128]{2,1,0:T(8,128)}) custom-call(f32[16,72,128]{2,1,0:T(8,128)S(1)} %all-to-all-done.1.weights_ref, f32[32,48,128]{2,1,0:T(8,128)S(1)} %bitcast.9, f32[24,1024]{1,0:T(8,128)S(1)} %get-tuple-element.16.gate_ref, f32[8,128]{1,0:T(8,128)S(1)} %get-tuple-element.17.small_ref, ...), custom_call_target="tpu_custom_call" | custom-call | tf_op jit(solution)/shard_map/pallas_call | solution.py:318
  47.3 12.3 %all-to-all-start.2 = ((f32[8,24,128]{2,1,0:T(8,128)}), f32[8,24,128]{2,1,0:T(8,128)S(1)}, u32[]{:S(2)}, u32[]{:S(2)}) async-start(f32[8,24,128]{2,1,0:T(8,128)} %get-tuple-element.19), calls=%async_computation.2 | async-start | bytes 196608 | tf_op jit(solution)/shard_map/all_to_all | solution.py:334
  59.6 12.8 %all_gather.10 = f32[96,128]{1,0:T(8,128)S(1)} all-gather(f32[24,128]{1,0:T(8,128)S(1)} %get-tuple-element.20), channel_id=1, replica_groups=mesh['y'=4,'zh'=4,'core'=2,'zl'=4,'x'=4] {'x'}, dimensions={0}, use_global_device_ids=true | all-gather | bytes 61440 | tf_op jit(solution)/shard_map/all_gather | solution.py:335
  72.4 0.0 all-to-all-done.2.blocks_ref
  72.4 0.8 shard_map.134
  73.1 0.0 copy-start
  73.2 8.1 %all-to-all-start.3 = ((f32[32,24,128]{2,1,0:T(8,128)}), f32[32,24,128]{2,1,0:T(8,128)S(1)}, u32[]{:S(2)}, u32[]{:S(2)}) async-start(f32[32,24,128]{2,1,0:T(8,128)} %shard_map.134), calls=%async_computation.3 | async-start | bytes 786432 | tf_op jit(solution)/shard_map/all_to_all | solution.py:340
  81.2 11.8 %all_gather.11.left_ref = f32[384,128]{1,0:T(8,128)S(1)} all-gather(f32[96,128]{1,0:T(8,128)S(1)} %all_gather.10), channel_id=1, replica_groups={{0,8,12,4},{1,9,13,5},{2,10,14,6},{3,11,15,7},{16,24,28,20},{17,25,29,2..., dimensions={0}, use_global_device_ids=true | all-gather | bytes 245760 | tf_op jit(solution)/shard_map/all_gather | solution.py:342
  93.1 0.0 all-to-all-done.3
  93.1 0.0 copy-done
  93.1 5.0 %shard_map.135 = f32[24,48,128]{2,1,0:T(8,128)} custom-call(f32[384,128]{1,0:T(8,128)S(1)} %all_gather.11.left_ref, f32[768,128]{1,0:T(8,128)S(1)} %bitcast.10, f32[24,48,128]{2,1,0:T(8,128)S(1)} %copy-done, bf16[2048,256]{1,0:T(8,128)(2,1)S(1)} %get-tuple-element.23.spread_ref, f32[8,128]{1,0:T(8,128)S(1)} %get-tuple-element.17.small_ref), custom_call_target="tpu_custom_call" | custom-call | tf_op jit(solution)/shard_map/pallas_call | solution.py:343
Async XLA Ops:
  0.6 19.3 %copy-start.4 = (f32[64,256]{1,0:T(8,128)S(1)}, f32[64,256]{1,0:T(8,128)}, u32[]{:S(2)}) copy-start(f32[64,256]{1,0:T(8,128)} %gate_w_ref.1) | copy-start | bytes 196612
  2.4 17.6 %copy-start.2 = (f32[24,4,64]{2,1,0:T(4,128)S(1)}, f32[24,4,64]{2,1,0:T(4,128)}, u32[]{:S(2)}) copy-start(f32[24,4,64]{2,1,0:T(4,128)} %align_ref.5) | copy-start | bytes 73732
  2.4 17.6 %copy-start.3 = (f32[8,24,48]{2,1,0:T(8,128)S(1)}, f32[8,24,48]{2,1,0:T(8,128)}, u32[]{:S(2)}) copy-start(f32[8,24,48]{2,1,0:T(8,128)} %pair_w_ref.1) | copy-start | bytes 110596
  2.4 23.0 %all-to-all-start = ((f32[4,48,128]{2,1,0:T(8,128)}), f32[4,48,128]{2,1,0:T(8,128)S(1)}, u32[]{:S(2)}, u32[]{:S(2)}) async-start(f32[4,48,128]{2,1,0:T(8,128)} %shard_map.131), calls=%async_computation | async-start | bytes 196608 | tf_op jit(solution)/shard_map/all_to_all | solution.py:312
  20.0 0.7 copy-start.9
  20.0 0.7 copy-start.10
  20.0 0.7 copy-start.11
  20.7 1.0 %copy-start.1 = (f32[1024,128]{1,0:T(8,128)S(1)}, f32[1024,128]{1,0:T(8,128)}, u32[]{:S(2)}) copy-start(f32[1024,128]{1,0:T(8,128)} %outer_ref.1) | copy-start | bytes 1572868
  25.4 19.5 %all-to-all-start.1 = ((f32[16,72,128]{2,1,0:T(8,128)}), f32[16,72,128]{2,1,0:T(8,128)S(1)}, u32[]{:S(2)}, u32[]{:S(2)}) async-start(f32[16,72,128]{2,1,0:T(8,128)} %get-tuple-element.14), calls=%async_computation.1 | async-start | bytes 1179648 | tf_op jit(solution)/shard_map/all_to_all | solution.py:316
  30.7 14.2 %copy-start.5 = (f32[64,256]{1,0:T(8,128)S(1)}, f32[64,256]{1,0:T(8,128)}, u32[]{:S(2)}) copy-start(f32[64,256]{1,0:T(8,128)} %value_ref.1) | copy-start | bytes 196612
  30.7 14.2 %copy-start.6 = (f32[256,64]{0,1:T(8,128)S(1)}, f32[256,64]{0,1:T(8,128)}, u32[]{:S(2)}) copy-start(f32[256,64]{0,1:T(8,128)} %param.18) | copy-start | bytes 196612
  30.7 14.2 %copy-start.7 = (f32[64,32]{0,1:T(8,128)S(1)}, f32[64,32]{0,1:T(8,128)}, u32[]{:S(2)}) copy-start(f32[64,32]{0,1:T(8,128)} %param.20) | copy-start | bytes 24580
  30.7 14.2 %copy-start.8 = (f32[64,32]{0,1:T(8,128)S(1)}, f32[64,32]{0,1:T(8,128)}, u32[]{:S(2)}) copy-start(f32[64,32]{0,1:T(8,128)} %param.21) | copy-start | bytes 24580
  47.3 25.1 %all-to-all-start.2 = ((f32[8,24,128]{2,1,0:T(8,128)}), f32[8,24,128]{2,1,0:T(8,128)S(1)}, u32[]{:S(2)}, u32[]{:S(2)}) async-start(f32[8,24,128]{2,1,0:T(8,128)} %get-tuple-element.19), calls=%async_computation.2 | async-start | bytes 196608 | tf_op jit(solution)/shard_map/all_to_all | solution.py:334
  73.1 19.9 %copy-start = (f32[24,48,128]{2,1,0:T(8,128)S(1)}, f32[24,48,128]{2,1,0:T(8,128)}, u32[]{:S(2)}) copy-start(f32[24,48,128]{2,1,0:T(8,128)} %state_ref.1) | copy-start | bytes 1769476
  73.2 19.9 %all-to-all-start.3 = ((f32[32,24,128]{2,1,0:T(8,128)}), f32[32,24,128]{2,1,0:T(8,128)S(1)}, u32[]{:S(2)}, u32[]{:S(2)}) async-start(f32[32,24,128]{2,1,0:T(8,128)} %shard_map.134), calls=%async_computation.3 | async-start | bytes 786432 | tf_op jit(solution)/shard_map/all_to_all | solution.py:340

commit v7 on v6

--- a/solution.py
+++ b/solution.py
@@ -12,9 +12,9 @@
 ROW = ("y", "zh", "core")
 COL = ("zl", "x")
 ALL = ROW + COL
-FAR = (2, 3, 0, 1)
+FAR = (2, 0, 3, 1)
 RING = (0, 2, 3, 1)
-MIDDLE = (5, *range(5), *range(6, 16))
+MIDDLE = (6, *range(6), *range(7, 16))
 LANES = 128
 HALVES = (slice(0, 64), slice(64, 128))
 

time: 98.7 us -> 98.1 us (level)
  blocking collectives: 38.7 us -> 37.6 us
    all_gather x1, blocking collectives: 12.8 us -> 11.7 us  [on_device(): left = lax.all_gather(left, 'x', axis=0, tiled=True)]
where the time goes in v7:
time: 98.1 us; the launch traced here: 97.5 us
  starting transfers between devices  44.2 us (45%)
  blocking collectives  37.6 us (38%)
  Pallas kernels  11.2 us (11%)
  waiting for transfers between devices  2.02 us (2%)
  local copies, waits for them, and re-layouts  1.74 us (2%)
    all_to_all x1, starting transfers between devices, on_device(): lax.all_to_all(normed, 'zh', 0, 0, axis_index_groups=[list(FAR)], tiled=T...  17.6 us
    all_gather x1, blocking collectives, on_device(): lax.all_gather(near, ('y', 'core'), axis=0, tiled=True).reshape(32, 48, 128)  14.1 us
    all_to_all x1, starting transfers between devices, on_device(): lax.all_to_all(right, ALL, 0, 0, axis_index_groups=mirrored(), tiled=True)  12.8 us
    all_gather x1, blocking collectives, on_device(): lax.all_gather(left, 'zl', axis=0, axis_index_groups=[list(RING)], tiled=...  11.8 us
    all_gather x1, blocking collectives, on_device(): left = lax.all_gather(left, 'x', axis=0, tiled=True)  11.7 us
    all_to_all x1, starting transfers between devices, on_device(): right_all = lax.all_to_all(right, ('y', 'core', 'x'), 0, 0, tiled=True)  8.5 us
    all_to_all x1, starting transfers between devices, on_device(): lax.all_to_all(packed, COL, 0, 0, axis_index_groups=[list(MIDDLE)], tiled...  5.31 us
    pallas_call x1, Pallas kernels, on_device(): pl.pallas_call(outer_kernel, out_shape=shape(24, 48, 128), scratch_shapes...  4.95 us
  transfers between devices with their start and end apart: 4, of which 1 were waited for; matrix products, arithmetic and copies ran while one was open for 0% of the time, Pallas kernels for 1%

profile of v7, /device:TPU:2, one launch (start us, length us, event | category | flops | bytes accessed | tf_op | source)
XLA Modules:
  0.0 97.5 jit_solution(4893474482790531651)
XLA Ops:
  0.6 0.0 copy-start.4
  0.6 1.7 %shard_map.131 = f32[4,48,128]{2,1,0:T(8,128)} custom-call(f32[24,4,64]{2,1,0:T(4,128)} %align_ref.5, f32[1,64]{1,0:T(1,128)} %bitcast.14), custom_call_target="tpu_custom_call" | custom-call | tf_op jit(solution)/shard_map/pallas_call | solution.py:291
  2.4 0.0 copy-start.2
  2.4 0.0 copy-start.3
  2.4 17.6 %all-to-all-start = ((f32[4,48,128]{2,1,0:T(8,128)}), f32[4,48,128]{2,1,0:T(8,128)S(1)}, u32[]{:S(2)}, u32[]{:S(2)}) async-start(f32[4,48,128]{2,1,0:T(8,128)} %shard_map.131), calls=%async_computation | async-start | bytes 196608 | tf_op jit(solution)/shard_map/all_to_all | solution.py:312
  20.0 0.0 copy-start.9
  20.0 0.0 copy-start.10
  20.0 0.0 copy-start.11
  20.0 0.0 copy-done.4
  20.0 0.0 copy-done.2
  20.0 0.0 copy-done.3
  20.0 0.6 copy-done.9
  20.6 0.0 copy-done.10
  20.6 0.0 copy-done.11
  20.7 0.0 copy-start.1
  20.7 1.0 %copy-done.1 = f32[1024,128]{1,0:T(8,128)S(1)} copy-done((f32[1024,128]{1,0:T(8,128)S(1)}, f32[1024,128]{1,0:T(8,128)}, u32[]{:S(2)}) %copy-start.1) | copy-done | bytes 524312
  21.7 1.4 %shard_map.132 = (f32[16,72,128]{2,1,0:T(8,128)}, f32[24,1024]{1,0:T(8,128)S(1)}, bf16[2048,256]{1,0:T(8,128)(2,1)S(1)}, f32[8,128]{1,0:T(8,128)S(1)}) custom-call(f32[8,24,48]{2,1,0:T(8,128)S(1)} %copy-done.3, f32[24,4,64]{2,1,0:T(4,128)S(1)} %copy-done.2, f32[64,256]{1,0:T(8,128)S(1)} %copy-done.4, f32[1024,128]{1,0:T(8,128)S(1)} %copy-done.1, ...), custom_call_target="tpu_custom_call" | custom-call | tf_op jit(solution)/shard_map/pallas_call | solution.py:294
  23.1 2.0 %all-to-all-done = f32[4,48,128]{2,1,0:T(8,128)S(1)} async-done(((f32[4,48,128]{2,1,0:T(8,128)}), f32[4,48,128]{2,1,0:T(8,128)S(1)}, u32[]{:S(2)}, u32[]{:S(2)}) %all-to-all-start) | async-done | bytes 98336 | tf_op jit(solution)/shard_map/all_to_all | solution.py:312
  25.1 5.3 %all-to-all-start.1 = ((f32[16,72,128]{2,1,0:T(8,128)}), f32[16,72,128]{2,1,0:T(8,128)S(1)}, u32[]{:S(2)}, u32[]{:S(2)}) async-start(f32[16,72,128]{2,1,0:T(8,128)} %get-tuple-element.14), calls=%async_computation.1 | async-start | bytes 1179648 | tf_op jit(solution)/shard_map/all_to_all | solution.py:316
  30.4 0.0 copy-start.5
  30.4 0.0 copy-start.6
  30.5 0.0 copy-start.7
  30.5 0.0 copy-start.8
  30.5 14.1 %all_gather.9 = f32[1536,128]{1,0:T(8,128)S(1)} all-gather(f32[192,128]{1,0:T(8,128)S(1)} %bitcast.18), channel_id=1, replica_groups=mesh['y'=4,'zh'=4,'core'=2,'zl'=4,'x'=4] {'y','core'}, dimensions={0}, use_global_device_ids=true | all-gather | bytes 884736 | tf_op jit(solution)/shard_map/all_gather | solution.py:317
  44.6 0.0 all-to-all-done.1.weights_ref
  44.6 0.0 copy-done.5
  44.6 0.0 copy-done.6
  44.6 0.0 copy-done.7
  44.6 0.0 copy-done.8
  44.6 2.4 %shard_map.133 = (f32[24,4,64]{2,1,0:T(4,128)}, f32[24,128]{1,0:T(8,128)S(1)}, f32[8,24,128]{2,1,0:T(8,128)}) custom-call(f32[16,72,128]{2,1,0:T(8,128)S(1)} %all-to-all-done.1.weights_ref, f32[32,48,128]{2,1,0:T(8,128)S(1)} %bitcast.9, f32[24,1024]{1,0:T(8,128)S(1)} %get-tuple-element.16.gate_ref, f32[8,128]{1,0:T(8,128)S(1)} %get-tuple-element.17.small_ref, ...), custom_call_target="tpu_custom_call" | custom-call | tf_op jit(solution)/shard_map/pallas_call | solution.py:318
  47.0 12.8 %all-to-all-start.2 = ((f32[8,24,128]{2,1,0:T(8,128)}), f32[8,24,128]{2,1,0:T(8,128)S(1)}, u32[]{:S(2)}, u32[]{:S(2)}) async-start(f32[8,24,128]{2,1,0:T(8,128)} %get-tuple-element.19), calls=%async_computation.2 | async-start | bytes 196608 | tf_op jit(solution)/shard_map/all_to_all | solution.py:334
  59.8 11.7 %all_gather.10 = f32[96,128]{1,0:T(8,128)S(1)} all-gather(f32[24,128]{1,0:T(8,128)S(1)} %get-tuple-element.20), channel_id=1, replica_groups=mesh['y'=4,'zh'=4,'core'=2,'zl'=4,'x'=4] {'x'}, dimensions={0}, use_global_device_ids=true | all-gather | bytes 61440 | tf_op jit(solution)/shard_map/all_gather | solution.py:335
  71.5 0.0 all-to-all-done.2.blocks_ref
  71.5 0.8 shard_map.134
  72.2 0.0 copy-start
  72.2 8.5 %all-to-all-start.3 = ((f32[32,24,128]{2,1,0:T(8,128)}), f32[32,24,128]{2,1,0:T(8,128)S(1)}, u32[]{:S(2)}, u32[]{:S(2)}) async-start(f32[32,24,128]{2,1,0:T(8,128)} %shard_map.134), calls=%async_computation.3 | async-start | bytes 786432 | tf_op jit(solution)/shard_map/all_to_all | solution.py:340
  80.8 11.8 %all_gather.11.left_ref = f32[384,128]{1,0:T(8,128)S(1)} all-gather(f32[96,128]{1,0:T(8,128)S(1)} %all_gather.10), channel_id=1, replica_groups={{0,8,12,4},{1,9,13,5},{2,10,14,6},{3,11,15,7},{16,24,28,20},{17,25,29,2..., dimensions={0}, use_global_device_ids=true | all-gather | bytes 245760 | tf_op jit(solution)/shard_map/all_gather | solution.py:342
  92.5 0.0 all-to-all-done.3
  92.5 0.0 copy-done
  92.5 5.0 %shard_map.135 = f32[24,48,128]{2,1,0:T(8,128)} custom-call(f32[384,128]{1,0:T(8,128)S(1)} %all_gather.11.left_ref, f32[768,128]{1,0:T(8,128)S(1)} %bitcast.10, f32[24,48,128]{2,1,0:T(8,128)S(1)} %copy-done, bf16[2048,256]{1,0:T(8,128)(2,1)S(1)} %get-tuple-element.23.spread_ref, f32[8,128]{1,0:T(8,128)S(1)} %get-tuple-element.17.small_ref), custom_call_target="tpu_custom_call" | custom-call | tf_op jit(solution)/shard_map/pallas_call | solution.py:343
Async XLA Ops:
  0.6 19.3 %copy-start.4 = (f32[64,256]{1,0:T(8,128)S(1)}, f32[64,256]{1,0:T(8,128)}, u32[]{:S(2)}) copy-start(f32[64,256]{1,0:T(8,128)} %gate_w_ref.1) | copy-start | bytes 196612
  2.4 17.6 %copy-start.2 = (f32[24,4,64]{2,1,0:T(4,128)S(1)}, f32[24,4,64]{2,1,0:T(4,128)}, u32[]{:S(2)}) copy-start(f32[24,4,64]{2,1,0:T(4,128)} %align_ref.5) | copy-start | bytes 73732
  2.4 17.6 %copy-start.3 = (f32[8,24,48]{2,1,0:T(8,128)S(1)}, f32[8,24,48]{2,1,0:T(8,128)}, u32[]{:S(2)}) copy-start(f32[8,24,48]{2,1,0:T(8,128)} %pair_w_ref.1) | copy-start | bytes 110596
  2.4 22.8 %all-to-all-start = ((f32[4,48,128]{2,1,0:T(8,128)}), f32[4,48,128]{2,1,0:T(8,128)S(1)}, u32[]{:S(2)}, u32[]{:S(2)}) async-start(f32[4,48,128]{2,1,0:T(8,128)} %shard_map.131), calls=%async_computation | async-start | bytes 196608 | tf_op jit(solution)/shard_map/all_to_all | solution.py:312
  20.0 0.7 copy-start.9
  20.0 0.7 copy-start.10
  20.0 0.7 copy-start.11
  20.7 1.0 %copy-start.1 = (f32[1024,128]{1,0:T(8,128)S(1)}, f32[1024,128]{1,0:T(8,128)}, u32[]{:S(2)}) copy-start(f32[1024,128]{1,0:T(8,128)} %outer_ref.1) | copy-start | bytes 1572868
  25.1 19.5 %all-to-all-start.1 = ((f32[16,72,128]{2,1,0:T(8,128)}), f32[16,72,128]{2,1,0:T(8,128)S(1)}, u32[]{:S(2)}, u32[]{:S(2)}) async-start(f32[16,72,128]{2,1,0:T(8,128)} %get-tuple-element.14), calls=%async_computation.1 | async-start | bytes 1179648 | tf_op jit(solution)/shard_map/all_to_all | solution.py:316
  30.4 14.2 %copy-start.5 = (f32[64,256]{1,0:T(8,128)S(1)}, f32[64,256]{1,0:T(8,128)}, u32[]{:S(2)}) copy-start(f32[64,256]{1,0:T(8,128)} %value_ref.1) | copy-start | bytes 196612
  30.4 14.2 %copy-start.6 = (f32[256,64]{0,1:T(8,128)S(1)}, f32[256,64]{0,1:T(8,128)}, u32[]{:S(2)}) copy-start(f32[256,64]{0,1:T(8,128)} %param.18) | copy-start | bytes 196612
  30.5 14.2 %copy-start.7 = (f32[64,32]{0,1:T(8,128)S(1)}, f32[64,32]{0,1:T(8,128)}, u32[]{:S(2)}) copy-start(f32[64,32]{0,1:T(8,128)} %param.20) | copy-start | bytes 24580
  30.5 14.2 %copy-start.8 = (f32[64,32]{0,1:T(8,128)S(1)}, f32[64,32]{0,1:T(8,128)}, u32[]{:S(2)}) copy-start(f32[64,32]{0,1:T(8,128)} %param.21) | copy-start | bytes 24580
  47.0 24.5 %all-to-all-start.2 = ((f32[8,24,128]{2,1,0:T(8,128)}), f32[8,24,128]{2,1,0:T(8,128)S(1)}, u32[]{:S(2)}, u32[]{:S(2)}) async-start(f32[8,24,128]{2,1,0:T(8,128)} %get-tuple-element.19), calls=%async_computation.2 | async-start | bytes 196608 | tf_op jit(solution)/shard_map/all_to_all | solution.py:334
  72.2 20.3 %copy-start = (f32[24,48,128]{2,1,0:T(8,128)S(1)}, f32[24,48,128]{2,1,0:T(8,128)}, u32[]{:S(2)}) copy-start(f32[24,48,128]{2,1,0:T(8,128)} %state_ref.1) | copy-start | bytes 1769476
  72.2 20.3 %all-to-all-start.3 = ((f32[32,24,128]{2,1,0:T(8,128)}), f32[32,24,128]{2,1,0:T(8,128)S(1)}, u32[]{:S(2)}, u32[]{:S(2)}) async-start(f32[32,24,128]{2,1,0:T(8,128)} %shard_map.134), calls=%async_computation.3 | async-start | bytes 786432 | tf_op jit(solution)/shard_map/all_to_all | solution.py:340

commit v8 on v7

--- a/solution.py
+++ b/solution.py
@@ -115,6 +115,10 @@
     return one(ah, bh) + (one(ah, bl) + one(al, bh))
 
 
+def turned_dot(a, b):
+    return lax.dot_general(a, b, (((0,), (0,)), ((), ())), preferred_element_type=F32)
+
+
 def landed(row):
     y, zh, core = row // 8, row // 2 % 4, row % 2
     return (y * 2 + core) * 4 + FAR.index(zh)
@@ -134,7 +138,6 @@
     left_ref,
     right_ref,
     left_tmp,
-    right_tmp,
 ):
     rows = align_ref.shape[0]
     columns = 2 * rows
@@ -143,7 +146,7 @@
     first = jnp.concatenate([weights_ref[k, 0:columns, :] for k in order], axis=0)
     tails = [weights_ref[k, columns:, :] for k in order]
     second = jnp.concatenate([t[:, half] for t in tails for half in HALVES], axis=0)
-    weights = jnp.concatenate([first.T, second.T], axis=0)
+    weights = jnp.concatenate([first, second], axis=1)
     wh, wl = split(weights)
     mixed = []
     for p in range(2):
@@ -151,7 +154,7 @@
             gathered_ref[landed(r), p * rows : (p + 1) * rows, :] for r in range(32)
         ]
         fh, fl = split(jnp.concatenate(blocks, axis=0))
-        mixed.append(dot(wh, fh) + (dot(wh, fl) + dot(wl, fh)))
+        mixed.append(turned_dot(wh, fh) + (turned_dot(wh, fl) + turned_dot(wl, fh)))
     lane = lax.broadcasted_iota(jnp.int32, (rows, 512), 1)
     lane_head = lax.rem(lax.div(lane, 32), heads)
     vh, vl = split(twice(value_ref[...]))
@@ -169,13 +172,13 @@
     for s in range(4):
         out_ref[:, s, :] = aligned[s * rows : (s + 1) * rows]
     normed = normalize(aligned, small_ref[0:1, 0:64])
-    left_tmp[:, 0:32] = dot3_turned(normed, left_w_ref[...])
-    right_tmp[:, 0:32] = dot3_turned(normed, right_w_ref[...])
+    both = jnp.concatenate([left_w_ref[...], right_w_ref[...]], axis=0)
+    left_tmp[:, 0:64] = dot3_turned(normed, both)
     left = jnp.concatenate(
         [left_tmp[pl.ds(k, rows, stride=4), 0:32] for k in range(4)], axis=1
     )
     right = jnp.concatenate(
-        [right_tmp[pl.ds(k, rows, stride=4), 0:32] for k in range(4)], axis=1
+        [left_tmp[pl.ds(k, rows, stride=4), :][:, 32:64] for k in range(4)], axis=1
     )
     fill(left_ref, left)
     y, zl = lax.axis_index("y"), lax.axis_index("zl")
@@ -318,7 +321,7 @@
     alignment_out, left, right = pl.pallas_call(
         average_kernel,
         out_shape=(shape(24, 4, 64), shape(24, 128), shape(8, 24, 128)),
-        scratch_shapes=[pltpu.VMEM((96, 128), F32), pltpu.VMEM((96, 128), F32)],
+        scratch_shapes=[pltpu.VMEM((96, 128), F32)],
         compiler_params=PARAMS,
     )(
         weights,

time: 98.1 us -> 98.1 us (level)
  no operation moved by 1% of the time
where the time goes in v8:
time: 98.1 us; the launch traced here: 97.5 us
  starting transfers between devices  44.2 us (45%)
  blocking collectives  37.6 us (38%)
  Pallas kernels  11.2 us (11%)
  waiting for transfers between devices  2.02 us (2%)
  local copies, waits for them, and re-layouts  1.74 us (2%)
    all_to_all x1, starting transfers between devices, on_device(): lax.all_to_all(normed, 'zh', 0, 0, axis_index_groups=[list(FAR)], tiled=T...  17.6 us
    all_gather x1, blocking collectives, on_device(): lax.all_gather(near, ('y', 'core'), axis=0, tiled=True).reshape(32, 48, 128)  14.1 us
    all_to_all x1, starting transfers between devices, on_device(): lax.all_to_all(right, ALL, 0, 0, axis_index_groups=mirrored(), tiled=True)  12.8 us
    all_gather x1, blocking collectives, on_device(): lax.all_gather(left, 'zl', axis=0, axis_index_groups=[list(RING)], tiled=...  11.8 us
    all_gather x1, blocking collectives, on_device(): left = lax.all_gather(left, 'x', axis=0, tiled=True)  11.7 us
    all_to_all x1, starting transfers between devices, on_device(): right_all = lax.all_to_all(right, ('y', 'core', 'x'), 0, 0, tiled=True)  8.49 us
    all_to_all x1, starting transfers between devices, on_device(): lax.all_to_all(packed, COL, 0, 0, axis_index_groups=[list(MIDDLE)], tiled...  5.31 us
    pallas_call x1, Pallas kernels, on_device(): pl.pallas_call(outer_kernel, out_shape=shape(24, 48, 128), scratch_shapes...  4.95 us
  transfers between devices with their start and end apart: 4, of which 1 were waited for; matrix products, arithmetic and copies ran while one was open for 0% of the time, Pallas kernels for 1%

profile of v8, /device:TPU:2, one launch (start us, length us, event | category | flops | bytes accessed | tf_op | source)
XLA Modules:
  0.0 97.5 jit_solution(5679651866542225371)
XLA Ops:
  0.6 0.0 copy-start.4
  0.6 1.7 %shard_map.131 = f32[4,48,128]{2,1,0:T(8,128)} custom-call(f32[24,4,64]{2,1,0:T(4,128)} %align_ref.5, f32[1,64]{1,0:T(1,128)} %bitcast.14), custom_call_target="tpu_custom_call" | custom-call | tf_op jit(solution)/shard_map/pallas_call | solution.py:294
  2.4 0.0 copy-start.2
  2.4 0.0 copy-start.3
  2.4 17.6 %all-to-all-start = ((f32[4,48,128]{2,1,0:T(8,128)}), f32[4,48,128]{2,1,0:T(8,128)S(1)}, u32[]{:S(2)}, u32[]{:S(2)}) async-start(f32[4,48,128]{2,1,0:T(8,128)} %shard_map.131), calls=%async_computation | async-start | bytes 196608 | tf_op jit(solution)/shard_map/all_to_all | solution.py:315
  20.0 0.0 copy-start.9
  20.0 0.0 copy-start.10
  20.0 0.0 copy-start.11
  20.0 0.0 copy-done.4
  20.0 0.0 copy-done.2
  20.0 0.0 copy-done.3
  20.0 0.6 copy-done.9
  20.6 0.0 copy-done.10
  20.6 0.0 copy-done.11
  20.7 0.0 copy-start.1
  20.7 1.0 %copy-done.1 = f32[1024,128]{1,0:T(8,128)S(1)} copy-done((f32[1024,128]{1,0:T(8,128)S(1)}, f32[1024,128]{1,0:T(8,128)}, u32[]{:S(2)}) %copy-start.1) | copy-done | bytes 524312
  21.7 1.4 %shard_map.132 = (f32[16,72,128]{2,1,0:T(8,128)}, f32[24,1024]{1,0:T(8,128)S(1)}, bf16[2048,256]{1,0:T(8,128)(2,1)S(1)}, f32[8,128]{1,0:T(8,128)S(1)}) custom-call(f32[8,24,48]{2,1,0:T(8,128)S(1)} %copy-done.3, f32[24,4,64]{2,1,0:T(4,128)S(1)} %copy-done.2, f32[64,256]{1,0:T(8,128)S(1)} %copy-done.4, f32[1024,128]{1,0:T(8,128)S(1)} %copy-done.1, ...), custom_call_target="tpu_custom_call" | custom-call | tf_op jit(solution)/shard_map/pallas_call | solution.py:297
  23.1 2.0 %all-to-all-done = f32[4,48,128]{2,1,0:T(8,128)S(1)} async-done(((f32[4,48,128]{2,1,0:T(8,128)}), f32[4,48,128]{2,1,0:T(8,128)S(1)}, u32[]{:S(2)}, u32[]{:S(2)}) %all-to-all-start) | async-done | bytes 98336 | tf_op jit(solution)/shard_map/all_to_all | solution.py:315
  25.1 5.3 %all-to-all-start.1 = ((f32[16,72,128]{2,1,0:T(8,128)}), f32[16,72,128]{2,1,0:T(8,128)S(1)}, u32[]{:S(2)}, u32[]{:S(2)}) async-start(f32[16,72,128]{2,1,0:T(8,128)} %get-tuple-element.14), calls=%async_computation.1 | async-start | bytes 1179648 | tf_op jit(solution)/shard_map/all_to_all | solution.py:319
  30.4 0.0 copy-start.5
  30.4 0.0 copy-start.6
  30.5 0.0 copy-start.7
  30.5 0.0 copy-start.8
  30.5 14.1 %all_gather.9 = f32[1536,128]{1,0:T(8,128)S(1)} all-gather(f32[192,128]{1,0:T(8,128)S(1)} %bitcast.18), channel_id=1, replica_groups=mesh['y'=4,'zh'=4,'core'=2,'zl'=4,'x'=4] {'y','core'}, dimensions={0}, use_global_device_ids=true | all-gather | bytes 884736 | tf_op jit(solution)/shard_map/all_gather | solution.py:320
  44.6 0.0 all-to-all-done.1.weights_ref
  44.6 0.0 copy-done.5
  44.6 0.0 copy-done.6
  44.6 0.0 copy-done.7
  44.6 0.0 copy-done.8
  44.6 2.4 %shard_map.133 = (f32[24,4,64]{2,1,0:T(4,128)}, f32[24,128]{1,0:T(8,128)S(1)}, f32[8,24,128]{2,1,0:T(8,128)}) custom-call(f32[16,72,128]{2,1,0:T(8,128)S(1)} %all-to-all-done.1.weights_ref, f32[32,48,128]{2,1,0:T(8,128)S(1)} %bitcast.9, f32[24,1024]{1,0:T(8,128)S(1)} %get-tuple-element.16.gate_ref, f32[8,128]{1,0:T(8,128)S(1)} %get-tuple-element.17.small_ref, ...), custom_call_target="tpu_custom_call" | custom-call | tf_op jit(solution)/shard_map/pallas_call | solution.py:321
  47.0 12.8 %all-to-all-start.2 = ((f32[8,24,128]{2,1,0:T(8,128)}), f32[8,24,128]{2,1,0:T(8,128)S(1)}, u32[]{:S(2)}, u32[]{:S(2)}) async-start(f32[8,24,128]{2,1,0:T(8,128)} %get-tuple-element.19), calls=%async_computation.2 | async-start | bytes 196608 | tf_op jit(solution)/shard_map/all_to_all | solution.py:337
  59.8 11.7 %all_gather.10 = f32[96,128]{1,0:T(8,128)S(1)} all-gather(f32[24,128]{1,0:T(8,128)S(1)} %get-tuple-element.20), channel_id=1, replica_groups=mesh['y'=4,'zh'=4,'core'=2,'zl'=4,'x'=4] {'x'}, dimensions={0}, use_global_device_ids=true | all-gather | bytes 61440 | tf_op jit(solution)/shard_map/all_gather | solution.py:338
  71.5 0.0 all-to-all-done.2.blocks_ref
  71.5 0.8 shard_map.134
  72.2 0.0 copy-start
  72.2 8.5 %all-to-all-start.3 = ((f32[32,24,128]{2,1,0:T(8,128)}), f32[32,24,128]{2,1,0:T(8,128)S(1)}, u32[]{:S(2)}, u32[]{:S(2)}) async-start(f32[32,24,128]{2,1,0:T(8,128)} %shard_map.134), calls=%async_computation.3 | async-start | bytes 786432 | tf_op jit(solution)/shard_map/all_to_all | solution.py:343
  80.7 11.8 %all_gather.11.left_ref = f32[384,128]{1,0:T(8,128)S(1)} all-gather(f32[96,128]{1,0:T(8,128)S(1)} %all_gather.10), channel_id=1, replica_groups={{0,8,12,4},{1,9,13,5},{2,10,14,6},{3,11,15,7},{16,24,28,20},{17,25,29,2..., dimensions={0}, use_global_device_ids=true | all-gather | bytes 245760 | tf_op jit(solution)/shard_map/all_gather | solution.py:345
  92.5 0.0 all-to-all-done.3
  92.5 0.0 copy-done
  92.5 5.0 %shard_map.135 = f32[24,48,128]{2,1,0:T(8,128)} custom-call(f32[384,128]{1,0:T(8,128)S(1)} %all_gather.11.left_ref, f32[768,128]{1,0:T(8,128)S(1)} %bitcast.10, f32[24,48,128]{2,1,0:T(8,128)S(1)} %copy-done, bf16[2048,256]{1,0:T(8,128)(2,1)S(1)} %get-tuple-element.23.spread_ref, f32[8,128]{1,0:T(8,128)S(1)} %get-tuple-element.17.small_ref), custom_call_target="tpu_custom_call" | custom-call | tf_op jit(solution)/shard_map/pallas_call | solution.py:346
Async XLA Ops:
  0.6 19.3 %copy-start.4 = (f32[64,256]{1,0:T(8,128)S(1)}, f32[64,256]{1,0:T(8,128)}, u32[]{:S(2)}) copy-start(f32[64,256]{1,0:T(8,128)} %gate_w_ref.1) | copy-start | bytes 196612
  2.4 17.6 %copy-start.2 = (f32[24,4,64]{2,1,0:T(4,128)S(1)}, f32[24,4,64]{2,1,0:T(4,128)}, u32[]{:S(2)}) copy-start(f32[24,4,64]{2,1,0:T(4,128)} %align_ref.5) | copy-start | bytes 73732
  2.4 17.6 %copy-start.3 = (f32[8,24,48]{2,1,0:T(8,128)S(1)}, f32[8,24,48]{2,1,0:T(8,128)}, u32[]{:S(2)}) copy-start(f32[8,24,48]{2,1,0:T(8,128)} %pair_w_ref.1) | copy-start | bytes 110596
  2.4 22.8 %all-to-all-start = ((f32[4,48,128]{2,1,0:T(8,128)}), f32[4,48,128]{2,1,0:T(8,128)S(1)}, u32[]{:S(2)}, u32[]{:S(2)}) async-start(f32[4,48,128]{2,1,0:T(8,128)} %shard_map.131), calls=%async_computation | async-start | bytes 196608 | tf_op jit(solution)/shard_map/all_to_all | solution.py:315
  20.0 0.7 copy-start.9
  20.0 0.7 copy-start.10
  20.0 0.7 copy-start.11
  20.7 1.0 %copy-start.1 = (f32[1024,128]{1,0:T(8,128)S(1)}, f32[1024,128]{1,0:T(8,128)}, u32[]{:S(2)}) copy-start(f32[1024,128]{1,0:T(8,128)} %outer_ref.1) | copy-start | bytes 1572868
  25.1 19.5 %all-to-all-start.1 = ((f32[16,72,128]{2,1,0:T(8,128)}), f32[16,72,128]{2,1,0:T(8,128)S(1)}, u32[]{:S(2)}, u32[]{:S(2)}) async-start(f32[16,72,128]{2,1,0:T(8,128)} %get-tuple-element.14), calls=%async_computation.1 | async-start | bytes 1179648 | tf_op jit(solution)/shard_map/all_to_all | solution.py:319
  30.4 14.2 %copy-start.5 = (f32[64,256]{1,0:T(8,128)S(1)}, f32[64,256]{1,0:T(8,128)}, u32[]{:S(2)}) copy-start(f32[64,256]{1,0:T(8,128)} %value_ref.1) | copy-start | bytes 196612
  30.4 14.2 %copy-start.6 = (f32[256,64]{0,1:T(8,128)S(1)}, f32[256,64]{0,1:T(8,128)}, u32[]{:S(2)}) copy-start(f32[256,64]{0,1:T(8,128)} %param.18) | copy-start | bytes 196612
  30.5 14.2 %copy-start.7 = (f32[64,32]{0,1:T(8,128)S(1)}, f32[64,32]{0,1:T(8,128)}, u32[]{:S(2)}) copy-start(f32[64,32]{0,1:T(8,128)} %param.20) | copy-start | bytes 24580
  30.5 14.2 %copy-start.8 = (f32[64,32]{0,1:T(8,128)S(1)}, f32[64,32]{0,1:T(8,128)}, u32[]{:S(2)}) copy-start(f32[64,32]{0,1:T(8,128)} %param.21) | copy-start | bytes 24580
  47.0 24.5 %all-to-all-start.2 = ((f32[8,24,128]{2,1,0:T(8,128)}), f32[8,24,128]{2,1,0:T(8,128)S(1)}, u32[]{:S(2)}, u32[]{:S(2)}) async-start(f32[8,24,128]{2,1,0:T(8,128)} %get-tuple-element.19), calls=%async_computation.2 | async-start | bytes 196608 | tf_op jit(solution)/shard_map/all_to_all | solution.py:337
  72.2 20.3 %copy-start = (f32[24,48,128]{2,1,0:T(8,128)S(1)}, f32[24,48,128]{2,1,0:T(8,128)}, u32[]{:S(2)}) copy-start(f32[24,48,128]{2,1,0:T(8,128)} %state_ref.1) | copy-start | bytes 1769476
  72.2 20.3 %all-to-all-start.3 = ((f32[32,24,128]{2,1,0:T(8,128)}), f32[32,24,128]{2,1,0:T(8,128)S(1)}, u32[]{:S(2)}, u32[]{:S(2)}) async-start(f32[32,24,128]{2,1,0:T(8,128)} %shard_map.134), calls=%async_computation.3 | async-start | bytes 786432 | tf_op jit(solution)/shard_map/all_to_all | solution.py:343

commit v9 on v8

--- a/solution.py
+++ b/solution.py
@@ -12,7 +12,7 @@
 ROW = ("y", "zh", "core")
 COL = ("zl", "x")
 ALL = ROW + COL
-FAR = (2, 0, 3, 1)
+FAR = (2, 3, 1, 0)
 RING = (0, 2, 3, 1)
 MIDDLE = (6, *range(6), *range(7, 16))
 LANES = 128

time: 98.1 us -> 98.3 us (level)
  no operation moved by 1% of the time
where the time goes in v9:
time: 98.3 us; the launch traced here: 97.7 us
  starting transfers between devices  43.7 us (44%)
  blocking collectives  38.3 us (39%)
  Pallas kernels  11.2 us (11%)
  waiting for transfers between devices  2.02 us (2%)
  local copies, waits for them, and re-layouts  1.74 us (2%)
    all_to_all x1, starting transfers between devices, on_device(): lax.all_to_all(normed, 'zh', 0, 0, axis_index_groups=[list(FAR)], tiled=T...  17.6 us
    all_gather x1, blocking collectives, on_device(): lax.all_gather(near, ('y', 'core'), axis=0, tiled=True).reshape(32, 48, 128)  14.1 us
    all_gather x1, blocking collectives, on_device(): left = lax.all_gather(left, 'x', axis=0, tiled=True)  12.4 us
    all_to_all x1, starting transfers between devices, on_device(): lax.all_to_all(right, ALL, 0, 0, axis_index_groups=mirrored(), tiled=True)  12 us
    all_gather x1, blocking collectives, on_device(): lax.all_gather(left, 'zl', axis=0, axis_index_groups=[list(RING)], tiled=...  11.8 us
    all_to_all x1, starting transfers between devices, on_device(): right_all = lax.all_to_all(right, ('y', 'core', 'x'), 0, 0, tiled=True)  8.45 us
    all_to_all x1, starting transfers between devices, on_device(): lax.all_to_all(packed, COL, 0, 0, axis_index_groups=[list(MIDDLE)], tiled...  5.56 us
    pallas_call x1, Pallas kernels, on_device(): pl.pallas_call(outer_kernel, out_shape=shape(24, 48, 128), scratch_shapes...  4.95 us
  transfers between devices with their start and end apart: 4, of which 1 were waited for; matrix products, arithmetic and copies ran while one was open for 0% of the time, Pallas kernels for 1%

profile of v9, /device:TPU:2, one launch (start us, length us, event | category | flops | bytes accessed | tf_op | source)
XLA Modules:
  0.0 97.7 jit_solution(14991613549994499945)
XLA Ops:
  0.6 0.0 copy-start.4
  0.6 1.7 %shard_map.131 = f32[4,48,128]{2,1,0:T(8,128)} custom-call(f32[24,4,64]{2,1,0:T(4,128)} %align_ref.5, f32[1,64]{1,0:T(1,128)} %bitcast.14), custom_call_target="tpu_custom_call" | custom-call | tf_op jit(solution)/shard_map/pallas_call | solution.py:294
  2.4 0.0 copy-start.2
  2.4 0.0 copy-start.3
  2.4 17.6 %all-to-all-start = ((f32[4,48,128]{2,1,0:T(8,128)}), f32[4,48,128]{2,1,0:T(8,128)S(1)}, u32[]{:S(2)}, u32[]{:S(2)}) async-start(f32[4,48,128]{2,1,0:T(8,128)} %shard_map.131), calls=%async_computation | async-start | bytes 196608 | tf_op jit(solution)/shard_map/all_to_all | solution.py:315
  20.0 0.0 copy-start.9
  20.0 0.0 copy-start.10
  20.0 0.0 copy-start.11
  20.0 0.0 copy-done.4
  20.0 0.0 copy-done.2
  20.0 0.0 copy-done.3
  20.0 0.6 copy-done.9
  20.6 0.0 copy-done.10
  20.6 0.0 copy-done.11
  20.7 0.0 copy-start.1
  20.7 1.0 %copy-done.1 = f32[1024,128]{1,0:T(8,128)S(1)} copy-done((f32[1024,128]{1,0:T(8,128)S(1)}, f32[1024,128]{1,0:T(8,128)}, u32[]{:S(2)}) %copy-start.1) | copy-done | bytes 524312
  21.7 1.4 %shard_map.132 = (f32[16,72,128]{2,1,0:T(8,128)}, f32[24,1024]{1,0:T(8,128)S(1)}, bf16[2048,256]{1,0:T(8,128)(2,1)S(1)}, f32[8,128]{1,0:T(8,128)S(1)}) custom-call(f32[8,24,48]{2,1,0:T(8,128)S(1)} %copy-done.3, f32[24,4,64]{2,1,0:T(4,128)S(1)} %copy-done.2, f32[64,256]{1,0:T(8,128)S(1)} %copy-done.4, f32[1024,128]{1,0:T(8,128)S(1)} %copy-done.1, ...), custom_call_target="tpu_custom_call" | custom-call | tf_op jit(solution)/shard_map/pallas_call | solution.py:297
  23.1 2.0 %all-to-all-done = f32[4,48,128]{2,1,0:T(8,128)S(1)} async-done(((f32[4,48,128]{2,1,0:T(8,128)}), f32[4,48,128]{2,1,0:T(8,128)S(1)}, u32[]{:S(2)}, u32[]{:S(2)}) %all-to-all-start) | async-done | bytes 98336 | tf_op jit(solution)/shard_map/all_to_all | solution.py:315
  25.1 5.6 %all-to-all-start.1 = ((f32[16,72,128]{2,1,0:T(8,128)}), f32[16,72,128]{2,1,0:T(8,128)S(1)}, u32[]{:S(2)}, u32[]{:S(2)}) async-start(f32[16,72,128]{2,1,0:T(8,128)} %get-tuple-element.14), calls=%async_computation.1 | async-start | bytes 1179648 | tf_op jit(solution)/shard_map/all_to_all | solution.py:319
  30.7 0.0 copy-start.5
  30.7 0.0 copy-start.6
  30.7 0.0 copy-start.7
  30.7 0.0 copy-start.8
  30.7 14.1 %all_gather.9 = f32[1536,128]{1,0:T(8,128)S(1)} all-gather(f32[192,128]{1,0:T(8,128)S(1)} %bitcast.18), channel_id=1, replica_groups=mesh['y'=4,'zh'=4,'core'=2,'zl'=4,'x'=4] {'y','core'}, dimensions={0}, use_global_device_ids=true | all-gather | bytes 884736 | tf_op jit(solution)/shard_map/all_gather | solution.py:320
  44.8 0.0 all-to-all-done.1.weights_ref
  44.9 0.0 copy-done.5
  44.9 0.0 copy-done.6
  44.9 0.0 copy-done.7
  44.9 0.0 copy-done.8
  44.9 2.4 %shard_map.133 = (f32[24,4,64]{2,1,0:T(4,128)}, f32[24,128]{1,0:T(8,128)S(1)}, f32[8,24,128]{2,1,0:T(8,128)}) custom-call(f32[16,72,128]{2,1,0:T(8,128)S(1)} %all-to-all-done.1.weights_ref, f32[32,48,128]{2,1,0:T(8,128)S(1)} %bitcast.9, f32[24,1024]{1,0:T(8,128)S(1)} %get-tuple-element.16.gate_ref, f32[8,128]{1,0:T(8,128)S(1)} %get-tuple-element.17.small_ref, ...), custom_call_target="tpu_custom_call" | custom-call | tf_op jit(solution)/shard_map/pallas_call | solution.py:321
  47.2 12.0 %all-to-all-start.2 = ((f32[8,24,128]{2,1,0:T(8,128)}), f32[8,24,128]{2,1,0:T(8,128)S(1)}, u32[]{:S(2)}, u32[]{:S(2)}) async-start(f32[8,24,128]{2,1,0:T(8,128)} %get-tuple-element.19), calls=%async_computation.2 | async-start | bytes 196608 | tf_op jit(solution)/shard_map/all_to_all | solution.py:337
  59.3 12.4 %all_gather.10 = f32[96,128]{1,0:T(8,128)S(1)} all-gather(f32[24,128]{1,0:T(8,128)S(1)} %get-tuple-element.20), channel_id=1, replica_groups=mesh['y'=4,'zh'=4,'core'=2,'zl'=4,'x'=4] {'x'}, dimensions={0}, use_global_device_ids=true | all-gather | bytes 61440 | tf_op jit(solution)/shard_map/all_gather | solution.py:338
  71.7 0.0 all-to-all-done.2.blocks_ref
  71.7 0.8 shard_map.134
  72.5 0.0 copy-start
  72.5 8.5 %all-to-all-start.3 = ((f32[32,24,128]{2,1,0:T(8,128)}), f32[32,24,128]{2,1,0:T(8,128)S(1)}, u32[]{:S(2)}, u32[]{:S(2)}) async-start(f32[32,24,128]{2,1,0:T(8,128)} %shard_map.134), calls=%async_computation.3 | async-start | bytes 786432 | tf_op jit(solution)/shard_map/all_to_all | solution.py:343
  81.0 11.8 %all_gather.11.left_ref = f32[384,128]{1,0:T(8,128)S(1)} all-gather(f32[96,128]{1,0:T(8,128)S(1)} %all_gather.10), channel_id=1, replica_groups={{0,8,12,4},{1,9,13,5},{2,10,14,6},{3,11,15,7},{16,24,28,20},{17,25,29,2..., dimensions={0}, use_global_device_ids=true | all-gather | bytes 245760 | tf_op jit(solution)/shard_map/all_gather | solution.py:345
  92.7 0.0 all-to-all-done.3
  92.7 0.0 copy-done
  92.7 5.0 %shard_map.135 = f32[24,48,128]{2,1,0:T(8,128)} custom-call(f32[384,128]{1,0:T(8,128)S(1)} %all_gather.11.left_ref, f32[768,128]{1,0:T(8,128)S(1)} %bitcast.10, f32[24,48,128]{2,1,0:T(8,128)S(1)} %copy-done, bf16[2048,256]{1,0:T(8,128)(2,1)S(1)} %get-tuple-element.23.spread_ref, f32[8,128]{1,0:T(8,128)S(1)} %get-tuple-element.17.small_ref), custom_call_target="tpu_custom_call" | custom-call | tf_op jit(solution)/shard_map/pallas_call | solution.py:346
Async XLA Ops:
  0.6 19.3 %copy-start.4 = (f32[64,256]{1,0:T(8,128)S(1)}, f32[64,256]{1,0:T(8,128)}, u32[]{:S(2)}) copy-start(f32[64,256]{1,0:T(8,128)} %gate_w_ref.1) | copy-start | bytes 196612
  2.4 17.6 %copy-start.2 = (f32[24,4,64]{2,1,0:T(4,128)S(1)}, f32[24,4,64]{2,1,0:T(4,128)}, u32[]{:S(2)}) copy-start(f32[24,4,64]{2,1,0:T(4,128)} %align_ref.5) | copy-start | bytes 73732
  2.4 17.6 %copy-start.3 = (f32[8,24,48]{2,1,0:T(8,128)S(1)}, f32[8,24,48]{2,1,0:T(8,128)}, u32[]{:S(2)}) copy-start(f32[8,24,48]{2,1,0:T(8,128)} %pair_w_ref.1) | copy-start | bytes 110596
  2.4 22.8 %all-to-all-start = ((f32[4,48,128]{2,1,0:T(8,128)}), f32[4,48,128]{2,1,0:T(8,128)S(1)}, u32[]{:S(2)}, u32[]{:S(2)}) async-start(f32[4,48,128]{2,1,0:T(8,128)} %shard_map.131), calls=%async_computation | async-start | bytes 196608 | tf_op jit(solution)/shard_map/all_to_all | solution.py:315
  20.0 0.7 copy-start.9
  20.0 0.7 copy-start.10
  20.0 0.7 copy-start.11
  20.7 1.0 %copy-start.1 = (f32[1024,128]{1,0:T(8,128)S(1)}, f32[1024,128]{1,0:T(8,128)}, u32[]{:S(2)}) copy-start(f32[1024,128]{1,0:T(8,128)} %outer_ref.1) | copy-start | bytes 1572868
  25.1 19.7 %all-to-all-start.1 = ((f32[16,72,128]{2,1,0:T(8,128)}), f32[16,72,128]{2,1,0:T(8,128)S(1)}, u32[]{:S(2)}, u32[]{:S(2)}) async-start(f32[16,72,128]{2,1,0:T(8,128)} %get-tuple-element.14), calls=%async_computation.1 | async-start | bytes 1179648 | tf_op jit(solution)/shard_map/all_to_all | solution.py:319
  30.7 14.2 %copy-start.5 = (f32[64,256]{1,0:T(8,128)S(1)}, f32[64,256]{1,0:T(8,128)}, u32[]{:S(2)}) copy-start(f32[64,256]{1,0:T(8,128)} %value_ref.1) | copy-start | bytes 196612
  30.7 14.2 %copy-start.6 = (f32[256,64]{0,1:T(8,128)S(1)}, f32[256,64]{0,1:T(8,128)}, u32[]{:S(2)}) copy-start(f32[256,64]{0,1:T(8,128)} %param.18) | copy-start | bytes 196612
  30.7 14.2 %copy-start.7 = (f32[64,32]{0,1:T(8,128)S(1)}, f32[64,32]{0,1:T(8,128)}, u32[]{:S(2)}) copy-start(f32[64,32]{0,1:T(8,128)} %param.20) | copy-start | bytes 24580
  30.7 14.2 %copy-start.8 = (f32[64,32]{0,1:T(8,128)S(1)}, f32[64,32]{0,1:T(8,128)}, u32[]{:S(2)}) copy-start(f32[64,32]{0,1:T(8,128)} %param.21) | copy-start | bytes 24580
  47.2 24.5 %all-to-all-start.2 = ((f32[8,24,128]{2,1,0:T(8,128)}), f32[8,24,128]{2,1,0:T(8,128)S(1)}, u32[]{:S(2)}, u32[]{:S(2)}) async-start(f32[8,24,128]{2,1,0:T(8,128)} %get-tuple-element.19), calls=%async_computation.2 | async-start | bytes 196608 | tf_op jit(solution)/shard_map/all_to_all | solution.py:337
  72.5 20.2 %copy-start = (f32[24,48,128]{2,1,0:T(8,128)S(1)}, f32[24,48,128]{2,1,0:T(8,128)}, u32[]{:S(2)}) copy-start(f32[24,48,128]{2,1,0:T(8,128)} %state_ref.1) | copy-start | bytes 1769476
  72.5 20.2 %all-to-all-start.3 = ((f32[32,24,128]{2,1,0:T(8,128)}), f32[32,24,128]{2,1,0:T(8,128)S(1)}, u32[]{:S(2)}, u32[]{:S(2)}) async-start(f32[32,24,128]{2,1,0:T(8,128)} %shard_map.134), calls=%async_computation.3 | async-start | bytes 786432 | tf_op jit(solution)/shard_map/all_to_all | solution.py:343
